TPU v7x, 32 devices: a whole 2x2x4 slice. The times are simulated.
32 devices in a mesh: gz: 8 (over z, core), xy: 4 (over y, x).
Axes of the slice: x: 2, y: 2, z: 4, core: 2. Of those that a mesh axis runs over, the one named last changes fastest.
Arguments:
- density: float32 [512, 32, 512], P('xy', 'gz'), may hold values from 0.5 to 2
- momentum: float32 [3, 512, 32, 512], P(None, 'xy', 'gz'), may hold values from -3 to 3
- magnetic: float32 [3, 512, 32, 512], P(None, 'xy', 'gz'), may hold values from -3 to 3
- arm_potential: float32 [512, 512], P('xy'), may hold values from -10 to 10
- sn_cells: int32 [32, 3], P(('gz', 'xy')), may hold values from 0 to 511, as said below
- sn_counts: int32 [32], P(('gz', 'xy')), may hold values from 0 to 3
Outputs:
- new_density: float32 [512, 32, 512], P('xy', 'gz')
- new_momentum: float32 [3, 512, 32, 512], P(None, 'xy', 'gz')
- new_magnetic: float32 [3, 512, 32, 512], P(None, 'xy', 'gz')
- density_modes: float32 [2, 32, 512, 512], P(None, 'gz', 'xy')
Inputs may be any that keep to these rules, and one draw needn't show every extreme that they name: `sn_cells`: row e is the centre of an event held by device e // 1 of the joined axes gz+xy (gz slowest); its x lies among that device's 128 x rows and its z among its 4 z planes. `sn_counts`: 0 marks an empty slot.
All inputs are finite; a program needn't handle non-finite values.
Results may differ from a plain program's by a relative error of at most 0.00023.
Values sent between devices are 32-bit elements; how exact they have to be, the bound alone decides.
No kernel may reach another device: no remote copies, remote signals or barrier semaphores. Data moves between devices by JAX's collectives and lax.ppermute only.
A program may use at most 384 MiB of HBM per device.

v0:
```python
import math

import jax
import jax.numpy as jnp
from jax import lax
from jax.sharding import PartitionSpec as P

NX = 512
NY = 512
SUPERNOVA_RADIUS = 16


sound_square = 1.0
time_step = 0.1
diffusion = 0.05
mass_yield = 1.0
push_yield = 2.0


def from_behind(block, axis, distance):
    devices = range(lax.axis_size(axis))
    route = [((i - distance) % len(devices), i) for i in devices]
    return lax.ppermute(block, axis, route)


def with_halo(array, sides, width):
    for axis, dim in sides:
        peers, length = (lax.axis_size(axis), array.shape[dim])
        up = [(i, (i + 1) % peers) for i in range(peers)]
        down = [(j, i) for i, j in up]
        last = lax.slice_in_dim(array, length - width, length, axis=dim)
        leading = lax.slice_in_dim(array, 0, width, axis=dim)
        before = lax.ppermute(last, axis, up)
        after = lax.ppermute(leading, axis, down)
        array = jnp.concatenate([before, array, after], axis=dim)
    return array


def fluxes(mass_density, momenta, induction, direction):
    velocity = [momenta[component] / mass_density for component in range(3)]
    pressure = sound_square * mass_density + 0.5 * (
        induction[0] * induction[0] + induction[1] * induction[1] + induction[2] * induction[2]
    )
    result = [momenta[direction]]
    for component in range(3):
        term = (
            momenta[component] * velocity[direction] - induction[component] * induction[direction]
        )
        if component == direction:
            term = term + pressure
        result.append(term)
    for component in range(3):
        result.append(
            velocity[direction] * induction[component] - induction[direction] * velocity[component]
        )
    return jnp.stack(result)


def pick_rows(field, start, count, axis):
    return lax.slice_in_dim(field, start, start + count, axis=axis)


def central_pad(field, axis):
    count = field.shape[axis] - 4
    return (
        pick_rows(field, 0, count, axis)
        - 8.0 * pick_rows(field, 1, count, axis)
        + 8.0 * pick_rows(field, 3, count, axis)
        - pick_rows(field, 4, count, axis)
    ) / 12.0


def second_pad(field, axis):
    count = field.shape[axis] - 4
    return (
        pick_rows(field, 1, count, axis)
        + pick_rows(field, 3, count, axis)
        - 2.0 * pick_rows(field, 2, count, axis)
    )


def central_wrap(field, axis):
    return (
        jnp.roll(field, 2, axis)
        - 8.0 * jnp.roll(field, 1, axis)
        + 8.0 * jnp.roll(field, -1, axis)
        - jnp.roll(field, -2, axis)
    ) / 12.0


def second_wrap(field, axis):
    return jnp.roll(field, 1, axis) + jnp.roll(field, -1, axis) - 2.0 * field


def offsets(reach, count):
    kept = sorted({step % count for step in range(-reach, reach + 1)})
    return [step - count if 2 * step > count else step for step in kept]


def deposit(event_cells, counts, row_start, row_count, plane_start, planes, depth_all):
    centre_row = event_cells[:, 0][:, None]
    centre_col = event_cells[:, 1][:, None]
    centre_plane = event_cells[:, 2][:, None]
    along_row = row_start + jnp.arange(row_count, dtype=jnp.int32)
    along_plane = plane_start + jnp.arange(planes, dtype=jnp.int32)
    along_col = jnp.arange(NY, dtype=jnp.int32)
    row_offset = ((along_row[None, :] - centre_row + NX // 2) % NX - NX // 2).astype(jnp.float32)[
        :, :, None, None
    ]
    plane_offset = (
        (along_plane[None, :] - centre_plane + depth_all // 2) % depth_all - depth_all // 2
    ).astype(jnp.float32)[:, None, :, None]
    column_offset = ((along_col[None, :] - centre_col + NY // 2) % NY - NY // 2).astype(
        jnp.float32
    )[:, None, None, :]
    radius_squared = (
        row_offset * row_offset + plane_offset * plane_offset + column_offset * column_offset
    )
    weights = (
        jnp.maximum(1.0 - radius_squared / (SUPERNOVA_RADIUS * SUPERNOVA_RADIUS), 0.0)
        * counts.astype(jnp.float32)[:, None, None, None]
    )
    impulse = push_yield / SUPERNOVA_RADIUS
    return jnp.stack(
        [
            mass_yield * jnp.sum(weights, axis=0),
            impulse * jnp.sum(weights * row_offset, axis=0),
            impulse * jnp.sum(weights * column_offset, axis=0),
            impulse * jnp.sum(weights * plane_offset, axis=0),
        ]
    )


def on_device(density, momentum, magnetic, arm_potential, sn_cells, sn_counts):
    row_count, planes, columns = density.shape
    across = lax.axis_size("xy")
    layers = lax.axis_size("gz")
    tile_row = lax.axis_index("xy")
    tile_plane = lax.axis_index("gz")
    depth_all = planes * layers
    row_steps = offsets(-(-SUPERNOVA_RADIUS // row_count), across)
    plane_steps = offsets(-(-SUPERNOVA_RADIUS // planes), layers)
    totals = jnp.zeros((len(plane_steps), 4, row_count, planes, columns), jnp.float32)
    for shift_row in row_steps:
        row_start = (tile_row + shift_row) % across * row_count
        pieces = jnp.stack(
            [
                deposit(
                    sn_cells,
                    sn_counts,
                    row_start,
                    row_count,
                    (tile_plane + shift_plane) % layers * planes,
                    planes,
                    depth_all,
                )
                for shift_plane in plane_steps
            ]
        )
        if shift_row != 0:
            pieces = from_behind(pieces, "xy", shift_row)
        totals = totals + pieces
    source = jnp.zeros((4, row_count, planes, columns), jnp.float32)
    for position, shift_plane in enumerate(plane_steps):
        portion = totals[position]
        if shift_plane != 0:
            portion = from_behind(portion, "gz", shift_plane)
        source = source + portion
    mass_density = density + source[0]
    momenta = momentum + source[1:]
    potential = jnp.broadcast_to(arm_potential[:, None, :], (row_count, planes, columns))
    fields_all = jnp.concatenate([mass_density[None], momenta, magnetic, potential[None]], axis=0)
    padded = with_halo(fields_all, (("gz", 2), ("xy", 1)), 2)
    along_x = padded[:, :, 2:-2, :]
    along_z = padded[:, 2:-2, :, :]
    interior = padded[:, 2:-2, 2:-2, :]
    divergence = central_pad(fluxes(along_x[0], along_x[1:4], along_x[4:7], 0), 1)
    divergence = divergence + central_wrap(fluxes(interior[0], interior[1:4], interior[4:7], 1), 3)
    divergence = divergence + central_pad(fluxes(along_z[0], along_z[1:4], along_z[4:7], 2), 2)
    smooth = second_pad(along_x[:7], 1) + second_wrap(interior[:7], 3) + second_pad(along_z[:7], 2)
    updated = interior[:7] - time_step * divergence + diffusion * smooth
    slope_x = central_pad(along_x[7], 0)
    slope_y = central_wrap(interior[7], 2)
    new_density = updated[0]
    new_momentum = jnp.stack(
        [
            updated[1] - time_step * mass_density * slope_x,
            updated[2] - time_step * mass_density * slope_y,
            updated[3],
        ]
    )
    new_magnetic = updated[4:7]
    wave_y = jnp.arange(NY, dtype=jnp.int32)
    angle_y = (wave_y[:, None] * wave_y[None, :] % NY).astype(jnp.float32) * (2.0 * math.pi / NY)
    cosine_y = jnp.cos(angle_y)
    sine_y = jnp.sin(angle_y)
    wave_x = jnp.arange(NX, dtype=jnp.int32)
    angle_x = (wave_x[:, None] * wave_x[None, :] % NX).astype(jnp.float32) * (2.0 * math.pi / NX)
    cosine_x = jnp.cos(angle_x)
    sine_x = jnp.sin(angle_x)
    real_y = jnp.einsum("xzy,yk->zkx", new_density, cosine_y, precision=lax.Precision.HIGHEST)
    imag_y = -jnp.einsum("xzy,yk->zkx", new_density, sine_y, precision=lax.Precision.HIGHEST)
    stacked = jnp.stack([real_y, imag_y])
    portion = lax.all_to_all(stacked, "xy", split_axis=2, concat_axis=3, tiled=True)
    real_part = portion[0]
    imag_part = portion[1]
    out_real = jnp.einsum(
        "zkx,xj->zkj", real_part, cosine_x, precision=lax.Precision.HIGHEST
    ) + jnp.einsum("zkx,xj->zkj", imag_part, sine_x, precision=lax.Precision.HIGHEST)
    out_imag = jnp.einsum(
        "zkx,xj->zkj", imag_part, cosine_x, precision=lax.Precision.HIGHEST
    ) - jnp.einsum("zkx,xj->zkj", real_part, sine_x, precision=lax.Precision.HIGHEST)
    spectrum = jnp.stack([out_real, out_imag])
    band = spectrum.shape[2]
    wave_ky = tile_row * band + jnp.arange(band, dtype=jnp.int32)
    keep = jnp.where((wave_ky[:, None] == 0) & (wave_x[None, :] == 0), 0.0, 1.0)
    spectrum = spectrum * (keep / math.sqrt(NX * NY))
    return (new_density, new_momentum, new_magnetic, spectrum)


def solution(mesh):
    in_specs = (
        P("xy", "gz", None),
        P(None, "xy", "gz", None),
        P(None, "xy", "gz", None),
        P("xy", None),
        P(("gz", "xy"), None),
        P(("gz", "xy")),
    )
    out_specs = (
        P("xy", "gz", None),
        P(None, "xy", "gz", None),
        P(None, "xy", "gz", None),
        P(None, "gz", "xy", None),
    )
    return jax.shard_map(
        on_device, mesh=mesh, in_specs=in_specs, out_specs=out_specs, check_vma=False
    )
```

profile of v0, /device:TPU:0, one launch (start us, length us, event | category | flops | bytes accessed | tf_op | source)
XLA Modules:
  0.0 2628.6 jit_solution(16370548706646424364)
XLA Ops:
  29.3 9.0 maximum_multiply_fusion.17
  38.3 4.9 fusion.38
  45.9 10.8 maximum_multiply_fusion.15
  56.8 4.9 fusion.40
  115.7 671.3 %collective-permute-done = f32[8,4,128,4,512]{4,2,3,1,0:T(8,128)} collective-permute-done((f32[8,4,128,4,512]{4,2,3,1,0:T(8,128)}, f32[8,4,128,4,512]{4,2,3,1,0:T(8,128)}, u32[]{:S(2)}, u32[]{:S(2)}) %collective-permute-start) | collective-permute-done | bytes 33554464 | tf_op jit(solution)/shard_map/ppermute | solution.py:23
  786.9 718.5 %collective-permute-done.1 = f32[8,4,128,4,512]{4,2,3,1,0:T(8,128)} collective-permute-done((f32[8,4,128,4,512]{4,2,3,1,0:T(8,128)}, f32[8,4,128,4,512]{4,2,3,1,0:T(8,128)}, u32[]{:S(2)}, u32[]{:S(2)}) %collective-permute-start.1) | collective-permute-done | bytes 33554464 | tf_op jit(solution)/shard_map/ppermute | solution.py:23
  1505.4 44.2 %add_add_fusion = f32[8,4,128,4,512]{4,2,3,1,0:T(8,128)} fusion(f32[8,4,128,4,512]{4,2,3,1,0:T(8,128)} %collective-permute-done.1, f32[8,4,128,4,512]{4,2,3,1,0:T(8,128)} %fusion.32, f32[8,4,128,4,512]{4,2,3,1,0:T(8,128)} %collective-permute-done), kind=kLoop, calls=%fused_computation | loop fusion | flops 16777216 | bytes 134217728 | tf_op jit(solution)/shard_map/add | solution.py:162
  1549.6 19.8 slice_bitcast_fusion.6
  1576.0 88.0 %collective-permute-done.2 = f32[4,128,4,512]{3,1,2,0:T(8,128)} collective-permute-done((f32[4,128,4,512]{3,1,2,0:T(8,128)}, f32[4,128,4,512]{3,1,2,0:T(8,128)}, u32[]{:S(2)}, u32[]{:S(2)}) %collective-permute-start.2) | collective-permute-done | bytes 4194336 | tf_op jit(solution)/shard_map/ppermute | solution.py:23
  1665.6 89.5 %collective-permute-start.8 = (f32[4,128,4,512]{3,1,2,0:T(8,128)}, f32[4,128,4,512]{3,1,2,0:T(8,128)}, u32[]{:S(2)}, u32[]{:S(2)}) collective-permute-start(f32[4,128,4,512]{3,1,2,0:T(8,128)} %get-tuple-element.56), channel_id=1, source_target_pairs={{4,0},{8,4},{12,8},{16,12},{20,16},{24,20},{28,24},{0,28},{5,1},{9... | collective-permute-start | bytes 12582920 | tf_op jit(solution)/shard_map/ppermute | solution.py:23
  1760.5 263.5 %collective-permute-done.4 = f32[4,128,4,512]{3,1,2,0:T(8,128)} collective-permute-done((f32[4,128,4,512]{3,1,2,0:T(8,128)}, f32[4,128,4,512]{3,1,2,0:T(8,128)}, u32[]{:S(2)}, u32[]{:S(2)}) %collective-permute-start.4) | collective-permute-done | bytes 4194336 | tf_op jit(solution)/shard_map/ppermute | solution.py:23
  2024.1 87.1 %collective-permute-done.8 = f32[4,128,4,512]{3,1,2,0:T(8,128)} collective-permute-done((f32[4,128,4,512]{3,1,2,0:T(8,128)}, f32[4,128,4,512]{3,1,2,0:T(8,128)}, u32[]{:S(2)}, u32[]{:S(2)}) %collective-permute-start.8) | collective-permute-done | bytes 4194336 | tf_op jit(solution)/shard_map/ppermute | solution.py:23
  2111.2 12.8 fusion.24
  2132.3 8.3 fusion.174
  2140.6 183.5 %collective-permute-start.10 = (f32[8,128,2,512]{3,1,2,0:T(8,128)}, f32[8,128,2,512]{3,1,2,0:T(8,128)}, u32[]{:S(2)}, u32[]{:S(2)}) collective-permute-start(f32[8,128,2,512]{3,1,2,0:T(8,128)} %get-tuple-element.67), channel_id=1, source_target_pairs={{4,0},{8,4},{12,8},{16,12},{20,16},{24,20},{28,24},{0,28},{5,1},{9... | collective-permute-start | bytes 12582920 | tf_op jit(solution)/shard_map/ppermute | solution.py:34
  2335.3 12.4 fusion.176
  2347.8 12.7 fusion.178
  2360.4 12.7 fusion.180
  2373.2 39.5 %collective-permute-done.10 = f32[8,128,2,512]{3,1,2,0:T(8,128)} collective-permute-done((f32[8,128,2,512]{3,1,2,0:T(8,128)}, f32[8,128,2,512]{3,1,2,0:T(8,128)}, u32[]{:S(2)}, u32[]{:S(2)}) %collective-permute-start.10) | collective-permute-done | bytes 4194336 | tf_op jit(solution)/shard_map/ppermute | solution.py:34
  2425.2 7.6 subtract_dynamic-update-slice_fusion.4
  2432.9 4.5 subtract_dynamic-update-slice_fusion.3
  2449.8 11.4 pad_maximum_fusion
  2463.5 4.5 add_dynamic-update-slice_fusion.1
  2480.3 23.0 maximum_maximum_fusion
  2503.2 49.8 %fusion.4 = f32[7,128,4,512]{3,1,2,0:T(8,128)} fusion(f32[8,128,2,512]{3,1,2,0:T(8,128)} %collective-permute-done.10, f32[1,128,4,512]{3,1,2,0:T(8,128)} %copy-done.8, f32[3,128,4,512]{3,1,2,0:T(8,128)S(1)} %copy.40, f32[3,128,4,512]{3,1,2,0:T(8,128)} %copy-done, f32[1,128,4,512]{3,1,2,0:T(8,128)} %bitcast.279, ...), kind=kLoop, calls=%fused_computation.10 | loop fusion | flops 84410368 | bytes 141557760 | tf_op jit(solution)/shard_map/add | solution.py:181
  2553.1 8.4 convolution_bitcast_fusion
  2561.5 8.8 fusion.51
  2573.1 4.4 all-to-all-start
  2600.2 6.8 fusion.74
  2607.5 6.3 fusion.72
  2613.8 6.3 fusion.50
  2620.1 6.5 fusion.49
  (268 shorter events, 184.3 us)
Async XLA Ops:
  56.7 8.4 copy-start.48
  56.7 8.4 copy-start.49
  56.7 8.4 copy-start.50
  56.8 8.3 copy-start.51
  61.7 725.3 %collective-permute-start = (f32[8,4,128,4,512]{4,2,3,1,0:T(8,128)}, f32[8,4,128,4,512]{4,2,3,1,0:T(8,128)}, u32[]{:S(2)}, u32[]{:S(2)}) collective-permute-start(f32[8,4,128,4,512]{4,2,3,1,0:T(8,128)} %fusion.40), channel_id=1, source_target_pairs={{3,0},{0,1},{1,2},{2,3},{7,4},{4,5},{5,6},{6,7},{11,8},{8,9},{9,10... | collective-permute-start | bytes 100663304 | tf_op jit(solution)/shard_map/ppermute | solution.py:23
  88.6 1416.8 %collective-permute-start.1 = (f32[8,4,128,4,512]{4,2,3,1,0:T(8,128)}, f32[8,4,128,4,512]{4,2,3,1,0:T(8,128)}, u32[]{:S(2)}, u32[]{:S(2)}) collective-permute-start(f32[8,4,128,4,512]{4,2,3,1,0:T(8,128)} %fusion.48), channel_id=1, source_target_pairs={{1,0},{2,1},{3,2},{0,3},{5,4},{6,5},{7,6},{4,7},{9,8},{10,9},{11,1... | collective-permute-start | bytes 100663304 | tf_op jit(solution)/shard_map/ppermute | solution.py:23
  1569.4 188.7 %copy-start.19 = (f32[128,512]{1,0:T(8,128)S(1)}, f32[128,512]{1,0:T(8,128)}, u32[]{:S(2)}) copy-start(f32[128,512]{1,0:T(8,128)} %param.9) | copy-start | bytes 786436
  1569.4 94.6 %collective-permute-start.2 = (f32[4,128,4,512]{3,1,2,0:T(8,128)}, f32[4,128,4,512]{3,1,2,0:T(8,128)}, u32[]{:S(2)}, u32[]{:S(2)}) collective-permute-start(f32[4,128,4,512]{3,1,2,0:T(8,128)} %get-tuple-element.55), channel_id=1, source_target_pairs={{28,0},{0,4},{4,8},{8,12},{12,16},{16,20},{20,24},{24,28},{29,1},{... | collective-permute-start | bytes 12582920 | tf_op jit(solution)/shard_map/ppermute | solution.py:23
  1569.5 96.2 %collective-permute-start.3 = (f32[4,128,4,512]{3,1,2,0:T(8,128)}, f32[4,128,4,512]{3,1,2,0:T(8,128)}, u32[]{:S(2)}, u32[]{:S(2)}) collective-permute-start(f32[4,128,4,512]{3,1,2,0:T(8,128)} %get-tuple-element.61), channel_id=1, source_target_pairs={{24,0},{28,4},{0,8},{4,12},{8,16},{12,20},{16,24},{20,28},{25,1},{... | collective-permute-start | bytes 12582920 | tf_op jit(solution)/shard_map/ppermute | solution.py:23
  1571.1 452.8 %collective-permute-start.4 = (f32[4,128,4,512]{3,1,2,0:T(8,128)}, f32[4,128,4,512]{3,1,2,0:T(8,128)}, u32[]{:S(2)}, u32[]{:S(2)}) collective-permute-start(f32[4,128,4,512]{3,1,2,0:T(8,128)} %get-tuple-element.60), channel_id=1, source_target_pairs={{20,0},{24,4},{28,8},{0,12},{4,16},{8,20},{12,24},{16,28},{21,1},{... | collective-permute-start | bytes 12582920 | tf_op jit(solution)/shard_map/ppermute | solution.py:23
  1573.6 450.5 %collective-permute-start.5 = (f32[4,128,4,512]{3,1,2,0:T(8,128)}, f32[4,128,4,512]{3,1,2,0:T(8,128)}, u32[]{:S(2)}, u32[]{:S(2)}) collective-permute-start(f32[4,128,4,512]{3,1,2,0:T(8,128)} %get-tuple-element.59), channel_id=1, source_target_pairs={{16,0},{20,4},{24,8},{28,12},{0,16},{4,20},{8,24},{12,28},{17,1},{... | collective-permute-start | bytes 12582920 | tf_op jit(solution)/shard_map/ppermute | solution.py:23
  1574.8 449.3 %collective-permute-start.6 = (f32[4,128,4,512]{3,1,2,0:T(8,128)}, f32[4,128,4,512]{3,1,2,0:T(8,128)}, u32[]{:S(2)}, u32[]{:S(2)}) collective-permute-start(f32[4,128,4,512]{3,1,2,0:T(8,128)} %get-tuple-element.58), channel_id=1, source_target_pairs={{12,0},{16,4},{20,8},{24,12},{28,16},{0,20},{4,24},{8,28},{13,1},{... | collective-permute-start | bytes 12582920 | tf_op jit(solution)/shard_map/ppermute | solution.py:23
  1664.0 360.1 %collective-permute-start.7 = (f32[4,128,4,512]{3,1,2,0:T(8,128)}, f32[4,128,4,512]{3,1,2,0:T(8,128)}, u32[]{:S(2)}, u32[]{:S(2)}) collective-permute-start(f32[4,128,4,512]{3,1,2,0:T(8,128)} %get-tuple-element.57), channel_id=1, source_target_pairs={{8,0},{12,4},{16,8},{20,12},{24,16},{28,20},{0,24},{4,28},{9,1},{1... | collective-permute-start | bytes 12582920 | tf_op jit(solution)/shard_map/ppermute | solution.py:23
  1665.6 445.5 %collective-permute-start.8 = (f32[4,128,4,512]{3,1,2,0:T(8,128)}, f32[4,128,4,512]{3,1,2,0:T(8,128)}, u32[]{:S(2)}, u32[]{:S(2)}) collective-permute-start(f32[4,128,4,512]{3,1,2,0:T(8,128)} %get-tuple-element.56), channel_id=1, source_target_pairs={{4,0},{8,4},{12,8},{16,12},{20,16},{24,20},{28,24},{0,28},{5,1},{9... | collective-permute-start | bytes 12582920 | tf_op jit(solution)/shard_map/ppermute | solution.py:23
  1760.4 363.5 %copy-start.66 = (f32[3,128,4,512]{3,2,1,0:T(4,128)S(1)}, f32[3,128,4,512]{3,2,1,0:T(4,128)}, u32[]{:S(2)}) copy-start(f32[3,128,4,512]{3,2,1,0:T(4,128)} %param.7) | copy-start | bytes 9437188
  2125.2 200.5 %copy-start = (f32[3,128,4,512]{3,1,2,0:T(8,128)}, f32[3,128,4,512]{3,1,2,0:T(8,128)S(1)}, u32[]{:S(2)}) copy-start(f32[3,128,4,512]{3,1,2,0:T(8,128)S(1)} %slice_add_fusion.1) | copy-start | bytes 9437188
  2126.2 199.5 %copy-start.3 = (f32[128,4,512]{2,0,1:T(8,128)}, f32[128,4,512]{2,0,1:T(8,128)S(1)}, u32[]{:S(2)}) copy-start(f32[128,4,512]{2,0,1:T(8,128)S(1)} %get-tuple-element.19) | copy-start | bytes 3145732
  2140.6 272.1 %collective-permute-start.10 = (f32[8,128,2,512]{3,1,2,0:T(8,128)}, f32[8,128,2,512]{3,1,2,0:T(8,128)}, u32[]{:S(2)}, u32[]{:S(2)}) collective-permute-start(f32[8,128,2,512]{3,1,2,0:T(8,128)} %get-tuple-element.67), channel_id=1, source_target_pairs={{4,0},{8,4},{12,8},{16,12},{20,16},{24,20},{28,24},{0,28},{5,1},{9... | collective-permute-start | bytes 12582920 | tf_op jit(solution)/shard_map/ppermute | solution.py:34
  2324.2 91.4 %collective-permute-start.9 = (f32[8,128,2,512]{3,1,2,0:T(8,128)}, f32[8,128,2,512]{3,1,2,0:T(8,128)}, u32[]{:S(2)}, u32[]{:S(2)}) collective-permute-start(f32[8,128,2,512]{3,1,2,0:T(8,128)} %get-tuple-element.66), channel_id=1, source_target_pairs={{0,4},{4,8},{8,12},{12,16},{16,20},{20,24},{24,28},{28,0},{1,5},{5... | collective-permute-start | bytes 12582920 | tf_op jit(solution)/shard_map/ppermute | solution.py:33
  2325.3 7.5 copy-start.13
  2326.3 6.5 copy-start.7
  2373.2 48.2 %copy-start.1 = (f32[3,128,4,512]{3,1,2,0:T(8,128)S(1)}, f32[3,128,4,512]{3,1,2,0:T(8,128)}, u32[]{:S(2)}) copy-start(f32[3,128,4,512]{3,1,2,0:T(8,128)} %copy-done) | copy-start | bytes 9437188
  2373.2 48.2 %copy-start.4 = (f32[128,4,512]{2,0,1:T(8,128)S(1)}, f32[128,4,512]{2,0,1:T(8,128)}, u32[]{:S(2)}) copy-start(f32[128,4,512]{2,0,1:T(8,128)} %copy-done.3) | copy-start | bytes 3145732
  2373.2 48.2 %copy-start.9 = (f32[1,128,4,512]{3,1,2,0:T(8,128)S(1)}, f32[1,128,4,512]{3,1,2,0:T(8,128)}, u32[]{:S(2)}) copy-start(f32[1,128,4,512]{3,1,2,0:T(8,128)} %copy-done.8) | copy-start | bytes 3145732
  2418.0 31.8 %collective-permute-start.11 = (f32[8,2,8,512]{3,1,2,0:T(2,128)}, f32[8,2,8,512]{3,1,2,0:T(2,128)S(1)}, u32[]{:S(2)}, u32[]{:S(2)}) collective-permute-start(f32[8,2,8,512]{3,1,2,0:T(2,128)} %get-tuple-element.64), channel_id=1, source_target_pairs={{0,1},{1,2},{2,3},{3,0},{4,5},{5,6},{6,7},{7,4},{8,9},{9,10},{10,1... | collective-permute-start | bytes 786440 | tf_op jit(solution)/shard_map/ppermute | solution.py:33
  2420.0 29.8 %collective-permute-start.12 = (f32[8,2,8,512]{3,1,2,0:T(2,128)}, f32[8,2,8,512]{3,1,2,0:T(2,128)}, u32[]{:S(2)}, u32[]{:S(2)}) collective-permute-start(f32[8,2,8,512]{3,1,2,0:T(2,128)} %get-tuple-element.65), channel_id=1, source_target_pairs={{1,0},{2,1},{3,2},{0,3},{5,4},{6,5},{7,6},{4,7},{9,8},{10,9},{11,1... | collective-permute-start | bytes 786440 | tf_op jit(solution)/shard_map/ppermute | solution.py:34
  2432.9 6.7 copy-start.18
  2449.8 30.5 %copy-start.67 = (f32[8,2,8,512]{3,1,2,0:T(2,128)}, f32[8,2,8,512]{3,1,2,0:T(2,128)S(1)}, u32[]{:S(2)}) copy-start(f32[8,2,8,512]{3,1,2,0:T(2,128)S(1)} %collective-permute-done.11) | copy-start | bytes 786436
  2463.5 12.1 copy-start.12
  2570.4 7.1 copy-start.20
  2573.1 23.6 all-to-all-start
  2613.8 12.9 copy-start.69
  (61 other events, 192.7 us)
where the time goes:
time: 2640 us; the launch traced here: 2630 us
  waiting for transfers between devices  1870 us (71%)
  other arithmetic  303 us (11%)
  starting transfers between devices  294 us (11%)
  local copies, waits for them, and re-layouts  114 us (4%)
  matrix products  43.2 us (2%)
    ppermute x9, waiting for transfers between devices, from_behind(): return lax.ppermute(block, axis, route)  1830 us
    ppermute x2, starting transfers between devices, with_halo(): after = lax.ppermute(leading, axis, down)  185 us
    ppermute x9, starting transfers between devices, from_behind(): return lax.ppermute(block, axis, route)  102 us
    unnamed x38, other arithmetic  102 us
  transfers between devices with their start and end apart: 14, of which 9 were waited for; matrix products, arithmetic and copies ran while one was open for 5% of the time, Pallas kernels for 0%

commit v1 on v0

--- a/solution.py
+++ b/solution.py
@@ -17,23 +17,13 @@
 push_yield = 2.0
 
 
-def from_behind(block, axis, distance):
-    devices = range(lax.axis_size(axis))
-    route = [((i - distance) % len(devices), i) for i in devices]
-    return lax.ppermute(block, axis, route)
-
-
-def with_halo(array, sides, width):
-    for axis, dim in sides:
-        peers, length = (lax.axis_size(axis), array.shape[dim])
-        up = [(i, (i + 1) % peers) for i in range(peers)]
-        down = [(j, i) for i, j in up]
-        last = lax.slice_in_dim(array, length - width, length, axis=dim)
-        leading = lax.slice_in_dim(array, 0, width, axis=dim)
-        before = lax.ppermute(last, axis, up)
-        after = lax.ppermute(leading, axis, down)
-        array = jnp.concatenate([before, array, after], axis=dim)
-    return array
+def neighbours(array, axis, dim, width):
+    peers, length = (lax.axis_size(axis), array.shape[dim])
+    up = [(i, (i + 1) % peers) for i in range(peers)]
+    down = [(j, i) for i, j in up]
+    last = lax.slice_in_dim(array, length - width, length, axis=dim)
+    leading = lax.slice_in_dim(array, 0, width, axis=dim)
+    return lax.ppermute(last, axis, up), lax.ppermute(leading, axis, down)
 
 
 def fluxes(mass_density, momenta, induction, direction):
@@ -90,11 +80,6 @@
 
 def second_wrap(field, axis):
     return jnp.roll(field, 1, axis) + jnp.roll(field, -1, axis) - 2.0 * field
-
-
-def offsets(reach, count):
-    kept = sorted({step % count for step in range(-reach, reach + 1)})
-    return [step - count if 2 * step > count else step for step in kept]
 
 
 def deposit(event_cells, counts, row_start, row_count, plane_start, planes, depth_all):
@@ -133,54 +118,41 @@
 
 def on_device(density, momentum, magnetic, arm_potential, sn_cells, sn_counts):
     row_count, planes, columns = density.shape
-    across = lax.axis_size("xy")
     layers = lax.axis_size("gz")
     tile_row = lax.axis_index("xy")
     tile_plane = lax.axis_index("gz")
     depth_all = planes * layers
-    row_steps = offsets(-(-SUPERNOVA_RADIUS // row_count), across)
-    plane_steps = offsets(-(-SUPERNOVA_RADIUS // planes), layers)
-    totals = jnp.zeros((len(plane_steps), 4, row_count, planes, columns), jnp.float32)
-    for shift_row in row_steps:
-        row_start = (tile_row + shift_row) % across * row_count
-        pieces = jnp.stack(
-            [
-                deposit(
-                    sn_cells,
-                    sn_counts,
-                    row_start,
-                    row_count,
-                    (tile_plane + shift_plane) % layers * planes,
-                    planes,
-                    depth_all,
-                )
-                for shift_plane in plane_steps
-            ]
-        )
-        if shift_row != 0:
-            pieces = from_behind(pieces, "xy", shift_row)
-        totals = totals + pieces
-    source = jnp.zeros((4, row_count, planes, columns), jnp.float32)
-    for position, shift_plane in enumerate(plane_steps):
-        portion = totals[position]
-        if shift_plane != 0:
-            portion = from_behind(portion, "gz", shift_plane)
-        source = source + portion
-    mass_density = density + source[0]
-    momenta = momentum + source[1:]
-    potential = jnp.broadcast_to(arm_potential[:, None, :], (row_count, planes, columns))
-    fields_all = jnp.concatenate([mass_density[None], momenta, magnetic, potential[None]], axis=0)
-    padded = with_halo(fields_all, (("gz", 2), ("xy", 1)), 2)
-    along_x = padded[:, :, 2:-2, :]
-    along_z = padded[:, 2:-2, :, :]
-    interior = padded[:, 2:-2, 2:-2, :]
+    events = jnp.concatenate([sn_cells, sn_counts[:, None]], axis=1)
+    events = lax.all_gather(events, ("gz", "xy"), axis=0, tiled=True)
+    below_a, above_a = neighbours(jnp.stack([density, momentum[2]]), "gz", 2, 2)
+    below_b, above_b = neighbours(jnp.concatenate([momentum[:2], magnetic]), "gz", 2, 2)
+    raw = jnp.concatenate([density[None], momentum, magnetic], axis=0)
+    before, after = neighbours(raw, "xy", 1, 2)
+    p_before, p_after = neighbours(arm_potential, "xy", 0, 2)
+    row_start = tile_row * row_count
+    plane_start = tile_plane * planes
+    source_x = deposit(events[:, :3], events[:, 3], row_start - 2, row_count + 4, plane_start, planes, depth_all)
+
+    def near(a, b, start):
+        field = jnp.concatenate([a[:1], b[:2], a[1:], b[2:]], axis=0)
+        extra = deposit(events[:, :3], events[:, 3], row_start, row_count, start, 2, depth_all)
+        return field.at[:4].add(extra)
+
+    along_x = jnp.concatenate([before, raw, after], axis=1)
+    along_x = along_x.at[:4].add(source_x)
+    interior = along_x[:, 2:-2]
+    along_z = jnp.concatenate(
+        [near(below_a, below_b, plane_start - 2), interior, near(above_a, above_b, plane_start + planes)], axis=2
+    )
+    mass_density = interior[0]
+    potential = jnp.concatenate([p_before, arm_potential, p_after], axis=0)
     divergence = central_pad(fluxes(along_x[0], along_x[1:4], along_x[4:7], 0), 1)
     divergence = divergence + central_wrap(fluxes(interior[0], interior[1:4], interior[4:7], 1), 3)
     divergence = divergence + central_pad(fluxes(along_z[0], along_z[1:4], along_z[4:7], 2), 2)
-    smooth = second_pad(along_x[:7], 1) + second_wrap(interior[:7], 3) + second_pad(along_z[:7], 2)
-    updated = interior[:7] - time_step * divergence + diffusion * smooth
-    slope_x = central_pad(along_x[7], 0)
-    slope_y = central_wrap(interior[7], 2)
+    smooth = second_pad(along_x, 1) + second_wrap(interior, 3) + second_pad(along_z, 2)
+    updated = interior - time_step * divergence + diffusion * smooth
+    slope_x = central_pad(potential, 0)[:, None, :]
+    slope_y = central_wrap(arm_potential, 1)[:, None, :]
     new_density = updated[0]
     new_momentum = jnp.stack(
         [
@@ -198,18 +170,18 @@
     angle_x = (wave_x[:, None] * wave_x[None, :] % NX).astype(jnp.float32) * (2.0 * math.pi / NX)
     cosine_x = jnp.cos(angle_x)
     sine_x = jnp.sin(angle_x)
-    real_y = jnp.einsum("xzy,yk->zkx", new_density, cosine_y, precision=lax.Precision.HIGHEST)
-    imag_y = -jnp.einsum("xzy,yk->zkx", new_density, sine_y, precision=lax.Precision.HIGHEST)
+    real_y = jnp.einsum("xzy,yk->zkx", new_density, cosine_y, precision=lax.Precision.HIGH)
+    imag_y = -jnp.einsum("xzy,yk->zkx", new_density, sine_y, precision=lax.Precision.HIGH)
     stacked = jnp.stack([real_y, imag_y])
     portion = lax.all_to_all(stacked, "xy", split_axis=2, concat_axis=3, tiled=True)
     real_part = portion[0]
     imag_part = portion[1]
     out_real = jnp.einsum(
-        "zkx,xj->zkj", real_part, cosine_x, precision=lax.Precision.HIGHEST
-    ) + jnp.einsum("zkx,xj->zkj", imag_part, sine_x, precision=lax.Precision.HIGHEST)
+        "zkx,xj->zkj", real_part, cosine_x, precision=lax.Precision.HIGH
+    ) + jnp.einsum("zkx,xj->zkj", imag_part, sine_x, precision=lax.Precision.HIGH)
     out_imag = jnp.einsum(
-        "zkx,xj->zkj", imag_part, cosine_x, precision=lax.Precision.HIGHEST
-    ) - jnp.einsum("zkx,xj->zkj", real_part, sine_x, precision=lax.Precision.HIGHEST)
+        "zkx,xj->zkj", imag_part, cosine_x, precision=lax.Precision.HIGH
+    ) - jnp.einsum("zkx,xj->zkj", real_part, sine_x, precision=lax.Precision.HIGH)
     spectrum = jnp.stack([out_real, out_imag])
     band = spectrum.shape[2]
     wave_ky = tile_row * band + jnp.arange(band, dtype=jnp.int32)

time: 2640 us -> 500 us (0.19)
  waiting for transfers between devices: 1870 us -> 6.05 us
  starting transfers between devices: 294 us -> 15.3 us
  blocking collectives: 0 us -> 123 us
  other arithmetic: 303 us -> 212 us
    ppermute x13 -> x8, waiting for transfers between devices: 1870 us -> 0.02 us  [neighbours(): return (lax.ppermute(last, axis, up), lax.ppermute(leading, axis, down))]
    ppermute x13 -> x8, starting transfers between devices: 289 us -> 10.6 us  [neighbours(): return (lax.ppermute(last, axis, up), lax.ppermute(leading, axis, down))]
    all_gather x0 -> x1, blocking collectives: none -> 123 us  [on_device(): events = lax.all_gather(events, ('gz', 'xy'), axis=0, tiled=True)]
    reduce_sum x0 -> x2, other arithmetic: none -> 73.7 us  [deposit(): jnp.sum(weights, axis=0)]
    unnamed x38 -> x19, other arithmetic: 102 us -> 30 us
    add x4 -> x5, other arithmetic: 108 us -> 58.1 us  [the longest x1 57.5 us: on_device(): updated = interior - time_step * divergence + diffusion * smooth]
    concatenate x4 -> x5, other arithmetic: 39.4 us -> 7.97 us  [the longest x1 3.05 us: on_device(): jnp.concatenate([momentum[:2], magnetic])]
  transfers between devices with their start and end apart: 14 -> 9, of which waited for: 9 -> 1; matrix products, arithmetic and copies ran while one was open for 5% -> 63% of each run, Pallas kernels for 0% -> 0%
where the time goes in v1:
time: 500 us; the launch traced here: 495 us
  other arithmetic  212 us (42%)
  blocking collectives  123 us (25%)
  local copies, waits for them, and re-layouts  100 us (20%)
  matrix products  36.1 us (7%)
  starting transfers between devices  15.3 us (3%)
  waiting for transfers between devices  6.05 us (1%)
    all_gather x1, blocking collectives, on_device(): events = lax.all_gather(events, ('gz', 'xy'), axis=0, tiled=True)  123 us
    reduce_sum x2, other arithmetic, deposit(): jnp.sum(weights, axis=0)  73.7 us
    add x1, other arithmetic, on_device(): updated = interior - time_step * divergence + diffusion * smooth  57.5 us
    unnamed x19, other arithmetic  30 us
    unnamed x90, local copies, waits for them, and re-layouts  21 us
    slice x4, local copies, waits for them, and re-layouts, central_wrap(): jnp.roll(field, -1, axis)  18.8 us
    slice x4, local copies, waits for them, and re-layouts, central_wrap(): jnp.roll(field, -2, axis)  17.3 us
    slice x2, local copies, waits for them, and re-layouts, second_wrap(): return jnp.roll(field, 1, axis) + jnp.roll(field, -1, axis) - 2.0 * field  16.1 us
  transfers between devices with their start and end apart: 9, of which 1 were waited for; matrix products, arithmetic and copies ran while one was open for 63% of the time, Pallas kernels for 0%

profile of v1, /device:TPU:0, one launch (start us, length us, event | category | flops | bytes accessed | tf_op | source)
XLA Modules:
  0.0 495.0 jit_solution(10834765770096026904)
XLA Ops:
  0.6 3.1 copy.39
  4.9 3.1 fusion.20
  8.0 4.5 collective-permute-start.5
  19.2 123.1 %all-gather = s32[32,1,4]{2,1,0:T(1,128)S(1)} all-gather(s32[1,1,4]{2,1,0:T(1,128)S(1)} %add_bitcast_fusion), channel_id=1, replica_groups=mesh['gz'=8,'xy'=4] {'gz','xy'}, dimensions={0}, use_global_device_ids=true | all-gather | bytes 528 | tf_op jit(solution)/shard_map/all_gather | solution.py:126
  154.6 18.2 %fusion.2 = (f32[128,2,512]{2,0,1:T(8,128)}, f32[128,2,512]{2,0,1:T(8,128)}, f32[128,2,512]{2,0,1:T(8,128)}, f32[128,2,512]{2,0,1:T(8,128)S(1)}, f32[128,2,512]{...) fusion(f32[32]{0:T(128)} %get-tuple-element.119, ...), kind=kLoop, calls=%fused_computation.14 | loop fusion | flops 99614720 | bytes 4407936 | tf_op jit(solution)/shard_map/reduce_sum | solution.py:111
  185.2 55.5 %fusion = (f32[132,4,512]{2,1,0:T(4,128)}, f32[132,4,512]{2,1,0:T(4,128)}, f32[132,4,512]{2,1,0:T(4,128)}, f32[132,4,512]{2,1,0:T(4,128)}) fusion(f32[32]{0:T(128)S(1)} %copy-done.29, f32[32,512]{1,0:T(8,128)S(1)} %fusion.67, f32[32,132,4]{0,2,1:T(4,128)} %copy.42, f32[32,4]{0,1:T(4,128)S(1)} %copy-done.27, f32[32,512]{1,0:T(8,128)S(1)} %fusion.63, ...), kind=kLoop, calls=%fused_computation.4 | loop fusion | flops 102727680 | bytes 4541568 | tf_op jit(solution)/shard_map/reduce_sum | solution.py:111
  262.9 12.4 %fusion.111 = (f32[7,128,4,510]{3,1,2,0:T(8,128)}, f32[7,128,4,510]{3,1,2,0:T(8,128)}) fusion(f32[7,128,4,512]{3,1,2,0:T(8,128)} %subtract_dynamic-update-slice_fusion.10), kind=kLoop, calls=%fused_computation.240 | loop fusion | bytes 29245440 | tf_op jit(solution)/shard_map/jit(_roll_static)/slice | solution.py:77
  275.3 4.1 fusion.112
  279.3 5.3 %fusion.114 = (f32[7,128,4,1]{3,1,2,0:T(8,128)}, f32[7,128,4,1]{3,1,2,0:T(8,128)}) fusion(f32[7,128,4,512]{3,1,2,0:T(8,128)} %subtract_dynamic-update-slice_fusion.10), kind=kLoop, calls=%fused_computation.243 | loop fusion | bytes 57344 | tf_op jit(solution)/shard_map/jit(_roll_static)/slice | solution.py:76
  284.7 2.5 fusion.110
  295.1 12.6 %fusion.113 = (f32[7,128,4,511]{3,1,2,0:T(8,128)}, f32[7,128,4,511]{3,1,2,0:T(8,128)}) fusion(f32[7,128,4,512]{3,1,2,0:T(8,128)} %subtract_dynamic-update-slice_fusion.10), kind=kLoop, calls=%fused_computation.242 | loop fusion | bytes 29302784 | tf_op jit(solution)/shard_map/jit(_roll_static)/slice | solution.py:76
  307.7 3.9 subtract_dynamic-update-slice_fusion.5
  311.6 7.6 %slice.574 = f32[7,128,4,512]{3,1,2,0:T(8,128)} slice(f32[7,132,4,512]{3,1,2,0:T(8,128)} %copy-done), slice={[0:7], [2:130], [0:4], [0:512]} | slice | bytes 14680064 | tf_op jit(solution)/shard_map/slice | solution.py:143
  319.2 13.7 %fusion.109 = (f32[7,128,4,511]{3,1,2,0:T(8,128)}, f32[7,128,4,511]{3,1,2,0:T(8,128)}) fusion(f32[7,132,4,512]{3,1,2,0:T(8,128)} %copy-done), kind=kLoop, calls=%fused_computation.238 | loop fusion | bytes 29302784 | tf_op jit(solution)/shard_map/jit(_roll_static)/slice | solution.py:82
  332.9 2.9 collective-permute-start.7
  352.5 2.7 subtract_dynamic-update-slice_fusion.4
  357.6 3.0 add_dynamic-update-slice_fusion
  360.6 2.6 subtract_dynamic-update-slice_fusion.2
  363.2 2.7 subtract_dynamic-update-slice_fusion.1
  367.7 57.5 %fusion.7 = f32[7,128,4,512]{3,1,2,0:T(8,128)} fusion(f32[7,128,2,512]{3,1,2,0:T(8,128)S(1)} %fusion.22, f32[7,128,4,512]{3,1,2,0:T(8,128)} %slice.574, f32[7,128,2,512]{3,1,2,0:T(8,128)} %copy-done.5, f32[7,132,4,512]{3,1,2,0:T(8,128)} %copy-done, f32[7,128,8,512]{3,1,2,0:T(8,128)} %subtract_dynamic-update-slice_fusion, ...), kind=kLoop, calls=%fused_computation.22 | loop fusion | flops 69730304 | bytes 139460608 | tf_op jit(solution)/shard_map/add | solution.py:153
  425.2 6.7 %fusion.25 = f32[1,4,512,128]{3,2,1,0:T(8,128)S(1)} fusion(f32[7,128,4,512]{3,1,2,0:T(8,128)} %fusion.7), kind=kOutput, calls=%fused_computation.81 | convolution fusion | flops 809238528 | bytes 2097152 | tf_op jit(solution)/shard_map/xzy,yk->zkx/dot_general | solution.py:174
  432.0 6.7 %convolution_bitcast_fusion = f32[1,4,512,128]{3,2,1,0:T(8,128)S(1)} fusion(f32[7,128,4,512]{3,1,2,0:T(8,128)} %fusion.7), kind=kOutput, calls=%fused_computation.82 | convolution fusion | flops 808976384 | bytes 2097152 | tf_op jit(solution)/shard_map/xzy,yk->zkx/dot_general | solution.py:173
  438.9 2.8 copy.53
  441.7 4.7 all-to-all-start
  453.1 3.7 copy.56
  456.8 3.7 copy.57
  460.5 6.0 %all-to-all-done = f32[2,4,512,128]{3,1,0,2:T(4,128)} async-done(((f32[2,4,512,128]{3,1,0,2:T(4,128)}), f32[2,4,512,128]{3,1,0,2:T(4,128)}, u32[]{:S(2)}, u32[]{:S(2)}) %all-to-all-start) | async-done | bytes 2097184 | tf_op jit(solution)/shard_map/all_to_all | solution.py:176
  466.5 2.9 copy.74
  470.0 5.8 %fusion.36 = f32[4,128,512]{2,1,0:T(8,128)} fusion(f32[4,128,512]{2,1,0:T(8,128)S(1)} %squeeze.8), kind=kOutput, calls=%fused_computation.107 | convolution fusion | flops 808976384 | bytes 2097152 | tf_op jit(solution)/shard_map/zkx,xj->zkj/dot_general | solution.py:182
  476.3 5.7 %fusion.38 = f32[4,128,512]{2,1,0:T(8,128)S(1)} fusion(f32[4,128,512]{2,1,0:T(8,128)S(1)} %squeeze.7), kind=kOutput, calls=%fused_computation.109 | convolution fusion | flops 808976384 | bytes 2097152 | tf_op jit(solution)/shard_map/zkx,xj->zkj/dot_general | solution.py:179
  482.1 5.5 %fusion.23 = f32[1,4,128,512]{3,2,1,0:T(8,128)S(1)} fusion(f32[4,128,512]{2,1,0:T(8,128)S(1)} %copy-done.33, f32[4,128,512]{2,1,0:T(8,128)S(1)} %squeeze.7), kind=kOutput, calls=%fused_computation.77 | convolution fusion | flops 809238528 | bytes 3145728 | tf_op jit(solution)/shard_map/zkx,xj->zkj/dot_general | solution.py:184
  487.6 5.5 %fusion.24 = f32[1,4,128,512]{3,2,1,0:T(8,128)S(1)} fusion(f32[4,128,512]{2,1,0:T(8,128)S(1)} %fusion.38, f32[4,128,512]{2,1,0:T(8,128)S(1)} %squeeze.8), kind=kOutput, calls=%fused_computation.79 | convolution fusion | flops 809238528 | bytes 3145728 | tf_op jit(solution)/shard_map/zkx,xj->zkj/dot_general | solution.py:181
  (183 shorter events, 91.9 us)
Async XLA Ops:
  0.6 3.2 copy-start.12
  4.9 10.3 %copy-start.3 = (f32[3,128,4,512]{3,1,2,0:T(8,128)}, f32[3,128,4,512]{3,1,2,0:T(8,128)S(1)}, u32[]{:S(2)}) copy-start(f32[3,128,4,512]{3,1,2,0:T(8,128)S(1)} %copy.40) | copy-start | bytes 9437188
  4.9 7.6 %copy-start.22 = (f32[128,4,512]{2,1,0:T(4,128)S(1)}, f32[128,4,512]{2,1,0:T(4,128)}, u32[]{:S(2)}) copy-start(f32[128,4,512]{2,1,0:T(4,128)} %param.12) | copy-start | bytes 3145732
  8.0 330.3 %collective-permute-start.5 = (f32[5,128,2,512]{3,1,2,0:T(8,128)}, f32[5,128,2,512]{3,1,2,0:T(8,128)}, u32[]{:S(2)}, u32[]{:S(2)}) collective-permute-start(f32[5,128,2,512]{3,1,2,0:T(8,128)} %get-tuple-element.97), channel_id=1, source_target_pairs={{4,0},{8,4},{12,8},{16,12},{20,16},{24,20},{28,24},{0,28},{5,1},{9... | collective-permute-start | bytes 7864328 | tf_op jit(solution)/shard_map/ppermute | solution.py:26
  14.6 4.6 copy-start.32
  14.6 136.6 %copy-start.8 = (f32[128,512]{1,0:T(8,128)S(1)}, f32[128,512]{1,0:T(8,128)}, u32[]{:S(2)}) copy-start(f32[128,512]{1,0:T(8,128)} %param.15) | copy-start | bytes 786436
  14.6 318.3 %collective-permute-start.4 = (f32[2,128,2,512]{3,1,2,0:T(8,128)}, f32[2,128,2,512]{3,1,2,0:T(8,128)}, u32[]{:S(2)}, u32[]{:S(2)}) collective-permute-start(f32[2,128,2,512]{3,1,2,0:T(8,128)} %get-tuple-element.101), channel_id=1, source_target_pairs={{4,0},{8,4},{12,8},{16,12},{20,16},{24,20},{28,24},{0,28},{5,1},{9... | collective-permute-start | bytes 3145736 | tf_op jit(solution)/shard_map/ppermute | solution.py:26
  16.1 229.3 %collective-permute-start.1 = (f32[7,2,4,512]{3,1,2,0:T(2,128)}, f32[7,2,4,512]{3,1,2,0:T(2,128)}, u32[]{:S(2)}, u32[]{:S(2)}) collective-permute-start(f32[7,2,4,512]{3,1,2,0:T(2,128)} %get-tuple-element.95), channel_id=1, source_target_pairs={{1,0},{2,1},{3,2},{0,3},{5,4},{6,5},{7,6},{4,7},{9,8},{10,9},{11,1... | collective-permute-start | bytes 344072 | tf_op jit(solution)/shard_map/ppermute | solution.py:26
  18.5 226.9 %collective-permute-start = (f32[7,2,4,512]{3,1,2,0:T(2,128)}, f32[7,2,4,512]{3,1,2,0:T(2,128)}, u32[]{:S(2)}, u32[]{:S(2)}) collective-permute-start(f32[7,2,4,512]{3,1,2,0:T(2,128)} %get-tuple-element.94), channel_id=1, source_target_pairs={{0,1},{1,2},{2,3},{3,0},{4,5},{5,6},{6,7},{7,4},{8,9},{9,10},{10,1... | collective-permute-start | bytes 344072 | tf_op jit(solution)/shard_map/ppermute | solution.py:26
  18.5 323.1 %collective-permute-start.3 = (f32[5,128,2,512]{3,1,2,0:T(8,128)}, f32[5,128,2,512]{3,1,2,0:T(8,128)}, u32[]{:S(2)}, u32[]{:S(2)}) collective-permute-start(f32[5,128,2,512]{3,1,2,0:T(8,128)} %get-tuple-element.96), channel_id=1, source_target_pairs={{0,4},{4,8},{8,12},{12,16},{16,20},{20,24},{24,28},{28,0},{1,5},{5... | collective-permute-start | bytes 7864328 | tf_op jit(solution)/shard_map/ppermute | solution.py:26
  172.8 12.3 %copy-start.27 = (f32[32,4]{0,1:T(4,128)S(1)}, f32[32,4]{0,1:T(4,128)}, u32[]{:S(2)}) copy-start(f32[32,4]{0,1:T(4,128)} %fusion.83) | copy-start | bytes 1540
  172.8 12.3 %copy-start.29 = (f32[32]{0:T(128)S(1)}, f32[32]{0:T(128)}, u32[]{:S(2)}) copy-start(f32[32]{0:T(128)} %get-tuple-element.119) | copy-start | bytes 388
  240.7 3.2 copy-start.31
  240.7 4.7 copy-start.4
  240.7 4.7 copy-start.7
  245.4 91.7 %collective-permute-start.2 = (f32[2,128,2,512]{3,1,2,0:T(8,128)}, f32[2,128,2,512]{3,1,2,0:T(8,128)}, u32[]{:S(2)}, u32[]{:S(2)}) collective-permute-start(f32[2,128,2,512]{3,1,2,0:T(8,128)} %get-tuple-element.100), channel_id=1, source_target_pairs={{0,4},{4,8},{8,12},{12,16},{16,20},{20,24},{24,28},{28,0},{1,5},{5... | collective-permute-start | bytes 3145736 | tf_op jit(solution)/shard_map/ppermute | solution.py:26
  245.4 202.7 %collective-permute-start.6 = (f32[2,512]{1,0:T(2,128)}, f32[2,512]{1,0:T(2,128)}, u32[]{:S(2)}, u32[]{:S(2)}) collective-permute-start(f32[2,512]{1,0:T(2,128)} %get-tuple-element.107), channel_id=1, source_target_pairs={{0,1},{1,2},{2,3},{3,0},{4,5},{5,6},{6,7},{7,4},{8,9},{9,10},{10,1... | collective-permute-start | bytes 12296 | tf_op jit(solution)/shard_map/ppermute | solution.py:26
  249.7 11.5 %copy-start = (f32[7,132,4,512]{3,1,2,0:T(8,128)}, f32[7,132,4,512]{3,1,2,0:T(8,128)S(1)}, u32[]{:S(2)}) copy-start(f32[7,132,4,512]{3,1,2,0:T(8,128)S(1)} %get-tuple-element.76) | copy-start | bytes 22708228
  249.7 11.5 %copy-start.2 = (f32[4,132,4,512]{3,1,2,0:T(8,128)}, f32[4,132,4,512]{3,1,2,0:T(8,128)S(1)}, u32[]{:S(2)}) copy-start(f32[4,132,4,512]{3,1,2,0:T(8,128)S(1)} %get-tuple-element.77) | copy-start | bytes 12976132
  275.3 9.4 %copy-start.1 = (f32[7,132,4,512]{3,1,2,0:T(8,128)S(1)}, f32[7,132,4,512]{3,1,2,0:T(8,128)}, u32[]{:S(2)}) copy-start(f32[7,132,4,512]{3,1,2,0:T(8,128)} %copy-done) | copy-start | bytes 22708228
  275.3 11.9 %slice-start = ((s8[4456448]{0:T(1024)(128)(4,1)}), s8[4194304]{0:T(1024)(128)(4,1)S(1)}, s32[]{:S(2)}) async-start(s8[4456448]{0:T(1024)(128)(4,1)} %bitcast.78), calls=%async_computation.1 | async-start | bytes 8388608
  279.3 7.8 %slice-start.1 = ((s8[4456448]{0:T(1024)(128)(4,1)}), s8[262144]{0:T(1024)(128)(4,1)S(1)}, s32[]{:S(2)}) async-start(s8[4456448]{0:T(1024)(128)(4,1)} %bitcast.78), calls=%async_computation.2 | async-start | bytes 524288
  332.9 115.2 %collective-permute-start.7 = (f32[2,512]{1,0:T(2,128)S(1)}, f32[2,512]{1,0:T(2,128)S(1)}, u32[]{:S(2)}, u32[]{:S(2)}) collective-permute-start(f32[2,512]{1,0:T(2,128)S(1)} %get-tuple-element.106), channel_id=1, source_target_pairs={{1,0},{2,1},{3,2},{0,3},{5,4},{6,5},{7,6},{4,7},{9,8},{10,9},{11,1... | collective-permute-start | bytes 12296 | tf_op jit(solution)/shard_map/ppermute | solution.py:26
  345.1 3.3 slice-start.3
  438.9 7.6 %copy-start.9 = (f32[128,512]{1,0:T(8,128)S(1)}, f32[128,512]{1,0:T(8,128)}, u32[]{:S(2)}) copy-start(f32[128,512]{1,0:T(8,128)} %param.15) | copy-start | bytes 786436
  441.7 5.0 %copy-start.23 = (f32[128,2]{1,0:T(8,128)S(1)}, f32[128,2]{1,0:T(8,128)}, u32[]{:S(2)}) copy-start(f32[128,2]{1,0:T(8,128)} %get-tuple-element.110) | copy-start | bytes 3076
  441.7 5.0 %copy-start.24 = (f32[128,2]{1,0:T(8,128)S(1)}, f32[128,2]{1,0:T(8,128)}, u32[]{:S(2)}) copy-start(f32[128,2]{1,0:T(8,128)} %get-tuple-element.111) | copy-start | bytes 3076
  441.7 7.3 %slice-start.4 = ((s8[7340032]{0:T(1024)(128)(4,1)}), s8[3145728]{0:T(1024)(128)(4,1)S(1)}, s32[]{:S(2)}) async-start(s8[7340032]{0:T(1024)(128)(4,1)} %bitcast.82), calls=%async_computation.5 | async-start | bytes 6291456
  441.7 24.8 %all-to-all-start = ((f32[2,4,512,128]{3,1,0,2:T(4,128)}), f32[2,4,512,128]{3,1,0,2:T(4,128)}, u32[]{:S(2)}, u32[]{:S(2)}) async-start(f32[2,4,512,128]{3,1,0,2:T(4,128)} %copy.53), calls=%async_computation | async-start | bytes 4194304 | tf_op jit(solution)/shard_map/all_to_all | solution.py:176
  453.1 3.7 slice-start.6
  476.3 5.8 %copy-start.33 = (f32[4,128,512]{2,1,0:T(8,128)S(1)}, f32[4,128,512]{2,1,0:T(8,128)}, u32[]{:S(2)}) copy-start(f32[4,128,512]{2,1,0:T(8,128)} %fusion.36) | copy-start | bytes 3145732
  482.1 11.1 %copy-start.21 = (f32[128,512]{1,0:T(8,128)S(1)}, f32[128,512]{1,0:T(8,128)}, u32[]{:S(2)}) copy-start(f32[128,512]{1,0:T(8,128)} %select_multiply_fusion) | copy-start | bytes 786436
  (18 other events, 40.8 us)

commit v2 on v1

v2 whole, which is shorter than its diff:
```python
import functools
import math

import jax
import jax.numpy as jnp
import ml_dtypes
import numpy as np
from jax import lax
from jax.experimental import pallas as pl
from jax.experimental.pallas import tpu as pltpu
from jax.sharding import PartitionSpec as P

NX = 512
RADIUS = 16
IMPULSE = 2.0 / 16
TIME_STEP = 0.1
DIFFUSION = 0.05
NEAR = 8.0 * TIME_STEP / 12.0
FAR = TIME_STEP / 12.0
VMEM = 56 * 1024 * 1024


def pair(ref, *index):
    return jnp.concatenate([ref[(*index[:-1], 0, index[-1])], ref[(*index[:-1], 1, index[-1])]], axis=0)


def unpair(ref, value, *index):
    ref[(*index[:-1], 0, index[-1])] = value[:4]
    ref[(*index[:-1], 1, index[-1])] = value[4:]


def slots(shape):
    sub = lax.broadcasted_iota(jnp.int32, shape, len(shape) - 2)
    return jnp.where(sub >= 4, sub - 4, sub)


def turn(value, shift, axis):
    return pltpu.roll(value, shift % value.shape[axis], axis)


def gather_planes(values, plane):
    slot = slots(values[0].shape)
    out = turn(values[-1], len(values) - 1 - plane, 0)
    for c in reversed(range(len(values) - 1)):
        out = jnp.where(slot == c, turn(values[c], c - plane, 0), out)
    return out


def fluxes(rho, m, b, k):
    inv = 1.0 / rho
    v = [m[i] * inv for i in range(3)]
    total = rho + 0.5 * (b[0] * b[0] + b[1] * b[1] + b[2] * b[2])
    push = [m[i] * v[k] - b[i] * b[k] + (total if i == k else 0.0) for i in range(3)]
    turned = [None if i == k else v[k] * b[i] - b[k] * v[i] for i in range(3)]
    return push + turned


def pack_kernel(rho_ref, mz_ref, bx_ref, up_ref, down_ref):
    half = rho_ref.shape[1]

    def body(p, _):
        rho, mz, bx = pair(rho_ref, p), pair(mz_ref, 0, p), pair(bx_ref, 0, p)
        slot = slots(rho.shape)
        up = jnp.where(slot == 2, mz, gather_planes([rho, mz, mz, bx], 3))
        down = jnp.where(slot == 2, turn(mz, 1, 0), gather_planes([rho, mz, mz, bx], 0))
        unpair(up_ref, up, p)
        unpair(down_ref, down, p)
        return 0

    lax.fori_loop(0, half, body, 0)


def state_kernel(
    ev_ref, at_ref, rho_ref, mom_ref, mag_ref, before_ref, after_ref,
    u_ref, sb_ref, sa_ref, up_near, down_near, up_far, down_far, up_last, down_last, *, depth,
):
    half, ny = rho_ref.shape[1], rho_ref.shape[3]
    rows, events = 2 * half, ev_ref.shape[0] // 4
    row_start, plane_start = at_ref[0], at_ref[1]

    def raw(f, h, p):
        if f == 0:
            return rho_ref[h, p]
        return mom_ref[f - 1, h, p] if f < 4 else mag_ref[f - 4, h, p]

    def fill(p, _):
        for f in range(7):
            u_ref[f, p + 2] = jnp.concatenate([raw(f, 0, p), raw(f, 1, p)], axis=0)
        return 0

    lax.fori_loop(0, half, fill, 0)
    for f in range(7):
        for j in range(2):
            u_ref[f, j] = jnp.concatenate([before_ref[f, j], raw(f, 0, half - 2 + j)], axis=0)
            u_ref[f, half + 2 + j] = jnp.concatenate([raw(f, 1, j), after_ref[f, j]], axis=0)
    sb_ref[...] = jnp.zeros_like(sb_ref)
    sa_ref[...] = jnp.zeros_like(sa_ref)

    shape = (4, 8, 128)
    slot = slots(shape)
    sub = lax.broadcasted_iota(jnp.int32, shape, 1)
    step = lax.broadcasted_iota(jnp.int32, shape, 0)
    lane = lax.broadcasted_iota(jnp.int32, shape, 2)

    def wrapped(distance, size):
        distance = jnp.where(distance >= size // 2, distance - size, distance)
        return jnp.where(distance < -(size // 2), distance + size, distance)

    def event(e, _):
        row, col, plane, count = (ev_ref[4 * e + i] for i in range(4))
        rel = wrapped(row - row_start - half, NX)
        rel = rel + half

        @pl.when((count > 0) & (rel > -2 - RADIUS) & (rel < rows + 2 + RADIUS))
        def _():
            base = plane_start - plane
            dz = wrapped(slot + base, depth).astype(jnp.float32)
            dzb = wrapped(jnp.where(slot == 2, -2, -1) + base, depth).astype(jnp.float32)
            dza = wrapped(jnp.where(slot == 2, 5, 4) + base, depth).astype(jnp.float32)
            share = lambda d: jnp.where(slot == 0, 1.0, jnp.where(slot == 3, 0.0, IMPULSE * d))
            first = jnp.bitwise_and(col - RADIUS, ny - 1) // 128
            second = jnp.bitwise_and(col + RADIUS - 1, ny - 1) // 128

            def tile(t, _):
                index = jnp.where(t == 0, first, second)
                lanes = pl.ds(pl.multiple_of(index * 128, 128), 128)
                dy = wrapped(lane + index * 128 - col, ny).astype(jnp.float32)
                dy2 = dy * dy
                for h in range(2):
                    weight = jnp.where((sub >= 4) == (h == 1), count, 0).astype(jnp.float32)
                    low = jnp.clip(rel - RADIUS + 1 - h * half + 2, 0, half + 4) // 4
                    high = (jnp.clip(rel + RADIUS - 1 - h * half + 2, -1, half + 3) + 4) // 4

                    def chunk(n, _):
                        q = pl.ds(n * 4, 4)
                        dx = (step + (n * 4 - 2 + h * half - rel)).astype(jnp.float32)
                        flat = dx * dx + dy2
                        size = lambda d: jnp.maximum(1.0 - (flat + d * d) * (1.0 / (RADIUS * RADIUS)), 0.0) * weight
                        w = size(dz)
                        u_ref[0, q, :, lanes] += w
                        w = w * IMPULSE
                        u_ref[1, q, :, lanes] += w * dx
                        u_ref[2, q, :, lanes] += w * dy
                        u_ref[3, q, :, lanes] += w * dz
                        sb_ref[q, :, lanes] += size(dzb) * share(dzb)
                        sa_ref[q, :, lanes] += size(dza) * share(dza)
                        return 0

                    lax.fori_loop(low, high, chunk, 0)
                return 0

            lax.fori_loop(0, jnp.where(first == second, 1, 2), tile, 0)

        return 0

    lax.fori_loop(0, events, event, 0)

    def messages(p, _):
        u = [u_ref[f, p + 2] for f in range(7)]
        near = [u[1], u[2], u[5], u[6]]
        unpair(up_near, gather_planes(near, 3), p)
        unpair(down_near, gather_planes(near, 0), p)
        f = fluxes(u[0], u[1:4], u[4:7], 2)
        unpair(up_far, gather_planes(f[:4], 2), p)
        unpair(down_far, gather_planes(f[:4], 1), p)
        for ref, plane in ((up_last, 2), (down_last, 1)):
            low, high = turn(f[4], -plane, 0), turn(f[4], -plane - 3, 0)
            ref[p] = jnp.where(slots(low.shape) == 0, low, high)[:2]
        return 0

    lax.fori_loop(0, half, messages, 0)


def ends(below, above, c, fill):
    slot = slots(below.shape)
    rest = jnp.where(slot == 3, turn(above, 3 - c, 0), fill)
    return jnp.where(slot == 0, turn(below, -c, 0), rest)


def signs(shape):
    slot = slots(shape)
    return jnp.where(slot == 0, 1.0, jnp.where(slot == 3, -1.0, 0.0))


def along_y(f, u):
    low, high = NEAR * f + DIFFUSION * u, DIFFUSION * u - NEAR * f
    far = FAR * f
    return turn(low, 1, 1) + turn(high, -1, 1) + turn(far, -2, 1) - turn(far, 2, 1)


def along_z(f, u):
    slot = slots(u.shape)
    part = lambda keep, v: jnp.where(keep, v, 0.0)
    if f is None:
        return part(slot >= 1, turn(DIFFUSION * u, 1, 0)) + part(slot <= 2, turn(DIFFUSION * u, -1, 0))
    low, high = NEAR * f + DIFFUSION * u, DIFFUSION * u - NEAR * f
    far = FAR * f
    return (
        part(slot >= 1, turn(low, 1, 0)) + part(slot <= 2, turn(high, -1, 0))
        + part(slot <= 1, turn(far, -2, 0)) - part(slot >= 2, turn(far, 2, 0))
    )


def near_planes(f, u, sign):
    outer = DIFFUSION * u
    if f is None:
        return outer
    slot = slots(u.shape)
    t = (FAR * sign) * f
    inner = jnp.where(slot == 1, turn(t, 1, 0), jnp.where(slot == 2, turn(t, -1, 0), 0.0))
    return outer + 8.0 * t - inner


def density_kernel(u_ref, below_ref, above_ref, sb_ref, sa_ref, order_ref, high_ref, low_ref, out_ref, wave_ref, d_ref):
    half = below_ref.shape[1]
    rows = 2 * half

    def body(p, _):
        rho, my, mz = u_ref[0, p + 2], u_ref[2, p + 2], u_ref[3, p + 2]
        below, above = pair(below_ref, p) + sb_ref[p + 2], pair(above_ref, p) + sa_ref[p + 2]
        slot, sign = slots(rho.shape), signs(rho.shape)
        new = rho * (1.0 - 6.0 * DIFFUSION)
        new += DIFFUSION * (u_ref[0, p + 1] + u_ref[0, p + 3])
        new += NEAR * (u_ref[1, p + 1] - u_ref[1, p + 3]) + FAR * (u_ref[1, p + 4] - u_ref[1, p])
        new += along_y(my, rho) + along_z(mz, rho)
        new += near_planes(ends(below, above, 1, 0.0), ends(below, above, 0, 0.0), sign)
        new -= (FAR * sign) * ends(below, above, 2, 0.0)
        unpair(out_ref, new, p)
        d_ref[pl.ds(pl.multiple_of(p * 8, 8), 8), :] = new
        return 0

    lax.fori_loop(0, half, body, 0)
    d = d_ref[...]
    order = order_ref[...]
    dot = functools.partial(jnp.dot, preferred_element_type=jnp.float32)
    high = d.astype(jnp.bfloat16)
    low = (d - high.astype(jnp.float32)).astype(jnp.bfloat16)
    high = dot(order, high).astype(jnp.bfloat16)
    low = dot(order, low).astype(jnp.bfloat16)
    across = lambda a, b: lax.dot_general(a, b, (((1,), (1,)), ((), ())), preferred_element_type=jnp.float32)
    for part in range(2):
        c_high, c_low = high_ref[part], low_ref[part]
        for z in range(4):
            r_high, r_low = high[z * rows : (z + 1) * rows], low[z * rows : (z + 1) * rows]
            wave_ref[part, z] = across(c_high, r_high) + across(c_low, r_high) + across(c_high, r_low)


def main_kernel(u_ref, ba_ref, aa_ref, sb_ref, sa_ref, bn_ref, an_ref, g_ref, mom_ref, mag_ref, f_ref):
    chunk = ba_ref.shape[1]
    start = pl.program_id(0) * chunk
    total = u_ref.shape[1]
    kept = (0, 1, 2, 4, 5)

    @pl.when(pl.program_id(0) == 0)
    def _():
        def fx(q, _):
            u = [u_ref[f, q] for f in range(7)]
            f = fluxes(u[0], u[1:4], u[4:7], 0)
            for i, c in enumerate(kept):
                f_ref[i, q] = f[c]
            return 0

        lax.fori_loop(0, total, fx, 0)

    def body(r, _):
        q = start + r + 2
        u = [u_ref[f, q] for f in range(7)]
        fy = fluxes(u[0], u[1:4], u[4:7], 1)
        fz = fluxes(u[0], u[1:4], u[4:7], 2)
        sign = signs(u[0].shape)
        ba, aa = pair(ba_ref, r) + sb_ref[q], pair(aa_ref, r) + sa_ref[q]
        bn, an = pair(bn_ref, r), pair(an_ref, r)
        hm = [ends(bn, an, 0, 0.0), ends(bn, an, 1, 0.0), ends(ba, aa, 1, 0.0)]
        hb = [ends(ba, aa, 3, 0.0), ends(bn, an, 2, 0.0), ends(bn, an, 3, 0.0)]
        fh = fluxes(ends(ba, aa, 0, 1.0), hm, hb, 2)
        halo = hm + hb
        for c in range(6):
            field = u[c + 1]
            new = field * (1.0 - 6.0 * DIFFUSION)
            new += DIFFUSION * (u_ref[c + 1, q - 1] + u_ref[c + 1, q + 1])
            if c in kept:
                i = kept.index(c)
                new += NEAR * (f_ref[i, q - 1] - f_ref[i, q + 1]) + FAR * (f_ref[i, q + 2] - f_ref[i, q - 2])
            if fy[c] is None:
                new += DIFFUSION * (turn(field, 1, 1) + turn(field, -1, 1))
            else:
                new += along_y(fy[c], field)
            new += along_z(fz[c], field)
            new += near_planes(fh[c], halo[c], sign)
            if c < 2:
                g = [jnp.broadcast_to(g_ref[c, h, r], (4, field.shape[1])) for h in range(2)]
                new += u[0] * jnp.concatenate(g, axis=0)
            if c < 3:
                unpair(mom_ref, new, c, r)
            else:
                unpair(mag_ref, new, c - 3, r)
        return 0

    lax.fori_loop(0, chunk, body, 0)


def far_kernel(bf_ref, af_ref, bl_ref, al_ref, mom_in, mag_in, mom_ref, mag_ref):
    chunk = bf_ref.shape[1]

    def body(r, _):
        below, above = pair(bf_ref, r), pair(af_ref, r)
        sign = FAR * signs(below.shape)
        sub = lax.broadcasted_iota(jnp.int32, below.shape, 0)
        bl, al = bl_ref[r], al_ref[r]
        last = jnp.zeros_like(below)
        for h in range(2):
            last = jnp.where(sub == 4 * h, bl[h : h + 1], jnp.where(sub == 4 * h + 3, al[h : h + 1], last))
        for c in range(4):
            term = sign * ends(below, above, c, 0.0)
            if c < 3:
                unpair(mom_ref, pair(mom_in, c, r) - term, c, r)
            else:
                unpair(mag_ref, pair(mag_in, 0, r) - term, 0, r)
        unpair(mag_ref, pair(mag_in, 1, r) - sign * last, 1, r)
        return 0

    lax.fori_loop(0, chunk, body, 0)


def modes_kernel(at_ref, w_ref, ch_ref, cl_ref, sh_ref, sl_ref, out_ref):
    dot = functools.partial(jnp.dot, preferred_element_type=jnp.float32)

    def split(x):
        high = x.astype(jnp.bfloat16)
        return high, (x - high.astype(jnp.float32)).astype(jnp.bfloat16)

    re, im = split(w_ref[0, 0]), split(w_ref[1, 0])
    times = lambda x, h, l: dot(x[0], h[...]) + dot(x[0], l[...]) + dot(x[1], h[...])
    scale = 1.0 / math.sqrt(NX * w_ref.shape[3])
    shape = out_ref.shape[2:]
    ky = lax.broadcasted_iota(jnp.int32, shape, 0) + at_ref[2]
    kx = lax.broadcasted_iota(jnp.int32, shape, 1)
    keep = jnp.where((ky == 0) & (kx == 0), 0.0, scale)
    out_ref[0, 0] = (times(re, ch_ref, cl_ref) + times(im, sh_ref, sl_ref)) * keep
    out_ref[1, 0] = (times(im, ch_ref, cl_ref) - times(re, sh_ref, sl_ref)) * keep


def cost(flops, bytes_accessed):
    return pl.CostEstimate(flops=int(flops), bytes_accessed=int(bytes_accessed), transcendentals=0)


def tables(size):
    angle = (np.outer(np.arange(size), np.arange(size)) % size) * (2.0 * np.pi / size)
    result = []
    for table in (np.cos(angle), np.sin(angle)):
        high = table.astype(np.float32).astype(ml_dtypes.bfloat16)
        low = (table - high.astype(np.float64)).astype(np.float32).astype(ml_dtypes.bfloat16)
        result += [high, low]
    return result


def row_order(half):
    matrix = np.zeros((8 * half, 8 * half), np.float32)
    for z in range(4):
        for h in range(2):
            for p in range(half):
                matrix[(z * 2 + h) * half + p, p * 8 + h * 4 + z] = 1.0
    return matrix.astype(ml_dtypes.bfloat16)


def shift(block, axis, step):
    n = lax.axis_size(axis)
    return lax.ppermute(block, axis, [(i, (i + step) % n) for i in range(n)])


def on_device(density, momentum, magnetic, arm_potential, sn_cells, sn_counts):
    rows, planes, ny = density.shape
    half = rows // 2
    layers, across = lax.axis_size("gz"), lax.axis_size("xy")
    devices = layers * across
    tile_row, tile_plane = lax.axis_index("xy"), lax.axis_index("gz")
    field = rows * planes * ny
    f32 = jnp.float32
    shape = jax.ShapeDtypeStruct
    whole = pl.BlockSpec(memory_space=pltpu.VMEM)
    smem = pl.BlockSpec(memory_space=pltpu.SMEM)
    params = pltpu.CompilerParams(vmem_limit_bytes=VMEM)
    message = shape((2, half, planes, ny), f32)

    slots_here = sn_cells.shape[0]
    mine = jnp.concatenate([sn_cells, sn_counts[:, None]], axis=1).reshape(1, 1, 4 * slots_here)
    mine = jnp.pad(mine, ((0, 0), (0, 0), (0, -(4 * slots_here) % 128)))
    events = lax.all_to_all(
        jnp.broadcast_to(mine, (devices, 1, mine.shape[2])), ("gz", "xy"), split_axis=0, concat_axis=0, tiled=True
    )
    events = events[:, 0, : 4 * slots_here].reshape(-1)
    at = jnp.stack([tile_row * rows, tile_plane * planes, tile_row * (ny // across)]).astype(jnp.int32)

    rho = density.reshape(2, half, planes, ny)
    mom = momentum.reshape(3, 2, half, planes, ny)
    mag = magnetic.reshape(3, 2, half, planes, ny)

    edge = lambda s: jnp.concatenate([density[None, s], momentum[:, s], magnetic[:, s]], axis=0)
    before = shift(edge(slice(rows - 2, rows)), "xy", 1)
    after = shift(edge(slice(0, 2)), "xy", -1)
    p_before = shift(arm_potential[rows - 2 :], "xy", 1)
    p_after = shift(arm_potential[:2], "xy", -1)

    one = lambda f: pl.BlockSpec((1, 2, half, planes, ny), lambda i, f=f: (f, 0, 0, 0, 0))
    full = lambda s: pl.BlockSpec(s, lambda i: (0,) * len(s))
    up, down = pl.pallas_call(
        pack_kernel,
        grid=(1,),
        in_specs=[full(message.shape), one(2), one(0)],
        out_specs=[full(message.shape)] * 2,
        out_shape=[message] * 2,
        compiler_params=params,
        cost_estimate=cost(20 * field, 5 * 4 * field),
        name="pack",
    )(rho, mom, mag)
    below_a, above_a = shift(up, "gz", 1), shift(down, "gz", -1)

    side = shape((half + 4, 8, ny), f32)
    last = shape((half, 2, ny), f32)
    state, sb, sa, up_n, down_n, up_f, down_f, up_l, down_l = pl.pallas_call(
        functools.partial(state_kernel, depth=planes * layers),
        in_specs=[smem, smem] + [whole] * 5,
        out_specs=[whole] * 9,
        out_shape=[shape((7, half + 4, 8, ny), f32), side, side] + [message] * 4 + [last] * 2,
        compiler_params=params,
        cost_estimate=cost(100 * field, 21 * 4 * field),
        name="state",
    )(events, at, rho, mom, mag, before, after)
    below_n, above_n = shift(up_n, "gz", 1), shift(down_n, "gz", -1)
    below_f, above_f = shift(up_f, "gz", 1), shift(down_f, "gz", -1)
    below_l, above_l = shift(up_l, "gz", 1), shift(down_l, "gz", -1)

    cos_high, cos_low, sin_high, sin_low = tables(ny)
    new_density, wave = pl.pallas_call(
        density_kernel,
        grid=(1,),
        in_specs=[
            full((4, half + 4, 8, ny)), full(message.shape), full(message.shape), full(side.shape), full(side.shape),
            full((8 * half, 8 * half)), full((2, ny, ny)), full((2, ny, ny)),
        ],
        out_specs=[full(message.shape), full((2, planes, ny, rows))],
        out_shape=[message, shape((2, planes, ny, rows), f32)],
        scratch_shapes=[pltpu.VMEM((8 * half, ny), f32)],
        compiler_params=params,
        cost_estimate=cost(60 * field, 13 * 4 * field),
        name="density",
    )(
        state, below_a, above_a, sb, sa, row_order(half), np.stack([cos_high, -sin_high]), np.stack([cos_low, -sin_low]),
    )
    portion = lax.all_to_all(wave, "xy", split_axis=2, concat_axis=3, tiled=True)

    p_all = jnp.concatenate([p_before, arm_potential, p_after], axis=0)
    grad_x = NEAR * (p_all[1:-3] - p_all[3:-1]) + FAR * (p_all[4:] - p_all[:-4])
    grad_y = NEAR * (jnp.roll(arm_potential, 1, 1) - jnp.roll(arm_potential, -1, 1)) + FAR * (
        jnp.roll(arm_potential, -2, 1) - jnp.roll(arm_potential, 2, 1)
    )
    gradient = jnp.stack([grad_x, grad_y]).reshape(2, 2, half, 1, ny)

    chunk = math.gcd(half, 8)
    steps = half // chunk
    halo = pl.BlockSpec((2, chunk, planes, ny), lambda i: (0, i, 0, 0))
    three = pl.BlockSpec((3, 2, chunk, planes, ny), lambda i: (0, 0, i, 0, 0))
    new_mom, new_mag = pl.pallas_call(
        main_kernel,
        grid=(steps,),
        in_specs=[
            full((7, half + 4, 8, ny)), halo, halo, full(side.shape), full(side.shape), halo, halo,
            pl.BlockSpec((2, 2, chunk, 1, ny), lambda i: (0, 0, i, 0, 0)),
        ],
        out_specs=[three, three],
        out_shape=[shape((3, 2, half, planes, ny), f32)] * 2,
        scratch_shapes=[pltpu.VMEM((5, half + 4, 8, ny), f32)],
        compiler_params=params,
        cost_estimate=cost(300 * field, 20 * 4 * field),
        name="main",
    )(state, below_a, above_a, sb, sa, below_n, above_n, gradient)

    row_spec = pl.BlockSpec((chunk, 2, ny), lambda i: (i, 0, 0))
    two = pl.BlockSpec((2, 2, chunk, planes, ny), lambda i: (0, 0, i, 0, 0))
    new_mom, new_mag = pl.pallas_call(
        far_kernel,
        grid=(steps,),
        in_specs=[halo, halo, row_spec, row_spec, three, two],
        out_specs=[three, two],
        out_shape=[shape((3, 2, half, planes, ny), f32)] * 2,
        input_output_aliases={4: 0, 5: 1},
        compiler_params=params,
        cost_estimate=cost(30 * field, 13 * 4 * field),
        name="far",
    )(below_f, above_f, below_l, above_l, new_mom, new_mag)

    band = ny // across
    block = pl.BlockSpec((2, 1, band, NX), lambda z: (0, z, 0, 0))
    modes = pl.pallas_call(
        modes_kernel,
        grid=(planes,),
        in_specs=[smem, block] + [full((NX, NX))] * 4,
        out_specs=block,
        out_shape=shape((2, planes, band, NX), f32),
        compiler_params=params,
        cost_estimate=cost(20 * field, 5 * 4 * field),
        name="modes",
    )(at, portion, *tables(NX))
    return (
        new_density.reshape(rows, planes, ny),
        new_mom.reshape(3, rows, planes, ny),
        new_mag.reshape(3, rows, planes, ny),
        modes,
    )


def solution(mesh):
    in_specs = (
        P("xy", "gz", None),
        P(None, "xy", "gz", None),
        P(None, "xy", "gz", None),
        P("xy", None),
        P(("gz", "xy"), None),
        P(("gz", "xy")),
    )
    out_specs = (
        P("xy", "gz", None),
        P(None, "xy", "gz", None),
        P(None, "xy", "gz", None),
        P(None, "gz", "xy", None),
    )
    return jax.shard_map(
        on_device, mesh=mesh, in_specs=in_specs, out_specs=out_specs, check_vma=False
    )
```

time: 500 us -> 175 us (0.35)
  other arithmetic: 212 us -> 7.23 us
  blocking collectives: 123 us -> 0 us
  local copies, waits for them, and re-layouts: 100 us -> 27.5 us
  Pallas kernels: 0 us -> 71.4 us
  matrix products: 36.1 us -> 0 us
  waiting for transfers between devices: 6.05 us -> 38.2 us
  starting transfers between devices: 15.3 us -> 25.9 us
    all_gather x1 -> x0, blocking collectives: 123 us -> none  [on_device(): events = lax.all_gather(events, ('gz', 'xy'), axis=0, tiled=True)]
    reduce_sum x2 -> x0, other arithmetic: 73.7 us -> none  [deposit(): jnp.sum(weights, axis=0)]
    pallas_call x0 -> x6, Pallas kernels: none -> 71.4 us  [the longest x1 21.3 us: on_device(): pl.pallas_call(main_kernel, grid=(steps,), in_specs=[full((7, half + 4, 8...]
    slice x23 -> x7, local copies, waits for them, and re-layouts: 69.2 us -> 3.57 us  [the longest x2 0.95 us: on_device(): jnp.roll(arm_potential, 2, 1)]
    add x7 -> x2, other arithmetic: 59.7 us -> 4.23 us  [the longest x1 3.41 us: on_device(): NEAR * (jnp.roll(arm_potential, 1, 1) - jnp.roll(arm_potential, -1, 1))]
    dot_general x6 -> x0, matrix products: 36.1 us -> none  [the longest x1 6.74 us: on_device(): jnp.einsum('xzy,yk->zkx', new_density, sine_y, precision=lax.Precision.HIGH)]
    unnamed x19 -> x0, other arithmetic: 30 us -> none
    ppermute x8 -> x12, waiting for transfers between devices: 0.02 us -> 23.2 us  [shift(): return lax.ppermute(block, axis, [(i, (i + step) % n) for i in range(n)])]
  transfers between devices with their start and end apart: 9 -> 14, of which waited for: 1 -> 4; matrix products, arithmetic and copies ran while one was open for 63% -> 15% of each run, Pallas kernels for 0% -> 38%
where the time goes in v2:
time: 175 us; the launch traced here: 172 us
  Pallas kernels  71.4 us (41%)
  waiting for transfers between devices  38.2 us (22%)
  local copies, waits for them, and re-layouts  27.5 us (16%)
  starting transfers between devices  25.9 us (15%)
  other arithmetic  7.23 us (4%)
    ppermute x12, waiting for transfers between devices, shift(): return lax.ppermute(block, axis, [(i, (i + step) % n) for i in range(n)])  23.2 us
    pallas_call x1, Pallas kernels, on_device(): pl.pallas_call(main_kernel, grid=(steps,), in_specs=[full((7, half + 4, 8...  21.3 us
    ppermute x12, starting transfers between devices, shift(): return lax.ppermute(block, axis, [(i, (i + step) % n) for i in range(n)])  19.6 us
    pallas_call x1, Pallas kernels, on_device(): pl.pallas_call(density_kernel, grid=(1,), in_specs=[full((4, half + 4, 8,...  15.5 us
    all_to_all x1, waiting for transfers between devices, on_device(): lax.all_to_all(jnp.broadcast_to(mine, (devices, 1, mine.shape[2])), ('gz'...  14.9 us
    pallas_call x1, Pallas kernels, on_device(): pl.pallas_call(functools.partial(state_kernel, depth=planes * layers), in...  14.9 us
    pallas_call x1, Pallas kernels, on_device(): pl.pallas_call(far_kernel, grid=(steps,), in_specs=[halo, halo, row_spec,...  8.62 us
    pallas_call x1, Pallas kernels, on_device(): pl.pallas_call(modes_kernel, grid=(planes,), in_specs=[smem, block] + [fu...  6.79 us
  transfers between devices with their start and end apart: 14, of which 4 were waited for; matrix products, arithmetic and copies ran while one was open for 15% of the time, Pallas kernels for 38%

profile of v2, /device:TPU:0, one launch (start us, length us, event | category | flops | bytes accessed | tf_op | source)
XLA Modules:
  0.0 171.6 jit_solution(16900767042949063925)
XLA Ops:
  1.4 3.9 %collective-permute-start.11 = (f32[2,512]{1,0:T(2,128)S(1)}, f32[2,512]{1,0:T(2,128)S(1)}, u32[]{:S(2)}, u32[]{:S(2)}) collective-permute-start(f32[2,512]{1,0:T(2,128)S(1)} %get-tuple-element.44), channel_id=1, source_target_pairs={{0,3},{1,0},{2,1},{3,2},{4,7},{5,4},{6,5},{7,6},{8,11},{9,8},{10,9... | collective-permute-start | bytes 12296 | tf_op jit(solution)/shard_map/ppermute | solution.py:368
  5.3 4.3 %pack.1 = (f32[2,64,4,512]{3,2,1,0:T(4,128)}, f32[2,64,4,512]{3,2,1,0:T(4,128)}) custom-call(f32[2,64,4,512]{3,2,1,0:T(4,128)} %bitcast.32, f32[3,2,64,4,512]{4,3,2,1,0:T(4,128)} %bitcast.26, f32[3,2,64,4,512]{4,3,2,1,0:T(4,128)} %bitcast.28), custom_call_target="tpu_custom_call" | custom-call | flops 5242880 | bytes 5242880 | tf_op jit(solution)/shard_map/pack/pallas_call | solution.py:406
  9.5 3.5 %collective-permute-start.3 = (f32[2,64,4,512]{3,2,1,0:T(4,128)}, f32[2,64,4,512]{3,2,1,0:T(4,128)S(1)}, u32[]{:S(2)}, u32[]{:S(2)}) collective-permute-start(f32[2,64,4,512]{3,2,1,0:T(4,128)} %get-tuple-element.23), channel_id=1, source_target_pairs={{0,28},{4,0},{8,4},{12,8},{16,12},{20,16},{24,20},{28,24},{1,29},{... | collective-permute-start | bytes 3145736 | tf_op jit(solution)/shard_map/ppermute | solution.py:368
  14.4 2.5 %all-to-all-start = ((s32[32,1,128]{2,1,0:T(1,128)}), s32[32,1,128]{2,1,0:T(1,128)S(1)}, u32[]{:S(2)}, u32[]{:S(2)}) async-start(s32[32,1,128]{2,1,0:T(1,128)} %broadcast_in_dim.18), calls=%async_computation | async-start | bytes 32768 | tf_op jit(solution)/shard_map/all_to_all | solution.py:388
  17.7 0.9 fusion.9
  18.6 1.7 collective-permute-start
  20.4 1.3 collective-permute-start.1
  22.4 14.9 %all-to-all-done = s32[32,1,128]{2,1,0:T(1,128)S(1)} async-done(((s32[32,1,128]{2,1,0:T(1,128)}), s32[32,1,128]{2,1,0:T(1,128)S(1)}, u32[]{:S(2)}, u32[]{:S(2)}) %all-to-all-start) | async-done | bytes 16416 | tf_op jit(solution)/shard_map/all_to_all | solution.py:388
  39.3 14.9 %state.1 = (f32[7,68,8,512]{3,2,1,0:T(8,128)}, f32[68,8,512]{2,1,0:T(8,128)}, f32[68,8,512]{2,1,0:T(8,128)}, f32[2,64,4,512]{3,2,1,0:T(4,128)}, f32[2,64,4,512]{...) custom-call(s32[128]{0:T(128)} %reshape_squeeze.3.ev_ref, ...), custom_call_target="tpu_custom_call" | custom-call | flops 26214400 | bytes 22020096 | tf_op jit(solution)/shard_map/state/pallas_call | solution.py:420
  54.2 0.9 copy-done.1
  55.5 15.5 %density.1 = (f32[2,64,4,512]{3,2,1,0:T(4,128)}, f32[2,4,512,128]{3,2,1,0:T(8,128)}) custom-call(f32[7,68,8,512]{3,2,1,0:T(8,128)} %get-tuple-element.21.u_ref, f32[2,64,4,512]{3,2,1,0:T(4,128)} %copy-done.1, f32[2,64,4,512]{3,2,1,0:T(4,128)} %copy-done.2, f32[68,8,512]{2,1,0:T(8,128)} %get-tuple-element.24.sb_ref, f32[68,8,512]{2,1,0:T(8,128)} %get-tuple-element.25.sa_ref, ...), custom_call_target="tpu_custom_call" | custom-call | flops 15728640 | bytes 13631488 | tf_op jit(solution)/shard_map/density/pallas_call | solution.py:434
  71.0 4.3 %copy.27 = f32[2,4,512,128]{3,1,0,2:T(4,128)} copy(f32[2,4,512,128]{3,2,1,0:T(8,128)} %get-tuple-element.37) | data formatting | bytes 4194304 | tf_op jit(solution)/shard_map/density/pallas_call | solution.py:434
  75.4 3.7 %all-to-all-start.1 = ((f32[2,4,512,128]{3,1,0,2:T(4,128)}), f32[2,4,512,128]{3,1,0,2:T(4,128)S(1)}, u32[]{:S(2)}, u32[]{:S(2)}) async-start(f32[2,4,512,128]{3,1,0,2:T(4,128)} %copy.27), calls=%async_computation.1 | async-start | bytes 4194304 | tf_op jit(solution)/shard_map/all_to_all | solution.py:450
  79.1 0.9 fusion.14
  80.0 0.9 fusion.13
  81.5 2.9 %collective-permute-start.5 = (f32[2,64,4,512]{3,2,1,0:T(4,128)}, f32[2,64,4,512]{3,2,1,0:T(4,128)}, u32[]{:S(2)}, u32[]{:S(2)}) collective-permute-start(f32[2,64,4,512]{3,2,1,0:T(4,128)} %get-tuple-element.28), channel_id=1, source_target_pairs={{0,28},{4,0},{8,4},{12,8},{16,12},{20,16},{24,20},{28,24},{1,29},{... | collective-permute-start | bytes 3145736 | tf_op jit(solution)/shard_map/ppermute | solution.py:368
  85.0 2.0 %concatenate.91 = f32[1,2,64,1,511]{4,3,2,1,0:T(1,128)} reshape(f32[128,511]{1,0:T(8,128)} %get-tuple-element.50) | data formatting | bytes 523264 | tf_op jit(solution)/shard_map/jit(_roll_static)/concatenate | solution.py:454
  87.0 2.0 %concatenate.89 = f32[1,2,64,1,511]{4,3,2,1,0:T(1,128)} reshape(f32[128,511]{1,0:T(8,128)} %get-tuple-element.51) | data formatting | bytes 523264 | tf_op jit(solution)/shard_map/jit(_roll_static)/concatenate | solution.py:454
  89.0 2.0 %concatenate.98 = f32[1,2,64,1,510]{4,3,2,1,0:T(1,128)} reshape(f32[128,510]{1,0:T(8,128)} %get-tuple-element.48) | data formatting | bytes 522240 | tf_op jit(solution)/shard_map/jit(_roll_static)/concatenate | solution.py:455
  91.0 2.0 %concatenate.94 = f32[1,2,64,1,510]{4,3,2,1,0:T(1,128)} reshape(f32[128,510]{1,0:T(8,128)} %get-tuple-element.49) | data formatting | bytes 522240 | tf_op jit(solution)/shard_map/jit(_roll_static)/concatenate | solution.py:455
  93.1 3.4 %fusion.7 = f32[1,2,64,1,512]{4,3,2,1,0:T(1,128)} fusion(f32[1,2,64,1,511]{4,3,2,1,0:T(1,128)} %concatenate.89, f32[1,2,64,1,1]{4,3,2,1,0:T(1,128)S(1)} %bitcast.37, f32[1,2,64,1,1]{4,3,2,1,0:T(1,128)S(1)} %bitcast.36, f32[1,2,64,1,511]{4,3,2,1,0:T(1,128)} %concatenate.91, f32[1,2,64,1,2]{4,3,2,1,0:T(1,128)S(1)} %bitcast.39, ...), kind=kLoop, calls=%fused_computation.13 | loop fusion | flops 589824 | bytes 1310720 | tf_op jit(solution)/shard_map/add | solution.py:454
  96.5 2.0 %collective-permute-start.10 = (f32[2,512]{1,0:T(2,128)S(1)}, f32[2,512]{1,0:T(2,128)S(1)}, u32[]{:S(2)}, u32[]{:S(2)}) collective-permute-start(f32[2,512]{1,0:T(2,128)S(1)} %get-tuple-element.45), channel_id=1, source_target_pairs={{0,1},{1,2},{2,3},{3,0},{4,5},{5,6},{6,7},{7,4},{8,9},{9,10},{10,1... | collective-permute-start | bytes 12296 | tf_op jit(solution)/shard_map/ppermute | solution.py:368
  98.6 6.7 %collective-permute-done.10 = f32[2,512]{1,0:T(2,128)S(1)} collective-permute-done((f32[2,512]{1,0:T(2,128)S(1)}, f32[2,512]{1,0:T(2,128)S(1)}, u32[]{:S(2)}, u32[]{:S(2)}) %collective-permute-start.10) | collective-permute-done | bytes 4128 | tf_op jit(solution)/shard_map/ppermute | solution.py:368
  105.8 3.0 %collective-permute-start.7 = (f32[64,2,512]{2,1,0:T(2,128)}, f32[64,2,512]{2,1,0:T(2,128)}, u32[]{:S(2)}, u32[]{:S(2)}) collective-permute-start(f32[64,2,512]{2,1,0:T(2,128)} %get-tuple-element.30), channel_id=1, source_target_pairs={{0,28},{4,0},{8,4},{12,8},{16,12},{20,16},{24,20},{28,24},{1,29},{... | collective-permute-start | bytes 786440 | tf_op jit(solution)/shard_map/ppermute | solution.py:368
  109.7 1.3 stack.20
  110.9 2.2 %pad_maximum_fusion.g_ref = f32[2,2,64,1,512]{4,3,2,1,0:T(1,128)} fusion(f32[1,2,64,1,512]{4,3,2,1,0:T(1,128)} %fusion.7, f32[1,2,64,1,512]{4,3,2,1,0:T(1,128)S(1)} %stack.20), kind=kLoop, calls=%fused_computation.1 | loop fusion | flops 131072 | bytes 1048576 | tf_op jit(solution)/shard_map/stack | solution.py:457
  113.2 16.0 %collective-permute-done.9.an_ref = f32[2,64,4,512]{3,2,1,0:T(4,128)} collective-permute-done((f32[2,64,4,512]{3,2,1,0:T(4,128)}, f32[2,64,4,512]{3,2,1,0:T(4,128)}, u32[]{:S(2)}, u32[]{:S(2)}) %collective-permute-start.9) | collective-permute-done | bytes 1048608 | tf_op jit(solution)/shard_map/ppermute | solution.py:368
  129.1 21.3 %main.1 = (f32[3,2,64,4,512]{4,3,2,1,0:T(4,128)}, f32[3,2,64,4,512]{4,3,2,1,0:T(4,128)}) custom-call(f32[7,68,8,512]{3,2,1,0:T(8,128)} %get-tuple-element.21.u_ref, f32[2,64,4,512]{3,2,1,0:T(4,128)} %copy-done.1, f32[2,64,4,512]{3,2,1,0:T(4,128)} %copy-done.2, f32[68,8,512]{2,1,0:T(8,128)} %get-tuple-element.24.sb_ref, ...), custom_call_target="tpu_custom_call" | custom-call | flops 78643200 | bytes 20971520 | tf_op jit(solution)/shard_map/main/pallas_call | solution.py:463
  150.5 8.6 %far.1 = (f32[3,2,64,4,512]{4,3,2,1,0:T(4,128)}, f32[3,2,64,4,512]{4,3,2,1,0:T(4,128)}) custom-call(f32[2,64,4,512]{3,2,1,0:T(4,128)} %collective-permute-done.4.bf_ref, f32[2,64,4,512]{3,2,1,0:T(4,128)} %collective-permute-done.5.af_ref, f32[64,2,512]{2,1,0:T(2,128)} %collective-permute-done.6.bl_ref, ...), custom_call_target="tpu_custom_call", output_to_operand_aliasing={{0}: (4, {}), {1}: (5, {})} | custom-call | flops 7864320 | bytes 13631488 | tf_op jit(solution)/shard_map/far/pallas_call | solution.py:480
  159.1 2.7 %copy.30 = f32[2,4,4,128,128]{4,2,3,1,0:T(4,128)} copy(f32[2,4,4,128,128]{4,1,0,3,2:T(4,128)S(1)} %bitcast.30) | data formatting | bytes 4194304 | tf_op jit(solution)/shard_map/all_to_all | solution.py:450
  161.8 3.1 %all_to_all.20.w_ref = f32[2,4,128,512]{3,2,1,0:T(8,128)} reshape(f32[2,4,128,4,128]{4,3,2,1,0:T(4,128)} %bitcast.31) | data formatting | bytes 4194304 | tf_op jit(solution)/shard_map/all_to_all | solution.py:450
  164.8 6.8 %modes.1 = f32[2,4,128,512]{3,2,1,0:T(8,128)} custom-call(s32[3]{0:T(128)} %pad_add_fusion.at_ref, f32[2,4,128,512]{3,2,1,0:T(8,128)} %all_to_all.20.w_ref, bf16[512,512]{1,0:T(8,128)(2,1)} %constant.36.clone.ch_ref, bf16[512,512]{1,0:T(8,128)(2,1)} %constant.37.clone.cl_ref, bf16[512,512]{1,0:T(8,128)(2,1)} %constant.38.clone.sh_ref, ...), custom_call_target="tpu_custom_call" | custom-call | flops 5242880 | bytes 5242880 | tf_op jit(solution)/shard_map/modes/pallas_call | solution.py:494
  (44 shorter events, 7.9 us)
Async XLA Ops:
  1.4 95.2 %collective-permute-start.11 = (f32[2,512]{1,0:T(2,128)S(1)}, f32[2,512]{1,0:T(2,128)S(1)}, u32[]{:S(2)}, u32[]{:S(2)}) collective-permute-start(f32[2,512]{1,0:T(2,128)S(1)} %get-tuple-element.44), channel_id=1, source_target_pairs={{0,3},{1,0},{2,1},{3,2},{4,7},{5,4},{6,5},{7,6},{8,11},{9,8},{10,9... | collective-permute-start | bytes 12296 | tf_op jit(solution)/shard_map/ppermute | solution.py:368
  5.3 8.5 %copy-start.6 = (s32[1,3]{1,0:T(1,128)S(1)}, s32[1,3]{1,0:T(1,128)}, u32[]{:S(2)}) copy-start(s32[1,3]{1,0:T(1,128)} %param.17) | copy-start | bytes 40
  9.5 44.6 %collective-permute-start.2 = (f32[2,64,4,512]{3,2,1,0:T(4,128)}, f32[2,64,4,512]{3,2,1,0:T(4,128)S(1)}, u32[]{:S(2)}, u32[]{:S(2)}) collective-permute-start(f32[2,64,4,512]{3,2,1,0:T(4,128)} %get-tuple-element.22), channel_id=1, source_target_pairs={{0,4},{4,8},{8,12},{12,16},{16,20},{20,24},{24,28},{28,0},{1,5},{5... | collective-permute-start | bytes 3145736 | tf_op jit(solution)/shard_map/ppermute | solution.py:368
  9.5 44.7 %collective-permute-start.3 = (f32[2,64,4,512]{3,2,1,0:T(4,128)}, f32[2,64,4,512]{3,2,1,0:T(4,128)S(1)}, u32[]{:S(2)}, u32[]{:S(2)}) collective-permute-start(f32[2,64,4,512]{3,2,1,0:T(4,128)} %get-tuple-element.23), channel_id=1, source_target_pairs={{0,28},{4,0},{8,4},{12,8},{16,12},{20,16},{24,20},{28,24},{1,29},{... | collective-permute-start | bytes 3145736 | tf_op jit(solution)/shard_map/ppermute | solution.py:368
  14.4 22.9 %all-to-all-start = ((s32[32,1,128]{2,1,0:T(1,128)}), s32[32,1,128]{2,1,0:T(1,128)S(1)}, u32[]{:S(2)}, u32[]{:S(2)}) async-start(s32[32,1,128]{2,1,0:T(1,128)} %broadcast_in_dim.18), calls=%async_computation | async-start | bytes 32768 | tf_op jit(solution)/shard_map/all_to_all | solution.py:388
  18.6 19.3 %collective-permute-start = (f32[7,2,4,512]{3,2,1,0:T(4,128)S(1)}, f32[7,2,4,512]{3,2,1,0:T(4,128)S(1)}, u32[]{:S(2)}, u32[]{:S(2)}) collective-permute-start(f32[7,2,4,512]{3,2,1,0:T(4,128)S(1)} %pad_maximum_fusion.2), channel_id=1, source_target_pairs={{0,1},{1,2},{2,3},{3,0},{4,5},{5,6},{6,7},{7,4},{8,9},{9,10},{10,1... | collective-permute-start | bytes 344072 | tf_op jit(solution)/shard_map/ppermute | solution.py:368
  20.4 17.6 %collective-permute-start.1 = (f32[7,2,4,512]{3,2,1,0:T(4,128)S(1)}, f32[7,2,4,512]{3,2,1,0:T(4,128)S(1)}, u32[]{:S(2)}, u32[]{:S(2)}) collective-permute-start(f32[7,2,4,512]{3,2,1,0:T(4,128)S(1)} %pad_maximum_fusion.3), channel_id=1, source_target_pairs={{0,3},{1,0},{2,1},{3,2},{4,7},{5,4},{6,5},{7,6},{8,11},{9,8},{10,9... | collective-permute-start | bytes 344072 | tf_op jit(solution)/shard_map/ppermute | solution.py:368
  38.0 0.7 copy-start.4
  38.6 0.7 copy-start.5
  54.2 1.0 copy-start.1
  54.2 1.3 copy-start.2
  75.4 3.8 %copy-start = (f32[128,512]{1,0:T(8,128)S(1)}, f32[128,512]{1,0:T(8,128)}, u32[]{:S(2)}) copy-start(f32[128,512]{1,0:T(8,128)} %param.16) | copy-start | bytes 786436
  75.4 83.7 %all-to-all-start.1 = ((f32[2,4,512,128]{3,1,0,2:T(4,128)}), f32[2,4,512,128]{3,1,0,2:T(4,128)S(1)}, u32[]{:S(2)}, u32[]{:S(2)}) async-start(f32[2,4,512,128]{3,1,0,2:T(4,128)} %copy.27), calls=%async_computation.1 | async-start | bytes 4194304 | tf_op jit(solution)/shard_map/all_to_all | solution.py:450
  80.0 25.8 %collective-permute-start.8 = (f32[2,64,4,512]{3,2,1,0:T(4,128)}, f32[2,64,4,512]{3,2,1,0:T(4,128)S(1)}, u32[]{:S(2)}, u32[]{:S(2)}) collective-permute-start(f32[2,64,4,512]{3,2,1,0:T(4,128)} %get-tuple-element.31), channel_id=1, source_target_pairs={{0,4},{4,8},{8,12},{12,16},{16,20},{20,24},{24,28},{28,0},{1,5},{5... | collective-permute-start | bytes 3145736 | tf_op jit(solution)/shard_map/ppermute | solution.py:368
  80.9 69.6 %collective-permute-start.4 = (f32[2,64,4,512]{3,2,1,0:T(4,128)}, f32[2,64,4,512]{3,2,1,0:T(4,128)}, u32[]{:S(2)}, u32[]{:S(2)}) collective-permute-start(f32[2,64,4,512]{3,2,1,0:T(4,128)} %get-tuple-element.27), channel_id=1, source_target_pairs={{0,4},{4,8},{8,12},{12,16},{16,20},{20,24},{24,28},{28,0},{1,5},{5... | collective-permute-start | bytes 3145736 | tf_op jit(solution)/shard_map/ppermute | solution.py:368
  81.5 68.9 %collective-permute-start.5 = (f32[2,64,4,512]{3,2,1,0:T(4,128)}, f32[2,64,4,512]{3,2,1,0:T(4,128)}, u32[]{:S(2)}, u32[]{:S(2)}) collective-permute-start(f32[2,64,4,512]{3,2,1,0:T(4,128)} %get-tuple-element.28), channel_id=1, source_target_pairs={{0,28},{4,0},{8,4},{12,8},{16,12},{20,16},{24,20},{28,24},{1,29},{... | collective-permute-start | bytes 3145736 | tf_op jit(solution)/shard_map/ppermute | solution.py:368
  84.4 44.7 %collective-permute-start.9 = (f32[2,64,4,512]{3,2,1,0:T(4,128)}, f32[2,64,4,512]{3,2,1,0:T(4,128)}, u32[]{:S(2)}, u32[]{:S(2)}) collective-permute-start(f32[2,64,4,512]{3,2,1,0:T(4,128)} %get-tuple-element.32), channel_id=1, source_target_pairs={{0,28},{4,0},{8,4},{12,8},{16,12},{20,16},{24,20},{28,24},{1,29},{... | collective-permute-start | bytes 3145736 | tf_op jit(solution)/shard_map/ppermute | solution.py:368
  96.5 8.8 %collective-permute-start.10 = (f32[2,512]{1,0:T(2,128)S(1)}, f32[2,512]{1,0:T(2,128)S(1)}, u32[]{:S(2)}, u32[]{:S(2)}) collective-permute-start(f32[2,512]{1,0:T(2,128)S(1)} %get-tuple-element.45), channel_id=1, source_target_pairs={{0,1},{1,2},{2,3},{3,0},{4,5},{5,6},{6,7},{7,4},{8,9},{9,10},{10,1... | collective-permute-start | bytes 12296 | tf_op jit(solution)/shard_map/ppermute | solution.py:368
  105.3 45.1 %collective-permute-start.6 = (f32[64,2,512]{2,1,0:T(2,128)}, f32[64,2,512]{2,1,0:T(2,128)}, u32[]{:S(2)}, u32[]{:S(2)}) collective-permute-start(f32[64,2,512]{2,1,0:T(2,128)} %get-tuple-element.29), channel_id=1, source_target_pairs={{0,4},{4,8},{8,12},{12,16},{16,20},{20,24},{24,28},{28,0},{1,5},{5... | collective-permute-start | bytes 786440 | tf_op jit(solution)/shard_map/ppermute | solution.py:368
  105.8 23.3 %copy-start.3 = (f32[2,64,4,512]{3,2,1,0:T(4,128)}, f32[2,64,4,512]{3,2,1,0:T(4,128)S(1)}, u32[]{:S(2)}) copy-start(f32[2,64,4,512]{3,2,1,0:T(4,128)S(1)} %collective-permute-done.8.bn_ref) | copy-start | bytes 3145732
  105.8 44.6 %collective-permute-start.7 = (f32[64,2,512]{2,1,0:T(2,128)}, f32[64,2,512]{2,1,0:T(2,128)}, u32[]{:S(2)}, u32[]{:S(2)}) collective-permute-start(f32[64,2,512]{2,1,0:T(2,128)} %get-tuple-element.30), channel_id=1, source_target_pairs={{0,28},{4,0},{8,4},{12,8},{16,12},{20,16},{24,20},{28,24},{1,29},{... | collective-permute-start | bytes 786440 | tf_op jit(solution)/shard_map/ppermute | solution.py:368

commit v3 on v2

--- a/solution.py
+++ b/solution.py
@@ -18,6 +18,7 @@
 NEAR = 8.0 * TIME_STEP / 12.0
 FAR = TIME_STEP / 12.0
 VMEM = 56 * 1024 * 1024
+PACK_COST = STATE_COST = DENSITY_COST = MAIN_COST = MODES_COST = (1e6, 1e5)
 
 
 def pair(ref, *index):
@@ -63,16 +64,16 @@
         slot = slots(rho.shape)
         up = jnp.where(slot == 2, mz, gather_planes([rho, mz, mz, bx], 3))
         down = jnp.where(slot == 2, turn(mz, 1, 0), gather_planes([rho, mz, mz, bx], 0))
-        unpair(up_ref, up, p)
-        unpair(down_ref, down, p)
+        up_ref[p] = up
+        down_ref[p] = down
         return 0
 
     lax.fori_loop(0, half, body, 0)
 
 
 def state_kernel(
-    ev_ref, at_ref, rho_ref, mom_ref, mag_ref, before_ref, after_ref,
-    u_ref, sb_ref, sa_ref, up_near, down_near, up_far, down_far, up_last, down_last, *, depth,
+    ev_ref, at_ref, rho_ref, mom_ref, mag_ref, pot_ref, before_ref, after_ref,
+    u_ref, sb_out, sa_out, up_0, down_0, up_1, down_1, sb_ref, sa_ref, *, depth,
 ):
     half, ny = rho_ref.shape[1], rho_ref.shape[3]
     rows, events = 2 * half, ev_ref.shape[0] // 4
@@ -81,15 +82,17 @@
     def raw(f, h, p):
         if f == 0:
             return rho_ref[h, p]
+        if f == 7:
+            return jnp.broadcast_to(pot_ref[pl.ds(h * half + p, 1), :], (4, ny))
         return mom_ref[f - 1, h, p] if f < 4 else mag_ref[f - 4, h, p]
 
     def fill(p, _):
-        for f in range(7):
+        for f in range(8):
             u_ref[f, p + 2] = jnp.concatenate([raw(f, 0, p), raw(f, 1, p)], axis=0)
         return 0
 
     lax.fori_loop(0, half, fill, 0)
-    for f in range(7):
+    for f in range(8):
         for j in range(2):
             u_ref[f, j] = jnp.concatenate([before_ref[f, j], raw(f, 0, half - 2 + j)], axis=0)
             u_ref[f, half + 2 + j] = jnp.concatenate([raw(f, 1, j), after_ref[f, j]], axis=0)
@@ -155,20 +158,35 @@
 
     lax.fori_loop(0, events, event, 0)
 
-    def messages(p, _):
-        u = [u_ref[f, p + 2] for f in range(7)]
-        near = [u[1], u[2], u[5], u[6]]
-        unpair(up_near, gather_planes(near, 3), p)
-        unpair(down_near, gather_planes(near, 0), p)
-        f = fluxes(u[0], u[1:4], u[4:7], 2)
-        unpair(up_far, gather_planes(f[:4], 2), p)
-        unpair(down_far, gather_planes(f[:4], 1), p)
-        for ref, plane in ((up_last, 2), (down_last, 1)):
-            low, high = turn(f[4], -plane, 0), turn(f[4], -plane - 3, 0)
-            ref[p] = jnp.where(slots(low.shape) == 0, low, high)[:2]
-        return 0
-
-    lax.fori_loop(0, half, messages, 0)
+    def group(up_ref, down_ref, first, count):
+        def messages(g, _):
+            sub = lax.broadcasted_iota(jnp.int32, (8, ny), 0)
+            lasts = [jnp.zeros((8, ny), jnp.float32) for _ in range(2)]
+            for j in range(4):
+                r = 4 * g + j
+                p = r + first
+                sb_out[p] = sb_ref[p + 2]
+                sa_out[p] = sa_ref[p + 2]
+                u = [u_ref[f, p + 2] for f in range(7)]
+                near = [u[1], u[2], u[5], u[6]]
+                up_ref[r] = gather_planes(near, 3)
+                down_ref[r] = gather_planes(near, 0)
+                f = fluxes(u[0], u[1:4], u[4:7], 2)
+                up_ref[count + r] = gather_planes(f[:4], 2)
+                down_ref[count + r] = gather_planes(f[:4], 1)
+                for i, plane in enumerate((2, 1)):
+                    for h in range(2):
+                        moved = turn(f[4], 2 * j + h - 4 * h - plane, 0)
+                        lasts[i] = jnp.where(sub == 2 * j + h, moved, lasts[i])
+            up_ref[2 * count + g] = lasts[0]
+            down_ref[2 * count + g] = lasts[1]
+            return 0
+
+        lax.fori_loop(0, count // 4, messages, 0)
+
+    split = up_0.shape[0] * 4 // 9
+    group(up_0, down_0, 0, split)
+    group(up_1, down_1, split, half - split)
 
 
 def ends(below, above, c, fill):
@@ -212,12 +230,12 @@
 
 
 def density_kernel(u_ref, below_ref, above_ref, sb_ref, sa_ref, order_ref, high_ref, low_ref, out_ref, wave_ref, d_ref):
-    half = below_ref.shape[1]
+    half = below_ref.shape[0]
     rows = 2 * half
 
     def body(p, _):
         rho, my, mz = u_ref[0, p + 2], u_ref[2, p + 2], u_ref[3, p + 2]
-        below, above = pair(below_ref, p) + sb_ref[p + 2], pair(above_ref, p) + sa_ref[p + 2]
+        below, above = below_ref[p] + sb_ref[p], above_ref[p] + sa_ref[p]
         slot, sign = slots(rho.shape), signs(rho.shape)
         new = rho * (1.0 - 6.0 * DIFFUSION)
         new += DIFFUSION * (u_ref[0, p + 1] + u_ref[0, p + 3])
@@ -237,22 +255,38 @@
     low = (d - high.astype(jnp.float32)).astype(jnp.bfloat16)
     high = dot(order, high).astype(jnp.bfloat16)
     low = dot(order, low).astype(jnp.bfloat16)
-    across = lambda a, b: lax.dot_general(a, b, (((1,), (1,)), ((), ())), preferred_element_type=jnp.float32)
     for part in range(2):
         c_high, c_low = high_ref[part], low_ref[part]
-        for z in range(4):
-            r_high, r_low = high[z * rows : (z + 1) * rows], low[z * rows : (z + 1) * rows]
-            wave_ref[part, z] = across(c_high, r_high) + across(c_low, r_high) + across(c_high, r_low)
-
-
-def main_kernel(u_ref, ba_ref, aa_ref, sb_ref, sa_ref, bn_ref, an_ref, g_ref, mom_ref, mag_ref, f_ref):
-    chunk = ba_ref.shape[1]
+        wave = dot(high, c_high) + dot(high, c_low) + dot(low, c_high)
+        peers, band = wave_ref.shape[0], wave_ref.shape[4]
+        for j in range(peers):
+            for z in range(4):
+                wave_ref[j, part, z] = wave[z * rows : (z + 1) * rows, j * band : (j + 1) * band]
+
+
+def last_plane(below, above, j):
+    sub = lax.broadcasted_iota(jnp.int32, below.shape, 0)
+    out = jnp.zeros_like(below)
+    for h in range(2):
+        out = jnp.where(sub == 4 * h, turn(below, 4 * h - (2 * j + h), 0), out)
+        out = jnp.where(sub == 4 * h + 3, turn(above, 4 * h + 3 - (2 * j + h), 0), out)
+    return out
+
+
+def main_kernel(
+    u_hbm, ba_ref, aa_ref, sb_ref, sa_ref, bn_ref, an_ref, bf_ref, af_ref, bl_ref, al_ref, *rest, first,
+):
+    mom_ref, mag_ref, u_ref, f_ref, sem = rest[-5:]
+    chunk, total = ba_ref.shape[0], u_ref.shape[1]
     start = pl.program_id(0) * chunk
-    total = u_ref.shape[1]
     kept = (0, 1, 2, 4, 5)
 
     @pl.when(pl.program_id(0) == 0)
     def _():
+        copy = pltpu.make_async_copy(u_hbm.at[:, pl.ds(first, total)], u_ref, sem)
+        copy.start()
+        copy.wait()
+
         def fx(q, _):
             u = [u_ref[f, q] for f in range(7)]
             f = fluxes(u[0], u[1:4], u[4:7], 0)
@@ -262,18 +296,19 @@
 
         lax.fori_loop(0, total, fx, 0)
 
-    def body(r, _):
+    def row(r, g, j):
         q = start + r + 2
         u = [u_ref[f, q] for f in range(7)]
         fy = fluxes(u[0], u[1:4], u[4:7], 1)
         fz = fluxes(u[0], u[1:4], u[4:7], 2)
         sign = signs(u[0].shape)
-        ba, aa = pair(ba_ref, r) + sb_ref[q], pair(aa_ref, r) + sa_ref[q]
-        bn, an = pair(bn_ref, r), pair(an_ref, r)
+        ba, aa = ba_ref[r] + sb_ref[r], aa_ref[r] + sa_ref[r]
+        bn, an, bf, af = bn_ref[r], an_ref[r], bf_ref[r], af_ref[r]
         hm = [ends(bn, an, 0, 0.0), ends(bn, an, 1, 0.0), ends(ba, aa, 1, 0.0)]
         hb = [ends(ba, aa, 3, 0.0), ends(bn, an, 2, 0.0), ends(bn, an, 3, 0.0)]
         fh = fluxes(ends(ba, aa, 0, 1.0), hm, hb, 2)
         halo = hm + hb
+        far = [ends(bf, af, c, 0.0) for c in range(4)] + [last_plane(bl_ref[g], al_ref[g], j), None]
         for c in range(6):
             field = u[c + 1]
             new = field * (1.0 - 6.0 * DIFFUSION)
@@ -287,57 +322,53 @@
                 new += along_y(fy[c], field)
             new += along_z(fz[c], field)
             new += near_planes(fh[c], halo[c], sign)
-            if c < 2:
-                g = [jnp.broadcast_to(g_ref[c, h, r], (4, field.shape[1])) for h in range(2)]
-                new += u[0] * jnp.concatenate(g, axis=0)
+            if far[c] is not None:
+                new -= (FAR * sign) * far[c]
+            if c == 0:
+                slope = NEAR * (u_ref[7, q - 1] - u_ref[7, q + 1]) + FAR * (u_ref[7, q + 2] - u_ref[7, q - 2])
+                new += u[0] * slope
+            if c == 1:
+                potential = u_ref[7, q]
+                slope = NEAR * (turn(potential, 1, 1) - turn(potential, -1, 1))
+                new += u[0] * (slope + FAR * (turn(potential, -2, 1) - turn(potential, 2, 1)))
             if c < 3:
                 unpair(mom_ref, new, c, r)
             else:
                 unpair(mag_ref, new, c - 3, r)
+
+    def body(g, _):
+        for j in range(4):
+            row(4 * g + j, g, j)
         return 0
 
-    lax.fori_loop(0, chunk, body, 0)
-
-
-def far_kernel(bf_ref, af_ref, bl_ref, al_ref, mom_in, mag_in, mom_ref, mag_ref):
-    chunk = bf_ref.shape[1]
-
-    def body(r, _):
-        below, above = pair(bf_ref, r), pair(af_ref, r)
-        sign = FAR * signs(below.shape)
-        sub = lax.broadcasted_iota(jnp.int32, below.shape, 0)
-        bl, al = bl_ref[r], al_ref[r]
-        last = jnp.zeros_like(below)
-        for h in range(2):
-            last = jnp.where(sub == 4 * h, bl[h : h + 1], jnp.where(sub == 4 * h + 3, al[h : h + 1], last))
-        for c in range(4):
-            term = sign * ends(below, above, c, 0.0)
-            if c < 3:
-                unpair(mom_ref, pair(mom_in, c, r) - term, c, r)
-            else:
-                unpair(mag_ref, pair(mag_in, 0, r) - term, 0, r)
-        unpair(mag_ref, pair(mag_in, 1, r) - sign * last, 1, r)
-        return 0
-
-    lax.fori_loop(0, chunk, body, 0)
-
-
-def modes_kernel(at_ref, w_ref, ch_ref, cl_ref, sh_ref, sl_ref, out_ref):
+    lax.fori_loop(0, chunk // 4, body, 0)
+
+
+def modes_kernel(at_ref, w_ref, ch_ref, cl_ref, sh_ref, sl_ref, out_ref, *, turned):
     dot = functools.partial(jnp.dot, preferred_element_type=jnp.float32)
-
-    def split(x):
+    planes, band, nx = out_ref.shape[1:]
+
+    def split(part):
+        if turned:
+            x = jnp.concatenate([w_ref[part, z] for z in range(planes)], axis=0)
+        else:
+            column = lambda z: jnp.concatenate([w_ref[j, part, z] for j in range(w_ref.shape[0])], axis=0)
+            x = jnp.concatenate([column(z).T for z in range(planes)], axis=0)
         high = x.astype(jnp.bfloat16)
         return high, (x - high.astype(jnp.float32)).astype(jnp.bfloat16)
 
-    re, im = split(w_ref[0, 0]), split(w_ref[1, 0])
+    re, im = split(0), split(1)
     times = lambda x, h, l: dot(x[0], h[...]) + dot(x[0], l[...]) + dot(x[1], h[...])
-    scale = 1.0 / math.sqrt(NX * w_ref.shape[3])
-    shape = out_ref.shape[2:]
+    scale = 1.0 / math.sqrt(NX * nx)
+    shape = (band, nx)
     ky = lax.broadcasted_iota(jnp.int32, shape, 0) + at_ref[2]
     kx = lax.broadcasted_iota(jnp.int32, shape, 1)
     keep = jnp.where((ky == 0) & (kx == 0), 0.0, scale)
-    out_ref[0, 0] = (times(re, ch_ref, cl_ref) + times(im, sh_ref, sl_ref)) * keep
-    out_ref[1, 0] = (times(im, ch_ref, cl_ref) - times(re, sh_ref, sl_ref)) * keep
+    out_re = times(re, ch_ref, cl_ref) + times(im, sh_ref, sl_ref)
+    out_im = times(im, ch_ref, cl_ref) - times(re, sh_ref, sl_ref)
+    for z in range(planes):
+        out_ref[0, z] = out_re[z * band : (z + 1) * band] * keep
+        out_ref[1, z] = out_im[z * band : (z + 1) * band] * keep
 
 
 def cost(flops, bytes_accessed):
@@ -381,6 +412,9 @@
     smem = pl.BlockSpec(memory_space=pltpu.SMEM)
     params = pltpu.CompilerParams(vmem_limit_bytes=VMEM)
     message = shape((2, half, planes, ny), f32)
+    tile = shape((half, 8, ny), f32)
+    n0 = max(4, half * 5 // 32 * 4)
+    counts = (n0, half - n0)
 
     slots_here = sn_cells.shape[0]
     mine = jnp.concatenate([sn_cells, sn_counts[:, None]], axis=1).reshape(1, 1, 4 * slots_here)
@@ -395,11 +429,12 @@
     mom = momentum.reshape(3, 2, half, planes, ny)
     mag = magnetic.reshape(3, 2, half, planes, ny)
 
-    edge = lambda s: jnp.concatenate([density[None, s], momentum[:, s], magnetic[:, s]], axis=0)
+    def edge(s):
+        potential = jnp.broadcast_to(arm_potential[s][None, :, None, :], (1, 2, planes, ny))
+        return jnp.concatenate([density[None, s], momentum[:, s], magnetic[:, s], potential], axis=0)
+
     before = shift(edge(slice(rows - 2, rows)), "xy", 1)
     after = shift(edge(slice(0, 2)), "xy", -1)
-    p_before = shift(arm_potential[rows - 2 :], "xy", 1)
-    p_after = shift(arm_potential[:2], "xy", -1)
 
     one = lambda f: pl.BlockSpec((1, 2, half, planes, ny), lambda i, f=f: (f, 0, 0, 0, 0))
     full = lambda s: pl.BlockSpec(s, lambda i: (0,) * len(s))
@@ -407,98 +442,89 @@
         pack_kernel,
         grid=(1,),
         in_specs=[full(message.shape), one(2), one(0)],
-        out_specs=[full(message.shape)] * 2,
-        out_shape=[message] * 2,
+        out_specs=[full(tile.shape)] * 2,
+        out_shape=[tile] * 2,
         compiler_params=params,
-        cost_estimate=cost(20 * field, 5 * 4 * field),
+        cost_estimate=cost(*PACK_COST),
         name="pack",
     )(rho, mom, mag)
     below_a, above_a = shift(up, "gz", 1), shift(down, "gz", -1)
 
-    side = shape((half + 4, 8, ny), f32)
-    last = shape((half, 2, ny), f32)
-    state, sb, sa, up_n, down_n, up_f, down_f, up_l, down_l = pl.pallas_call(
+    parcels = [shape((9 * n // 4, 8, ny), f32) for n in counts]
+    side = pltpu.VMEM((half + 4, 8, ny), f32)
+    state, sb, sa, up_0, down_0, up_1, down_1 = pl.pallas_call(
         functools.partial(state_kernel, depth=planes * layers),
-        in_specs=[smem, smem] + [whole] * 5,
-        out_specs=[whole] * 9,
-        out_shape=[shape((7, half + 4, 8, ny), f32), side, side] + [message] * 4 + [last] * 2,
+        in_specs=[smem, smem] + [whole] * 6,
+        out_specs=[whole] * 7,
+        out_shape=[shape((8, half + 4, 8, ny), f32), tile, tile, parcels[0], parcels[0], parcels[1], parcels[1]],
+        scratch_shapes=[side, side],
         compiler_params=params,
-        cost_estimate=cost(100 * field, 21 * 4 * field),
+        cost_estimate=cost(*STATE_COST),
         name="state",
-    )(events, at, rho, mom, mag, before, after)
-    below_n, above_n = shift(up_n, "gz", 1), shift(down_n, "gz", -1)
-    below_f, above_f = shift(up_f, "gz", 1), shift(down_f, "gz", -1)
-    below_l, above_l = shift(up_l, "gz", 1), shift(down_l, "gz", -1)
+    )(events, at, rho, mom, mag, arm_potential, before, after)
+    parcels_below = [shift(up_0, "gz", 1)]
+    parcels_above = [shift(down_0, "gz", -1)]
+    parcels_below.append(shift(up_1, "gz", 1))
+    parcels_above.append(shift(down_1, "gz", -1))
 
     cos_high, cos_low, sin_high, sin_low = tables(ny)
+    band = ny // across
     new_density, wave = pl.pallas_call(
         density_kernel,
         grid=(1,),
         in_specs=[
-            full((4, half + 4, 8, ny)), full(message.shape), full(message.shape), full(side.shape), full(side.shape),
+            full((4, half + 4, 8, ny)), full(tile.shape), full(tile.shape), full(tile.shape), full(tile.shape),
             full((8 * half, 8 * half)), full((2, ny, ny)), full((2, ny, ny)),
         ],
-        out_specs=[full(message.shape), full((2, planes, ny, rows))],
-        out_shape=[message, shape((2, planes, ny, rows), f32)],
+        out_specs=[full(message.shape), full((across, 2, planes, rows, band))],
+        out_shape=[message, shape((across, 2, planes, rows, band), f32)],
         scratch_shapes=[pltpu.VMEM((8 * half, ny), f32)],
         compiler_params=params,
-        cost_estimate=cost(60 * field, 13 * 4 * field),
+        cost_estimate=cost(*DENSITY_COST),
         name="density",
     )(
         state, below_a, above_a, sb, sa, row_order(half), np.stack([cos_high, -sin_high]), np.stack([cos_low, -sin_low]),
     )
-    portion = lax.all_to_all(wave, "xy", split_axis=2, concat_axis=3, tiled=True)
-
-    p_all = jnp.concatenate([p_before, arm_potential, p_after], axis=0)
-    grad_x = NEAR * (p_all[1:-3] - p_all[3:-1]) + FAR * (p_all[4:] - p_all[:-4])
-    grad_y = NEAR * (jnp.roll(arm_potential, 1, 1) - jnp.roll(arm_potential, -1, 1)) + FAR * (
-        jnp.roll(arm_potential, -2, 1) - jnp.roll(arm_potential, 2, 1)
-    )
-    gradient = jnp.stack([grad_x, grad_y]).reshape(2, 2, half, 1, ny)
-
-    chunk = math.gcd(half, 8)
-    steps = half // chunk
-    halo = pl.BlockSpec((2, chunk, planes, ny), lambda i: (0, i, 0, 0))
-    three = pl.BlockSpec((3, 2, chunk, planes, ny), lambda i: (0, 0, i, 0, 0))
-    new_mom, new_mag = pl.pallas_call(
-        main_kernel,
-        grid=(steps,),
-        in_specs=[
-            full((7, half + 4, 8, ny)), halo, halo, full(side.shape), full(side.shape), halo, halo,
-            pl.BlockSpec((2, 2, chunk, 1, ny), lambda i: (0, 0, i, 0, 0)),
-        ],
-        out_specs=[three, three],
-        out_shape=[shape((3, 2, half, planes, ny), f32)] * 2,
-        scratch_shapes=[pltpu.VMEM((5, half + 4, 8, ny), f32)],
-        compiler_params=params,
-        cost_estimate=cost(300 * field, 20 * 4 * field),
-        name="main",
-    )(state, below_a, above_a, sb, sa, below_n, above_n, gradient)
-
-    row_spec = pl.BlockSpec((chunk, 2, ny), lambda i: (i, 0, 0))
-    two = pl.BlockSpec((2, 2, chunk, planes, ny), lambda i: (0, 0, i, 0, 0))
-    new_mom, new_mag = pl.pallas_call(
-        far_kernel,
-        grid=(steps,),
-        in_specs=[halo, halo, row_spec, row_spec, three, two],
-        out_specs=[three, two],
-        out_shape=[shape((3, 2, half, planes, ny), f32)] * 2,
-        input_output_aliases={4: 0, 5: 1},
-        compiler_params=params,
-        cost_estimate=cost(30 * field, 13 * 4 * field),
-        name="far",
-    )(below_f, above_f, below_l, above_l, new_mom, new_mag)
-
-    band = ny // across
-    block = pl.BlockSpec((2, 1, band, NX), lambda z: (0, z, 0, 0))
+    portion = lax.all_to_all(wave, "xy", split_axis=0, concat_axis=0, tiled=True)
+
+    results = [shape((3, 2, half, planes, ny), f32)] * 2
+    new = []
+    for i, n in enumerate(counts):
+        first = i * n0
+        chunk = math.gcd(math.gcd(n0, half - n0), 8)
+        here = pl.BlockSpec((chunk, 8, ny), lambda k, o=first // chunk: (o + k, 0, 0))
+        near = pl.BlockSpec((chunk, 8, ny), lambda k: (k, 0, 0))
+        far = pl.BlockSpec((chunk, 8, ny), lambda k, o=n // chunk: (o + k, 0, 0))
+        last = pl.BlockSpec((chunk // 4, 8, ny), lambda k, o=8 * n // chunk: (o + k, 0, 0))
+        three = pl.BlockSpec((3, 2, chunk, planes, ny), lambda k, o=first // chunk: (0, 0, o + k, 0, 0))
+        below, above = parcels_below[i], parcels_above[i]
+        new = pl.pallas_call(
+            functools.partial(main_kernel, first=first),
+            grid=(n // chunk,),
+            in_specs=[pl.BlockSpec(memory_space=pl.ANY)] + [here] * 4 + [near] * 2 + [far] * 2 + [last] * 2
+            + [pl.BlockSpec(memory_space=pl.ANY)] * len(new),
+            out_specs=[three, three],
+            out_shape=results,
+            scratch_shapes=[
+                pltpu.VMEM((8, n + 4, 8, ny), f32), pltpu.VMEM((5, n + 4, 8, ny), f32), pltpu.SemaphoreType.DMA,
+            ],
+            input_output_aliases={11: 0, 12: 1} if new else {},
+            compiler_params=params,
+            cost_estimate=cost(*MAIN_COST),
+            name=f"main{i}",
+        )(state, below_a, above_a, sb, sa, below, above, below, above, below, above, *new)
+    new_mom, new_mag = new
+
+    turned = band % 128 != 0
+    if turned:
+        portion = portion.transpose(1, 2, 4, 0, 3).reshape(2, planes, band, NX)
     modes = pl.pallas_call(
-        modes_kernel,
-        grid=(planes,),
-        in_specs=[smem, block] + [full((NX, NX))] * 4,
-        out_specs=block,
+        functools.partial(modes_kernel, turned=turned),
+        in_specs=[smem] + [whole] * 5,
+        out_specs=whole,
         out_shape=shape((2, planes, band, NX), f32),
         compiler_params=params,
-        cost_estimate=cost(20 * field, 5 * 4 * field),
+        cost_estimate=cost(*MODES_COST),
         name="modes",
     )(at, portion, *tables(NX))
     return (

time: 175 us -> 148 us (0.85); the launches traced: 172 us -> 148 us
  local copies, waits for them, and re-layouts: 27.5 us -> 10.9 us
  waiting for transfers between devices: 38.2 us -> 45.2 us
  other arithmetic: 7.23 us -> 0.8 us
  Pallas kernels: 71.4 us -> 66.4 us
  starting transfers between devices: 25.9 us -> 22.9 us
    concatenate x5 -> x0, local copies, waits for them, and re-layouts: 8.01 us -> none  [the longest x1 2.02 us: on_device(): jnp.roll(arm_potential, -1, 1)]
    ppermute x12 -> x8, waiting for transfers between devices: 23.2 us -> 30.6 us  [shift(): return lax.ppermute(block, axis, [(i, (i + step) % n) for i in range(n)])]
    all_to_all x2 -> x0, local copies, waits for them, and re-layouts: 5.72 us -> none  [on_device(): lax.all_to_all(wave, 'xy', split_axis=2, concat_axis=3, tiled=True)]
    ppermute x12 -> x8, starting transfers between devices: 19.6 us -> 14.7 us  [shift(): return lax.ppermute(block, axis, [(i, (i + step) % n) for i in range(n)])]
    unnamed x15 -> x22, local copies, waits for them, and re-layouts: 2.64 us -> 7.18 us
    pallas_call x1 -> x0, local copies, waits for them, and re-layouts: 4.34 us -> none  [on_device(): pl.pallas_call(density_kernel, grid=(1,), in_specs=[full((4, half + 4, 8,...]
    add x2 -> x0, other arithmetic: 4.23 us -> none  [the longest x1 3.41 us: on_device(): NEAR * (jnp.roll(arm_potential, 1, 1) - jnp.roll(arm_potential, -1, 1))]
    pallas_call x3, Pallas kernels: 36.7 us -> 33.3 us  [the longest x2 26.4 us: on_device(): pl.pallas_call(functools.partial(main_kernel, first=first), grid=(n // ch...]
  transfers between devices with their start and end apart: 14 -> 10, of which waited for: 4 -> 4; matrix products, arithmetic and copies ran while one was open for 15% -> 3% of each run, Pallas kernels for 38% -> 28%
where the time goes in v3:
time: 148 us
  Pallas kernels  66.4 us (45%)
  waiting for transfers between devices  45.2 us (31%)
  starting transfers between devices  22.9 us (15%)
  local copies, waits for them, and re-layouts  10.9 us (7%)
    ppermute x8, waiting for transfers between devices, shift(): return lax.ppermute(block, axis, [(i, (i + step) % n) for i in range(n)])  30.6 us
    pallas_call x2, Pallas kernels, on_device(): pl.pallas_call(functools.partial(main_kernel, first=first), grid=(n // ch...  26.4 us
    pallas_call x1, Pallas kernels, on_device(): pl.pallas_call(functools.partial(state_kernel, depth=planes * layers), in...  15 us
    ppermute x8, starting transfers between devices, shift(): return lax.ppermute(block, axis, [(i, (i + step) % n) for i in range(n)])  14.7 us
    all_to_all x1, waiting for transfers between devices, on_device(): lax.all_to_all(jnp.broadcast_to(mine, (devices, 1, mine.shape[2])), ('gz'...  14.5 us
    pallas_call x1, Pallas kernels, on_device(): pl.pallas_call(density_kernel, grid=(1,), in_specs=[full((4, half + 4, 8,...  13.9 us
    unnamed x22, local copies, waits for them, and re-layouts  7.18 us
    pallas_call x1, Pallas kernels, on_device(): pl.pallas_call(functools.partial(modes_kernel, turned=turned), in_specs=[...  6.92 us
  transfers between devices with their start and end apart: 10, of which 4 were waited for; matrix products, arithmetic and copies ran while one was open for 3% of the time, Pallas kernels for 28%

profile of v3, /device:TPU:0, one launch (start us, length us, event | category | flops | bytes accessed | tf_op | source)
XLA Modules:
  0.0 147.6 jit_solution(10763378599864036453)
XLA Ops:
  0.6 4.2 %pack.1 = (f32[64,8,512]{2,1,0:T(8,128)}, f32[64,8,512]{2,1,0:T(8,128)}) custom-call(f32[2,64,4,512]{3,2,1,0:T(4,128)} %bitcast.22, f32[3,2,64,4,512]{4,3,2,1,0:T(4,128)} %bitcast.18, f32[3,2,64,4,512]{4,3,2,1,0:T(4,128)} %bitcast.20), custom_call_target="tpu_custom_call" | custom-call | flops 1000000 | bytes 100000 | tf_op jit(solution)/shard_map/pack/pallas_call | solution.py:441
  4.8 0.5 collective-permute-start.2
  5.3 4.0 %collective-permute-start.3 = (f32[64,8,512]{2,1,0:T(8,128)}, f32[64,8,512]{2,1,0:T(8,128)S(1)}, u32[]{:S(2)}, u32[]{:S(2)}) collective-permute-start(f32[64,8,512]{2,1,0:T(8,128)} %get-tuple-element.21), channel_id=1, source_target_pairs={{0,28},{4,0},{8,4},{12,8},{16,12},{20,16},{24,20},{28,24},{1,29},{... | collective-permute-start | bytes 3145736 | tf_op jit(solution)/shard_map/ppermute | solution.py:399
  9.3 0.7 slice_bitcast_fusion
  10.1 0.7 fusion.2
  10.8 0.9 fusion
  11.7 3.0 %collective-permute-start.1 = (f32[8,2,4,512]{3,2,1,0:T(4,128)S(1)}, f32[8,2,4,512]{3,2,1,0:T(4,128)S(1)}, u32[]{:S(2)}, u32[]{:S(2)}) collective-permute-start(f32[8,2,4,512]{3,2,1,0:T(4,128)S(1)} %pad_maximum_fusion.1), channel_id=1, source_target_pairs={{0,3},{1,0},{2,1},{3,2},{4,7},{5,4},{6,5},{7,6},{8,11},{9,8},{10,9... | collective-permute-start | bytes 393224 | tf_op jit(solution)/shard_map/ppermute | solution.py:399
  15.6 0.6 broadcast_in_dim.30
  16.2 4.5 %all-to-all-start = ((s32[32,1,128]{2,1,0:T(1,128)}), s32[32,1,128]{2,1,0:T(1,128)S(1)}, u32[]{:S(2)}, u32[]{:S(2)}) async-start(s32[32,1,128]{2,1,0:T(1,128)} %broadcast_in_dim.30), calls=%async_computation | async-start | bytes 32768 | tf_op jit(solution)/shard_map/all_to_all | solution.py:422
  20.7 0.7 pad_add_fusion.at_ref
  21.4 14.5 %all-to-all-done = s32[32,1,128]{2,1,0:T(1,128)S(1)} async-done(((s32[32,1,128]{2,1,0:T(1,128)}), s32[32,1,128]{2,1,0:T(1,128)S(1)}, u32[]{:S(2)}, u32[]{:S(2)}) %all-to-all-start) | async-done | bytes 16416 | tf_op jit(solution)/shard_map/all_to_all | solution.py:422
  36.0 0.7 reshape_squeeze.3.ev_ref
  36.6 0.6 copy-done.7
  37.3 0.7 copy-done.8
  37.9 15.0 %state.1 = (f32[8,68,8,512]{3,2,1,0:T(8,128)}, f32[64,8,512]{2,1,0:T(8,128)}, f32[64,8,512]{2,1,0:T(8,128)}, f32[90,8,512]{2,1,0:T(8,128)}, f32[90,8,512]{2,1,0:...) custom-call(s32[128]{0:T(128)} %reshape_squeeze.3.ev_ref, s32[3]{0:T(128)} %pad_add_fusion.at_ref, ...), custom_call_target="tpu_custom_call" | custom-call | flops 1000000 | bytes 100000 | tf_op jit(solution)/shard_map/state/pallas_call | solution.py:455
  53.0 1.0 copy-done.2
  53.9 0.3 copy-done.3
  54.3 13.9 %density.1 = (f32[2,64,4,512]{3,2,1,0:T(4,128)}, f32[4,2,4,128,128]{4,3,2,1,0:T(8,128)}) custom-call(f32[8,68,8,512]{3,2,1,0:T(8,128)} %get-tuple-element.19.u_ref.u_hbm, f32[64,8,512]{2,1,0:T(8,128)} %copy-done.2, f32[64,8,512]{2,1,0:T(8,128)} %copy-done.3, f32[64,8,512]{2,1,0:T(8,128)} %get-tuple-element.22.sb_ref, ...), custom_call_target="tpu_custom_call" | custom-call | flops 1000000 | bytes 100000 | tf_op jit(solution)/shard_map/density/pallas_call | solution.py:472
  68.1 3.7 %all-to-all-start.1 = ((f32[4,2,4,128,128]{4,3,2,1,0:T(8,128)}), f32[4,2,4,128,128]{4,3,2,1,0:T(8,128)S(1)}, u32[]{:S(2)}, u32[]{:S(2)}) async-start(f32[4,2,4,128,128]{4,3,2,1,0:T(8,128)} %get-tuple-element.33), calls=%async_computation.1 | async-start | bytes 4194304 | tf_op jit(solution)/shard_map/all_to_all | solution.py:488
  72.0 3.5 %collective-permute-start.7 = (f32[90,8,512]{2,1,0:T(8,128)}, f32[90,8,512]{2,1,0:T(8,128)S(1)}, u32[]{:S(2)}, u32[]{:S(2)}) collective-permute-start(f32[90,8,512]{2,1,0:T(8,128)} %get-tuple-element.28), channel_id=1, source_target_pairs={{0,28},{4,0},{8,4},{12,8},{16,12},{20,16},{24,20},{28,24},{1,29},{... | collective-permute-start | bytes 4423688 | tf_op jit(solution)/shard_map/ppermute | solution.py:399
  75.5 3.5 %collective-permute-start.5 = (f32[54,8,512]{2,1,0:T(8,128)S(1)}, f32[54,8,512]{2,1,0:T(8,128)S(1)}, u32[]{:S(2)}, u32[]{:S(2)}) collective-permute-start(f32[54,8,512]{2,1,0:T(8,128)S(1)} %copy-done.9), channel_id=1, source_target_pairs={{0,28},{4,0},{8,4},{12,8},{16,12},{20,16},{24,20},{28,24},{1,29},{... | collective-permute-start | bytes 2654216 | tf_op jit(solution)/shard_map/ppermute | solution.py:399
  79.0 29.3 %collective-permute-done.6.bn_ref.bf_ref.bl_ref = f32[90,8,512]{2,1,0:T(8,128)S(1)} collective-permute-done((f32[90,8,512]{2,1,0:T(8,128)}, f32[90,8,512]{2,1,0:T(8,128)S(1)}, u32[]{:S(2)}, u32[]{:S(2)}) %collective-permute-start.6) | collective-permute-done | bytes 1474592 | tf_op jit(solution)/shard_map/ppermute | solution.py:399
  108.4 0.2 collective-permute-done.7.an_ref.af_ref.al_ref
  108.6 0.9 copy-done
  109.5 1.1 copy-done.1
  110.6 15.6 %main0.1 = (f32[3,2,64,4,512]{4,3,2,1,0:T(4,128)}, f32[3,2,64,4,512]{4,3,2,1,0:T(4,128)}) custom-call(f32[8,68,8,512]{3,2,1,0:T(8,128)} %get-tuple-element.19.u_ref.u_hbm, f32[64,8,512]{2,1,0:T(8,128)} %copy-done.2, f32[64,8,512]{2,1,0:T(8,128)} %copy-done.3, f32[64,8,512]{2,1,0:T(8,128)} %get-tuple-element.22.sb_ref, ...), custom_call_target="tpu_custom_call" | custom-call | flops 1000000 | bytes 100000 | tf_op jit(solution)/shard_map/main0/pallas_call | solution.py:501
  126.2 1.1 collective-permute-done.4.bn_ref.bf_ref.bl_ref
  127.3 0.9 copy-done.5
  128.2 0.3 copy-done.6
  128.5 10.7 %main1.1 = (f32[3,2,64,4,512]{4,3,2,1,0:T(4,128)}, f32[3,2,64,4,512]{4,3,2,1,0:T(4,128)}) custom-call(f32[8,68,8,512]{3,2,1,0:T(8,128)} %get-tuple-element.19.u_ref.u_hbm, f32[64,8,512]{2,1,0:T(8,128)} %copy-done.2, f32[64,8,512]{2,1,0:T(8,128)} %copy-done.3, ...), custom_call_target="tpu_custom_call", output_to_operand_aliasing={{0}: (11, {}), {1}: (12, {})} | custom-call | flops 1000000 | bytes 100000 | tf_op jit(solution)/shard_map/main1/pallas_call | solution.py:501
  139.3 1.3 copy-done.4
  140.6 6.9 %modes.1 = f32[2,4,128,512]{3,2,1,0:T(8,128)} custom-call(s32[3]{0:T(128)} %pad_add_fusion.at_ref, f32[4,2,4,128,128]{4,3,2,1,0:T(8,128)} %copy-done.4, bf16[512,512]{1,0:T(8,128)(2,1)} %constant.32.clone.ch_ref, bf16[512,512]{1,0:T(8,128)(2,1)} %constant.33.clone.cl_ref, bf16[512,512]{1,0:T(8,128)(2,1)} %constant.34.clone.sh_ref, ...), custom_call_target="tpu_custom_call" | custom-call | flops 1000000 | bytes 100000 | tf_op jit(solution)/shard_map/modes/pallas_call | solution.py:521
  (29 shorter events, 0.4 us)
Async XLA Ops:
  0.6 14.9 %copy-start.10 = (s32[1,3]{1,0:T(1,128)S(1)}, s32[1,3]{1,0:T(1,128)}, u32[]{:S(2)}) copy-start(s32[1,3]{1,0:T(1,128)} %param.17) | copy-start | bytes 40
  4.8 48.1 %collective-permute-start.2 = (f32[64,8,512]{2,1,0:T(8,128)}, f32[64,8,512]{2,1,0:T(8,128)S(1)}, u32[]{:S(2)}, u32[]{:S(2)}) collective-permute-start(f32[64,8,512]{2,1,0:T(8,128)} %get-tuple-element.20), channel_id=1, source_target_pairs={{0,4},{4,8},{8,12},{12,16},{16,20},{20,24},{24,28},{28,0},{1,5},{5... | collective-permute-start | bytes 3145736 | tf_op jit(solution)/shard_map/ppermute | solution.py:399
  5.3 47.7 %collective-permute-start.3 = (f32[64,8,512]{2,1,0:T(8,128)}, f32[64,8,512]{2,1,0:T(8,128)S(1)}, u32[]{:S(2)}, u32[]{:S(2)}) collective-permute-start(f32[64,8,512]{2,1,0:T(8,128)} %get-tuple-element.21), channel_id=1, source_target_pairs={{0,28},{4,0},{8,4},{12,8},{16,12},{20,16},{24,20},{28,24},{1,29},{... | collective-permute-start | bytes 3145736 | tf_op jit(solution)/shard_map/ppermute | solution.py:399
  11.7 24.9 %collective-permute-start.1 = (f32[8,2,4,512]{3,2,1,0:T(4,128)S(1)}, f32[8,2,4,512]{3,2,1,0:T(4,128)S(1)}, u32[]{:S(2)}, u32[]{:S(2)}) collective-permute-start(f32[8,2,4,512]{3,2,1,0:T(4,128)S(1)} %pad_maximum_fusion.1), channel_id=1, source_target_pairs={{0,3},{1,0},{2,1},{3,2},{4,7},{5,4},{6,5},{7,6},{8,11},{9,8},{10,9... | collective-permute-start | bytes 393224 | tf_op jit(solution)/shard_map/ppermute | solution.py:399
  14.8 21.9 %collective-permute-start = (f32[8,2,4,512]{3,2,1,0:T(4,128)S(1)}, f32[8,2,4,512]{3,2,1,0:T(4,128)S(1)}, u32[]{:S(2)}, u32[]{:S(2)}) collective-permute-start(f32[8,2,4,512]{3,2,1,0:T(4,128)S(1)} %pad_maximum_fusion), channel_id=1, source_target_pairs={{0,1},{1,2},{2,3},{3,0},{4,5},{5,6},{6,7},{7,4},{8,9},{9,10},{10,1... | collective-permute-start | bytes 393224 | tf_op jit(solution)/shard_map/ppermute | solution.py:399
  16.2 19.7 %all-to-all-start = ((s32[32,1,128]{2,1,0:T(1,128)}), s32[32,1,128]{2,1,0:T(1,128)S(1)}, u32[]{:S(2)}, u32[]{:S(2)}) async-start(s32[32,1,128]{2,1,0:T(1,128)} %broadcast_in_dim.30), calls=%async_computation | async-start | bytes 32768 | tf_op jit(solution)/shard_map/all_to_all | solution.py:422
  36.6 0.6 copy-start.7
  37.3 0.7 copy-start.8
  53.0 1.0 copy-start.2
  53.0 1.3 copy-start.3
  68.1 7.4 %copy-start.9 = (f32[54,8,512]{2,1,0:T(8,128)S(1)}, f32[54,8,512]{2,1,0:T(8,128)}, u32[]{:S(2)}) copy-start(f32[54,8,512]{2,1,0:T(8,128)} %get-tuple-element.26) | copy-start | bytes 2654212
  68.1 71.1 %all-to-all-start.1 = ((f32[4,2,4,128,128]{4,3,2,1,0:T(8,128)}), f32[4,2,4,128,128]{4,3,2,1,0:T(8,128)S(1)}, u32[]{:S(2)}, u32[]{:S(2)}) async-start(f32[4,2,4,128,128]{4,3,2,1,0:T(8,128)} %get-tuple-element.33), calls=%async_computation.1 | async-start | bytes 4194304 | tf_op jit(solution)/shard_map/all_to_all | solution.py:488
  71.9 36.5 %collective-permute-start.6 = (f32[90,8,512]{2,1,0:T(8,128)}, f32[90,8,512]{2,1,0:T(8,128)S(1)}, u32[]{:S(2)}, u32[]{:S(2)}) collective-permute-start(f32[90,8,512]{2,1,0:T(8,128)} %get-tuple-element.27), channel_id=1, source_target_pairs={{0,4},{4,8},{8,12},{12,16},{16,20},{20,24},{24,28},{28,0},{1,5},{5... | collective-permute-start | bytes 4423688 | tf_op jit(solution)/shard_map/ppermute | solution.py:399
  72.0 36.6 %collective-permute-start.7 = (f32[90,8,512]{2,1,0:T(8,128)}, f32[90,8,512]{2,1,0:T(8,128)S(1)}, u32[]{:S(2)}, u32[]{:S(2)}) collective-permute-start(f32[90,8,512]{2,1,0:T(8,128)} %get-tuple-element.28), channel_id=1, source_target_pairs={{0,28},{4,0},{8,4},{12,8},{16,12},{20,16},{24,20},{28,24},{1,29},{... | collective-permute-start | bytes 4423688 | tf_op jit(solution)/shard_map/ppermute | solution.py:399
  75.5 51.8 %collective-permute-start.4 = (f32[54,8,512]{2,1,0:T(8,128)}, f32[54,8,512]{2,1,0:T(8,128)S(1)}, u32[]{:S(2)}, u32[]{:S(2)}) collective-permute-start(f32[54,8,512]{2,1,0:T(8,128)} %get-tuple-element.25), channel_id=1, source_target_pairs={{0,4},{4,8},{8,12},{12,16},{16,20},{20,24},{24,28},{28,0},{1,5},{5... | collective-permute-start | bytes 2654216 | tf_op jit(solution)/shard_map/ppermute | solution.py:399
  75.5 51.8 %collective-permute-start.5 = (f32[54,8,512]{2,1,0:T(8,128)S(1)}, f32[54,8,512]{2,1,0:T(8,128)S(1)}, u32[]{:S(2)}, u32[]{:S(2)}) collective-permute-start(f32[54,8,512]{2,1,0:T(8,128)S(1)} %copy-done.9), channel_id=1, source_target_pairs={{0,28},{4,0},{8,4},{12,8},{16,12},{20,16},{24,20},{28,24},{1,29},{... | collective-permute-start | bytes 2654216 | tf_op jit(solution)/shard_map/ppermute | solution.py:399
  108.4 1.1 copy-start
  109.5 1.1 copy-start.1
  127.3 0.9 copy-start.5
  127.3 1.2 copy-start.6
  139.3 1.3 copy-start.4

commit v4 on v3

--- a/solution.py
+++ b/solution.py
@@ -18,7 +18,8 @@
 NEAR = 8.0 * TIME_STEP / 12.0
 FAR = TIME_STEP / 12.0
 VMEM = 56 * 1024 * 1024
-PACK_COST = STATE_COST = DENSITY_COST = MAIN_COST = MODES_COST = (1e6, 1e5)
+PACK_COST = DENSITY_COST = MODES_COST = (1e6, 1e5)
+STATE_COST = MAIN_COST = (1e6, 4e8)
 
 
 def pair(ref, *index):
@@ -47,10 +48,12 @@
     return out
 
 
-def fluxes(rho, m, b, k):
+def shared(rho, m, b):
     inv = 1.0 / rho
-    v = [m[i] * inv for i in range(3)]
-    total = rho + 0.5 * (b[0] * b[0] + b[1] * b[1] + b[2] * b[2])
+    return [x * inv for x in m], rho + 0.5 * (b[0] * b[0] + b[1] * b[1] + b[2] * b[2])
+
+
+def fluxes(v, total, m, b, k):
     push = [m[i] * v[k] - b[i] * b[k] + (total if i == k else 0.0) for i in range(3)]
     turned = [None if i == k else v[k] * b[i] - b[k] * v[i] for i in range(3)]
     return push + turned
@@ -171,7 +174,7 @@
                 near = [u[1], u[2], u[5], u[6]]
                 up_ref[r] = gather_planes(near, 3)
                 down_ref[r] = gather_planes(near, 0)
-                f = fluxes(u[0], u[1:4], u[4:7], 2)
+                f = fluxes(*shared(u[0], u[1:4], u[4:7]), u[1:4], u[4:7], 2)
                 up_ref[count + r] = gather_planes(f[:4], 2)
                 down_ref[count + r] = gather_planes(f[:4], 1)
                 for i, plane in enumerate((2, 1)):
@@ -189,44 +192,26 @@
     group(up_1, down_1, split, half - split)
 
 
-def ends(below, above, c, fill):
-    slot = slots(below.shape)
-    rest = jnp.where(slot == 3, turn(above, 3 - c, 0), fill)
-    return jnp.where(slot == 0, turn(below, -c, 0), rest)
-
-
-def signs(shape):
-    slot = slots(shape)
-    return jnp.where(slot == 0, 1.0, jnp.where(slot == 3, -1.0, 0.0))
-
-
-def along_y(f, u):
-    low, high = NEAR * f + DIFFUSION * u, DIFFUSION * u - NEAR * f
-    far = FAR * f
-    return turn(low, 1, 1) + turn(high, -1, 1) + turn(far, -2, 1) - turn(far, 2, 1)
-
-
-def along_z(f, u):
-    slot = slots(u.shape)
-    part = lambda keep, v: jnp.where(keep, v, 0.0)
+def ends(below, above, c):
+    return jnp.where(slots(below.shape) == 3, turn(above, 3 - c, 0), turn(below, -c, 0))
+
+
+def along_y(f, b):
+    near, far = NEAR * f, FAR * f
+    return turn(b + near, 1, 1) + turn(b - near, -1, 1) + turn(far, -2, 1) - turn(far, 2, 1)
+
+
+def along_z(f, b, near_f, near_u, far_f):
+    slot = slots(b.shape)
+    first, last = slot == 0, slot == 3
+    outer = DIFFUSION * near_u
     if f is None:
-        return part(slot >= 1, turn(DIFFUSION * u, 1, 0)) + part(slot <= 2, turn(DIFFUSION * u, -1, 0))
-    low, high = NEAR * f + DIFFUSION * u, DIFFUSION * u - NEAR * f
-    far = FAR * f
-    return (
-        part(slot >= 1, turn(low, 1, 0)) + part(slot <= 2, turn(high, -1, 0))
-        + part(slot <= 1, turn(far, -2, 0)) - part(slot >= 2, turn(far, 2, 0))
-    )
-
-
-def near_planes(f, u, sign):
-    outer = DIFFUSION * u
-    if f is None:
-        return outer
-    slot = slots(u.shape)
-    t = (FAR * sign) * f
-    inner = jnp.where(slot == 1, turn(t, 1, 0), jnp.where(slot == 2, turn(t, -1, 0), 0.0))
-    return outer + 8.0 * t - inner
+        return jnp.where(first, outer, turn(b, 1, 0)) + jnp.where(last, outer, turn(b, -1, 0))
+    near = NEAR * f
+    outer += jnp.where(first, NEAR, -NEAR) * near_f
+    out = jnp.where(first, outer, turn(b + near, 1, 0)) + jnp.where(last, outer, turn(b - near, -1, 0))
+    beyond = jnp.where(slot == 1, turn(near_f, 1, 0), jnp.where(slot == 2, turn(near_f, -1, 0), far_f))
+    return out + FAR * (jnp.where(slot <= 1, turn(f, -2, 0), beyond) - jnp.where(slot >= 2, turn(f, 2, 0), beyond))
 
 
 def density_kernel(u_ref, below_ref, above_ref, sb_ref, sa_ref, order_ref, high_ref, low_ref, out_ref, wave_ref, d_ref):
@@ -236,13 +221,12 @@
     def body(p, _):
         rho, my, mz = u_ref[0, p + 2], u_ref[2, p + 2], u_ref[3, p + 2]
         below, above = below_ref[p] + sb_ref[p], above_ref[p] + sa_ref[p]
-        slot, sign = slots(rho.shape), signs(rho.shape)
+        b = DIFFUSION * rho
         new = rho * (1.0 - 6.0 * DIFFUSION)
         new += DIFFUSION * (u_ref[0, p + 1] + u_ref[0, p + 3])
         new += NEAR * (u_ref[1, p + 1] - u_ref[1, p + 3]) + FAR * (u_ref[1, p + 4] - u_ref[1, p])
-        new += along_y(my, rho) + along_z(mz, rho)
-        new += near_planes(ends(below, above, 1, 0.0), ends(below, above, 0, 0.0), sign)
-        new -= (FAR * sign) * ends(below, above, 2, 0.0)
+        new += along_y(my, b)
+        new += along_z(mz, b, ends(below, above, 1), ends(below, above, 0), ends(below, above, 2))
         unpair(out_ref, new, p)
         d_ref[pl.ds(pl.multiple_of(p * 8, 8), 8), :] = new
         return 0
@@ -266,11 +250,10 @@
 
 def last_plane(below, above, j):
     sub = lax.broadcasted_iota(jnp.int32, below.shape, 0)
-    out = jnp.zeros_like(below)
-    for h in range(2):
-        out = jnp.where(sub == 4 * h, turn(below, 4 * h - (2 * j + h), 0), out)
-        out = jnp.where(sub == 4 * h + 3, turn(above, 4 * h + 3 - (2 * j + h), 0), out)
-    return out
+    out = turn(below, -2 * j, 0)
+    out = jnp.where(sub == 3, turn(above, 3 - 2 * j, 0), out)
+    out = jnp.where(sub == 4, turn(below, 3 - 2 * j, 0), out)
+    return jnp.where(sub == 7, turn(above, 6 - 2 * j, 0), out)
 
 
 def main_kernel(
@@ -289,7 +272,7 @@
 
         def fx(q, _):
             u = [u_ref[f, q] for f in range(7)]
-            f = fluxes(u[0], u[1:4], u[4:7], 0)
+            f = fluxes(*shared(u[0], u[1:4], u[4:7]), u[1:4], u[4:7], 0)
             for i, c in enumerate(kept):
                 f_ref[i, q] = f[c]
             return 0
@@ -299,16 +282,16 @@
     def row(r, g, j):
         q = start + r + 2
         u = [u_ref[f, q] for f in range(7)]
-        fy = fluxes(u[0], u[1:4], u[4:7], 1)
-        fz = fluxes(u[0], u[1:4], u[4:7], 2)
-        sign = signs(u[0].shape)
+        v, pressure = shared(u[0], u[1:4], u[4:7])
+        fy = fluxes(v, pressure, u[1:4], u[4:7], 1)
+        fz = fluxes(v, pressure, u[1:4], u[4:7], 2)
         ba, aa = ba_ref[r] + sb_ref[r], aa_ref[r] + sa_ref[r]
         bn, an, bf, af = bn_ref[r], an_ref[r], bf_ref[r], af_ref[r]
-        hm = [ends(bn, an, 0, 0.0), ends(bn, an, 1, 0.0), ends(ba, aa, 1, 0.0)]
-        hb = [ends(ba, aa, 3, 0.0), ends(bn, an, 2, 0.0), ends(bn, an, 3, 0.0)]
-        fh = fluxes(ends(ba, aa, 0, 1.0), hm, hb, 2)
+        hm = [ends(bn, an, 0), ends(bn, an, 1), ends(ba, aa, 1)]
+        hb = [ends(ba, aa, 3), ends(bn, an, 2), ends(bn, an, 3)]
+        fh = fluxes(*shared(ends(ba, aa, 0), hm, hb), hm, hb, 2)
         halo = hm + hb
-        far = [ends(bf, af, c, 0.0) for c in range(4)] + [last_plane(bl_ref[g], al_ref[g], j), None]
+        far = [ends(bf, af, c) for c in range(4)] + [last_plane(bl_ref[g], al_ref[g], j), None]
         for c in range(6):
             field = u[c + 1]
             new = field * (1.0 - 6.0 * DIFFUSION)
@@ -316,14 +299,12 @@
             if c in kept:
                 i = kept.index(c)
                 new += NEAR * (f_ref[i, q - 1] - f_ref[i, q + 1]) + FAR * (f_ref[i, q + 2] - f_ref[i, q - 2])
+            b = DIFFUSION * field
             if fy[c] is None:
-                new += DIFFUSION * (turn(field, 1, 1) + turn(field, -1, 1))
+                new += turn(b, 1, 1) + turn(b, -1, 1)
             else:
-                new += along_y(fy[c], field)
-            new += along_z(fz[c], field)
-            new += near_planes(fh[c], halo[c], sign)
-            if far[c] is not None:
-                new -= (FAR * sign) * far[c]
+                new += along_y(fy[c], b)
+            new += along_z(fz[c], b, fh[c], halo[c], far[c])
             if c == 0:
                 slope = NEAR * (u_ref[7, q - 1] - u_ref[7, q + 1]) + FAR * (u_ref[7, q + 2] - u_ref[7, q - 2])
                 new += u[0] * slope
@@ -487,34 +468,6 @@
     )
     portion = lax.all_to_all(wave, "xy", split_axis=0, concat_axis=0, tiled=True)
 
-    results = [shape((3, 2, half, planes, ny), f32)] * 2
-    new = []
-    for i, n in enumerate(counts):
-        first = i * n0
-        chunk = math.gcd(math.gcd(n0, half - n0), 8)
-        here = pl.BlockSpec((chunk, 8, ny), lambda k, o=first // chunk: (o + k, 0, 0))
-        near = pl.BlockSpec((chunk, 8, ny), lambda k: (k, 0, 0))
-        far = pl.BlockSpec((chunk, 8, ny), lambda k, o=n // chunk: (o + k, 0, 0))
-        last = pl.BlockSpec((chunk // 4, 8, ny), lambda k, o=8 * n // chunk: (o + k, 0, 0))
-        three = pl.BlockSpec((3, 2, chunk, planes, ny), lambda k, o=first // chunk: (0, 0, o + k, 0, 0))
-        below, above = parcels_below[i], parcels_above[i]
-        new = pl.pallas_call(
-            functools.partial(main_kernel, first=first),
-            grid=(n // chunk,),
-            in_specs=[pl.BlockSpec(memory_space=pl.ANY)] + [here] * 4 + [near] * 2 + [far] * 2 + [last] * 2
-            + [pl.BlockSpec(memory_space=pl.ANY)] * len(new),
-            out_specs=[three, three],
-            out_shape=results,
-            scratch_shapes=[
-                pltpu.VMEM((8, n + 4, 8, ny), f32), pltpu.VMEM((5, n + 4, 8, ny), f32), pltpu.SemaphoreType.DMA,
-            ],
-            input_output_aliases={11: 0, 12: 1} if new else {},
-            compiler_params=params,
-            cost_estimate=cost(*MAIN_COST),
-            name=f"main{i}",
-        )(state, below_a, above_a, sb, sa, below, above, below, above, below, above, *new)
-    new_mom, new_mag = new
-
     turned = band % 128 != 0
     if turned:
         portion = portion.transpose(1, 2, 4, 0, 3).reshape(2, planes, band, NX)
@@ -527,6 +480,35 @@
         cost_estimate=cost(*MODES_COST),
         name="modes",
     )(at, portion, *tables(NX))
+    results = [shape((3, 2, half, planes, ny), f32)] * 2
+    new = []
+    for i, n in enumerate(counts):
+        first = i * n0
+        chunk = math.gcd(math.gcd(n0, half - n0), 8)
+        here = pl.BlockSpec((chunk, 8, ny), lambda k, o=first // chunk: (o + k, 0, 0))
+        near = pl.BlockSpec((chunk, 8, ny), lambda k: (k, 0, 0))
+        far = pl.BlockSpec((chunk, 8, ny), lambda k, o=n // chunk: (o + k, 0, 0))
+        last = pl.BlockSpec((chunk // 4, 8, ny), lambda k, o=8 * n // chunk: (o + k, 0, 0))
+        three = pl.BlockSpec((3, 2, chunk, planes, ny), lambda k, o=first // chunk: (0, 0, o + k, 0, 0))
+        below, above = parcels_below[i], parcels_above[i]
+        extra = [*new, modes] if new else []
+        new = pl.pallas_call(
+            functools.partial(main_kernel, first=first),
+            grid=(n // chunk,),
+            in_specs=[pl.BlockSpec(memory_space=pl.ANY)] + [here] * 4 + [near] * 2 + [far] * 2 + [last] * 2
+            + [pl.BlockSpec(memory_space=pl.ANY)] * len(extra),
+            out_specs=[three, three],
+            out_shape=results,
+            scratch_shapes=[
+                pltpu.VMEM((8, n + 4, 8, ny), f32), pltpu.VMEM((5, n + 4, 8, ny), f32), pltpu.SemaphoreType.DMA,
+            ],
+            input_output_aliases={11: 0, 12: 1} if new else {},
+            compiler_params=pltpu.CompilerParams(vmem_limit_bytes=62 * 1024 * 1024),
+            cost_estimate=cost(*MAIN_COST),
+            name=f"main{i}",
+        )(state, below_a, above_a, sb, sa, below, above, below, above, below, above, *extra)
+    new_mom, new_mag = new
+
     return (
         new_density.reshape(rows, planes, ny),
         new_mom.reshape(3, rows, planes, ny),

time: 148 us -> 132 us (0.89)
  waiting for transfers between devices: 45.2 us -> 32.4 us
  local copies, waits for them, and re-layouts: 10.9 us -> 6.59 us
  starting transfers between devices: 22.9 us -> 25.6 us
  Pallas kernels: 66.4 us -> 64.3 us
    all_to_all x1, waiting for transfers between devices: 14.5 us -> 0.01 us  [on_device(): lax.all_to_all(jnp.broadcast_to(mine, (devices, 1, mine.shape[2])), ('gz'...]
    unnamed x22 -> x12, local copies, waits for them, and re-layouts: 7.18 us -> 2.86 us
    all_to_all x1, starting transfers between devices: 4.52 us -> 7.3 us  [on_device(): lax.all_to_all(jnp.broadcast_to(mine, (devices, 1, mine.shape[2])), ('gz'...]
    ppermute x8, waiting for transfers between devices: 30.6 us -> 32.4 us  [shift(): return lax.ppermute(block, axis, [(i, (i + step) % n) for i in range(n)])]
    pallas_call x2, Pallas kernels: 26.4 us -> 24.8 us  [on_device(): pl.pallas_call(functools.partial(main_kernel, first=first), grid=(n // ch...]
  transfers between devices with their start and end apart: 10 -> 10, of which waited for: 4 -> 4; matrix products, arithmetic and copies ran while one was open for 3% -> 3% of each run, Pallas kernels for 28% -> 31%
where the time goes in v4:
time: 132 us
  Pallas kernels  64.3 us (49%)
  waiting for transfers between devices  32.4 us (25%)
  starting transfers between devices  25.6 us (19%)
  local copies, waits for them, and re-layouts  6.59 us (5%)
  other arithmetic  1.39 us (1%)
  between operations  1.39 us (1%)
    ppermute x8, waiting for transfers between devices, shift(): return lax.ppermute(block, axis, [(i, (i + step) % n) for i in range(n)])  32.4 us
    pallas_call x2, Pallas kernels, on_device(): pl.pallas_call(functools.partial(main_kernel, first=first), grid=(n // ch...  24.8 us
    pallas_call x1, Pallas kernels, on_device(): pl.pallas_call(functools.partial(state_kernel, depth=planes * layers), in...  14.7 us
    pallas_call x1, Pallas kernels, on_device(): pl.pallas_call(density_kernel, grid=(1,), in_specs=[full((4, half + 4, 8,...  13.7 us
    ppermute x8, starting transfers between devices, shift(): return lax.ppermute(block, axis, [(i, (i + step) % n) for i in range(n)])  13.7 us
    all_to_all x1, starting transfers between devices, on_device(): lax.all_to_all(jnp.broadcast_to(mine, (devices, 1, mine.shape[2])), ('gz'...  7.3 us
    pallas_call x1, Pallas kernels, on_device(): pl.pallas_call(functools.partial(modes_kernel, turned=turned), in_specs=[...  6.93 us
    all_to_all x1, starting transfers between devices, on_device(): lax.all_to_all(wave, 'xy', split_axis=0, concat_axis=0, tiled=True)  4.58 us
  transfers between devices with their start and end apart: 10, of which 4 were waited for; matrix products, arithmetic and copies ran while one was open for 3% of the time, Pallas kernels for 31%

profile of v4, /device:TPU:0, one launch (start us, length us, event | category | flops | bytes accessed | tf_op | source)
XLA Modules:
  0.0 131.7 jit_solution(5017447591604451269)
XLA Ops:
  1.3 0.7 add_bitcast_fusion
  2.0 0.6 broadcast_in_dim.30
  2.6 7.3 %all-to-all-start = ((s32[32,1,128]{2,1,0:T(1,128)}), s32[32,1,128]{2,1,0:T(1,128)S(1)}, u32[]{:S(2)}, u32[]{:S(2)}) async-start(s32[32,1,128]{2,1,0:T(1,128)} %broadcast_in_dim.30), calls=%async_computation | async-start | bytes 32768 | tf_op jit(solution)/shard_map/all_to_all | solution.py:403
  9.9 4.2 %pack.1 = (f32[64,8,512]{2,1,0:T(8,128)}, f32[64,8,512]{2,1,0:T(8,128)}) custom-call(f32[2,64,4,512]{3,2,1,0:T(4,128)} %bitcast.22, f32[3,2,64,4,512]{4,3,2,1,0:T(4,128)} %bitcast.18, f32[3,2,64,4,512]{4,3,2,1,0:T(4,128)} %bitcast.20), custom_call_target="tpu_custom_call" | custom-call | flops 1000000 | bytes 100000 | tf_op jit(solution)/shard_map/pack/pallas_call | solution.py:422
  14.1 0.3 collective-permute-start.2
  14.4 3.3 %collective-permute-start.3 = (f32[64,8,512]{2,1,0:T(8,128)}, f32[64,8,512]{2,1,0:T(8,128)S(1)}, u32[]{:S(2)}, u32[]{:S(2)}) collective-permute-start(f32[64,8,512]{2,1,0:T(8,128)} %get-tuple-element.21), channel_id=1, source_target_pairs={{0,28},{4,0},{8,4},{12,8},{16,12},{20,16},{24,20},{28,24},{1,29},{... | collective-permute-start | bytes 3145736 | tf_op jit(solution)/shard_map/ppermute | solution.py:380
  17.7 0.7 fusion.2
  18.4 0.7 slice_bitcast_fusion
  19.1 0.9 fusion
  20.1 1.8 %collective-permute-start = (f32[8,2,4,512]{3,2,1,0:T(4,128)S(1)}, f32[8,2,4,512]{3,2,1,0:T(4,128)S(1)}, u32[]{:S(2)}, u32[]{:S(2)}) collective-permute-start(f32[8,2,4,512]{3,2,1,0:T(4,128)S(1)} %pad_maximum_fusion), channel_id=1, source_target_pairs={{0,1},{1,2},{2,3},{3,0},{4,5},{5,6},{6,7},{7,4},{8,9},{9,10},{10,1... | collective-permute-start | bytes 393224 | tf_op jit(solution)/shard_map/ppermute | solution.py:380
  21.9 1.2 collective-permute-start.1
  23.2 0.6 pad_add_fusion.at_ref
  23.8 0.7 reshape_squeeze.3.ev_ref
  24.5 1.7 %collective-permute-done.before_ref = f32[8,2,4,512]{3,2,1,0:T(4,128)S(1)} collective-permute-done((f32[8,2,4,512]{3,2,1,0:T(4,128)S(1)}, f32[8,2,4,512]{3,2,1,0:T(4,128)S(1)}, u32[]{:S(2)}, u32[]{:S(2)}) %collective-permute-start) | collective-permute-done | bytes 131104 | tf_op jit(solution)/shard_map/ppermute | solution.py:380
  26.2 1.5 %collective-permute-done.1.after_ref = f32[8,2,4,512]{3,2,1,0:T(4,128)S(1)} collective-permute-done((f32[8,2,4,512]{3,2,1,0:T(4,128)S(1)}, f32[8,2,4,512]{3,2,1,0:T(4,128)S(1)}, u32[]{:S(2)}, u32[]{:S(2)}) %collective-permute-start.1) | collective-permute-done | bytes 131104 | tf_op jit(solution)/shard_map/ppermute | solution.py:380
  27.7 0.7 copy-done.4
  28.4 14.7 %state.1 = (f32[8,68,8,512]{3,2,1,0:T(8,128)}, f32[64,8,512]{2,1,0:T(8,128)}, f32[64,8,512]{2,1,0:T(8,128)}, f32[90,8,512]{2,1,0:T(8,128)}, f32[90,8,512]{2,1,0:...) custom-call(s32[128]{0:T(128)} %reshape_squeeze.3.ev_ref, s32[3]{0:T(128)} %pad_add_fusion.at_ref, ...), custom_call_target="tpu_custom_call" | custom-call | flops 1000000 | bytes 400000000 | tf_op jit(solution)/shard_map/state/pallas_call | solution.py:436
  43.1 0.0 collective-permute-done.2.below_ref.ba_ref
  43.1 0.0 collective-permute-done.3.above_ref.aa_ref
  43.1 1.0 copy-done.1
  44.1 0.3 copy-done.2
  44.4 13.7 %density.1 = (f32[2,64,4,512]{3,2,1,0:T(4,128)}, f32[4,2,4,128,128]{4,3,2,1,0:T(8,128)}) custom-call(f32[8,68,8,512]{3,2,1,0:T(8,128)} %get-tuple-element.19.u_ref.u_hbm, f32[64,8,512]{2,1,0:T(8,128)} %copy-done.1, f32[64,8,512]{2,1,0:T(8,128)} %copy-done.2, f32[64,8,512]{2,1,0:T(8,128)} %get-tuple-element.22.sb_ref, ...), custom_call_target="tpu_custom_call" | custom-call | flops 1000000 | bytes 100000 | tf_op jit(solution)/shard_map/density/pallas_call | solution.py:453
  58.2 4.6 %all-to-all-start.1 = ((f32[4,2,4,128,128]{4,3,2,1,0:T(8,128)}), f32[4,2,4,128,128]{4,3,2,1,0:T(8,128)}, u32[]{:S(2)}, u32[]{:S(2)}) async-start(f32[4,2,4,128,128]{4,3,2,1,0:T(8,128)} %get-tuple-element.31), calls=%async_computation.1 | async-start | bytes 4194304 | tf_op jit(solution)/shard_map/all_to_all | solution.py:469
  62.8 0.1 collective-permute-start.6
  62.8 3.5 %collective-permute-start.7 = (f32[90,8,512]{2,1,0:T(8,128)S(1)}, f32[90,8,512]{2,1,0:T(8,128)}, u32[]{:S(2)}, u32[]{:S(2)}) collective-permute-start(f32[90,8,512]{2,1,0:T(8,128)S(1)} %copy-done.5), channel_id=1, source_target_pairs={{0,28},{4,0},{8,4},{12,8},{16,12},{20,16},{24,20},{28,24},{1,29},{... | collective-permute-start | bytes 4423688 | tf_op jit(solution)/shard_map/ppermute | solution.py:380
  66.4 3.5 %collective-permute-start.5 = (f32[54,8,512]{2,1,0:T(8,128)}, f32[54,8,512]{2,1,0:T(8,128)}, u32[]{:S(2)}, u32[]{:S(2)}) collective-permute-start(f32[54,8,512]{2,1,0:T(8,128)} %get-tuple-element.26), channel_id=1, source_target_pairs={{0,28},{4,0},{8,4},{12,8},{16,12},{20,16},{24,20},{28,24},{1,29},{... | collective-permute-start | bytes 2654216 | tf_op jit(solution)/shard_map/ppermute | solution.py:380
  69.9 29.0 %collective-permute-done.6.bn_ref.bf_ref.bl_ref = f32[90,8,512]{2,1,0:T(8,128)S(1)} collective-permute-done((f32[90,8,512]{2,1,0:T(8,128)}, f32[90,8,512]{2,1,0:T(8,128)S(1)}, u32[]{:S(2)}, u32[]{:S(2)}) %collective-permute-start.6) | collective-permute-done | bytes 1474592 | tf_op jit(solution)/shard_map/ppermute | solution.py:380
  98.9 0.2 collective-permute-done.7.an_ref.af_ref.al_ref
  99.1 0.9 copy-done
  100.0 14.6 %main0.1 = (f32[3,2,64,4,512]{4,3,2,1,0:T(4,128)}, f32[3,2,64,4,512]{4,3,2,1,0:T(4,128)}) custom-call(f32[8,68,8,512]{3,2,1,0:T(8,128)} %get-tuple-element.19.u_ref.u_hbm, f32[64,8,512]{2,1,0:T(8,128)} %copy-done.1, f32[64,8,512]{2,1,0:T(8,128)} %copy-done.2, f32[64,8,512]{2,1,0:T(8,128)} %get-tuple-element.22.sb_ref, ...), custom_call_target="tpu_custom_call" | custom-call | flops 1000000 | bytes 400000000 | tf_op jit(solution)/shard_map/main0/pallas_call | solution.py:495
  114.6 6.9 %modes.1.rest_2_ = f32[2,4,128,512]{3,2,1,0:T(8,128)} custom-call(s32[3]{0:T(128)} %pad_add_fusion.at_ref, f32[4,2,4,128,128]{4,3,2,1,0:T(8,128)} %all-to-all-done.1.w_ref, bf16[512,512]{1,0:T(8,128)(2,1)} %constant.32.clone.ch_ref, bf16[512,512]{1,0:T(8,128)(2,1)} %constant.33.clone.cl_ref, bf16[512,512]{1,0:T(8,128)(2,1)} %constant.34.clone.sh_ref, ...), custom_call_target="tpu_custom_call" | custom-call | flops 1000000 | bytes 100000 | tf_op jit(solution)/shard_map/modes/pallas_call | solution.py:474
  121.6 10.2 %main1.1 = (f32[3,2,64,4,512]{4,3,2,1,0:T(4,128)}, f32[3,2,64,4,512]{4,3,2,1,0:T(4,128)}) custom-call(f32[8,68,8,512]{3,2,1,0:T(8,128)} %get-tuple-element.19.u_ref.u_hbm, f32[64,8,512]{2,1,0:T(8,128)} %copy-done.1, f32[64,8,512]{2,1,0:T(8,128)} %copy-done.2, ...), custom_call_target="tpu_custom_call", output_to_operand_aliasing={{0}: (11, {}), {1}: (12, {})} | custom-call | flops 1000000 | bytes 400000000 | tf_op jit(solution)/shard_map/main1/pallas_call | solution.py:495
  (19 shorter events, 0.2 us)
Async XLA Ops:
  2.6 21.1 %all-to-all-start = ((s32[32,1,128]{2,1,0:T(1,128)}), s32[32,1,128]{2,1,0:T(1,128)S(1)}, u32[]{:S(2)}, u32[]{:S(2)}) async-start(s32[32,1,128]{2,1,0:T(1,128)} %broadcast_in_dim.30), calls=%async_computation | async-start | bytes 32768 | tf_op jit(solution)/shard_map/all_to_all | solution.py:403
  14.1 29.0 %collective-permute-start.2 = (f32[64,8,512]{2,1,0:T(8,128)}, f32[64,8,512]{2,1,0:T(8,128)S(1)}, u32[]{:S(2)}, u32[]{:S(2)}) collective-permute-start(f32[64,8,512]{2,1,0:T(8,128)} %get-tuple-element.20), channel_id=1, source_target_pairs={{0,4},{4,8},{8,12},{12,16},{16,20},{20,24},{24,28},{28,0},{1,5},{5... | collective-permute-start | bytes 3145736 | tf_op jit(solution)/shard_map/ppermute | solution.py:380
  14.4 28.8 %collective-permute-start.3 = (f32[64,8,512]{2,1,0:T(8,128)}, f32[64,8,512]{2,1,0:T(8,128)S(1)}, u32[]{:S(2)}, u32[]{:S(2)}) collective-permute-start(f32[64,8,512]{2,1,0:T(8,128)} %get-tuple-element.21), channel_id=1, source_target_pairs={{0,28},{4,0},{8,4},{12,8},{16,12},{20,16},{24,20},{28,24},{1,29},{... | collective-permute-start | bytes 3145736 | tf_op jit(solution)/shard_map/ppermute | solution.py:380
  20.1 6.1 %collective-permute-start = (f32[8,2,4,512]{3,2,1,0:T(4,128)S(1)}, f32[8,2,4,512]{3,2,1,0:T(4,128)S(1)}, u32[]{:S(2)}, u32[]{:S(2)}) collective-permute-start(f32[8,2,4,512]{3,2,1,0:T(4,128)S(1)} %pad_maximum_fusion), channel_id=1, source_target_pairs={{0,1},{1,2},{2,3},{3,0},{4,5},{5,6},{6,7},{7,4},{8,9},{9,10},{10,1... | collective-permute-start | bytes 393224 | tf_op jit(solution)/shard_map/ppermute | solution.py:380
  21.9 5.8 %collective-permute-start.1 = (f32[8,2,4,512]{3,2,1,0:T(4,128)S(1)}, f32[8,2,4,512]{3,2,1,0:T(4,128)S(1)}, u32[]{:S(2)}, u32[]{:S(2)}) collective-permute-start(f32[8,2,4,512]{3,2,1,0:T(4,128)S(1)} %pad_maximum_fusion.1), channel_id=1, source_target_pairs={{0,3},{1,0},{2,1},{3,2},{4,7},{5,4},{6,5},{7,6},{8,11},{9,8},{10,9... | collective-permute-start | bytes 393224 | tf_op jit(solution)/shard_map/ppermute | solution.py:380
  26.2 1.5 %copy-start.3 = (f32[8,2,4,512]{3,2,1,0:T(4,128)}, f32[8,2,4,512]{3,2,1,0:T(4,128)S(1)}, u32[]{:S(2)}) copy-start(f32[8,2,4,512]{3,2,1,0:T(4,128)S(1)} %collective-permute-done.before_ref) | copy-start | bytes 393220
  27.7 0.7 copy-start.4
  43.1 1.0 copy-start.1
  43.1 1.3 copy-start.2
  58.2 4.7 %copy-start.5 = (f32[90,8,512]{2,1,0:T(8,128)S(1)}, f32[90,8,512]{2,1,0:T(8,128)}, u32[]{:S(2)}) copy-start(f32[90,8,512]{2,1,0:T(8,128)} %get-tuple-element.28) | copy-start | bytes 4423684
  58.2 56.4 %all-to-all-start.1 = ((f32[4,2,4,128,128]{4,3,2,1,0:T(8,128)}), f32[4,2,4,128,128]{4,3,2,1,0:T(8,128)}, u32[]{:S(2)}, u32[]{:S(2)}) async-start(f32[4,2,4,128,128]{4,3,2,1,0:T(8,128)} %get-tuple-element.31), calls=%async_computation.1 | async-start | bytes 4194304 | tf_op jit(solution)/shard_map/all_to_all | solution.py:469
  62.8 36.1 %collective-permute-start.6 = (f32[90,8,512]{2,1,0:T(8,128)}, f32[90,8,512]{2,1,0:T(8,128)S(1)}, u32[]{:S(2)}, u32[]{:S(2)}) collective-permute-start(f32[90,8,512]{2,1,0:T(8,128)} %get-tuple-element.27), channel_id=1, source_target_pairs={{0,4},{4,8},{8,12},{12,16},{16,20},{20,24},{24,28},{28,0},{1,5},{5... | collective-permute-start | bytes 4423688 | tf_op jit(solution)/shard_map/ppermute | solution.py:380
  62.8 36.3 %collective-permute-start.7 = (f32[90,8,512]{2,1,0:T(8,128)S(1)}, f32[90,8,512]{2,1,0:T(8,128)}, u32[]{:S(2)}, u32[]{:S(2)}) collective-permute-start(f32[90,8,512]{2,1,0:T(8,128)S(1)} %copy-done.5), channel_id=1, source_target_pairs={{0,28},{4,0},{8,4},{12,8},{16,12},{20,16},{24,20},{28,24},{1,29},{... | collective-permute-start | bytes 4423688 | tf_op jit(solution)/shard_map/ppermute | solution.py:380
  66.4 55.2 %collective-permute-start.4 = (f32[54,8,512]{2,1,0:T(8,128)}, f32[54,8,512]{2,1,0:T(8,128)}, u32[]{:S(2)}, u32[]{:S(2)}) collective-permute-start(f32[54,8,512]{2,1,0:T(8,128)} %get-tuple-element.25), channel_id=1, source_target_pairs={{0,4},{4,8},{8,12},{12,16},{16,20},{20,24},{24,28},{28,0},{1,5},{5... | collective-permute-start | bytes 2654216 | tf_op jit(solution)/shard_map/ppermute | solution.py:380
  66.4 55.2 %collective-permute-start.5 = (f32[54,8,512]{2,1,0:T(8,128)}, f32[54,8,512]{2,1,0:T(8,128)}, u32[]{:S(2)}, u32[]{:S(2)}) collective-permute-start(f32[54,8,512]{2,1,0:T(8,128)} %get-tuple-element.26), channel_id=1, source_target_pairs={{0,28},{4,0},{8,4},{12,8},{16,12},{20,16},{24,20},{28,24},{1,29},{... | collective-permute-start | bytes 2654216 | tf_op jit(solution)/shard_map/ppermute | solution.py:380
  98.9 1.1 copy-start

commit v5 on v4

--- a/solution.py
+++ b/solution.py
@@ -59,7 +59,16 @@
     return push + turned
 
 
-def pack_kernel(rho_ref, mz_ref, bx_ref, up_ref, down_ref):
+def pack_kernel(rho_ref, mz_ref, bx_ref, rho_a, mom_a, mag_a, pot_a, rho_z, mom_z, mag_z, pot_z, up_ref, down_ref, first_ref, last_ref):
+    for ref, rho, mom, mag, pot, skip in (
+        (first_ref, rho_a, mom_a, mag_a, pot_a, 0), (last_ref, rho_z, mom_z, mag_z, pot_z, pot_z.shape[0] - 2),
+    ):
+        for j in range(2):
+            ref[0, j] = rho[0, j]
+            for c in range(3):
+                ref[1 + c, j] = mom[c, 0, j]
+                ref[4 + c, j] = mag[c, 0, j]
+            ref[7, j] = jnp.broadcast_to(pot[skip + j : skip + j + 1], ref.shape[2:])
     half = rho_ref.shape[1]
 
     def body(p, _):
@@ -75,30 +84,76 @@
 
 
 def state_kernel(
-    ev_ref, at_ref, rho_ref, mom_ref, mag_ref, pot_ref, before_ref, after_ref,
-    u_ref, sb_out, sa_out, up_0, down_0, up_1, down_1, sb_ref, sa_ref, *, depth,
+    ev_ref, at_ref, rho_ref, mom_ref, mag_ref, pot_ref, before_ref, after_ref, rho_l, mom_l, mag_l, pot_l,
+    rho_h, mom_h, mag_h, pot_h, u_out, edge_out, sb_out, sa_out, *rest, depth, counts,
 ):
-    half, ny = rho_ref.shape[1], rho_ref.shape[3]
+    ups, downs, (s_ref, sb_ref, sa_ref) = rest[: len(rest) // 2 - 1], rest[len(rest) // 2 - 1 : -3], rest[-3:]
+    half, ny = s_ref.shape[1] - 4, s_ref.shape[3]
+    step_id = pl.program_id(0)
+
+    @pl.when(step_id == 0)
+    def _():
+        deposit(ev_ref, at_ref, s_ref, sb_ref, sa_ref, depth)
+        pieces = lambda rho, mom, mag, pot, j: (
+            [rho[0, j]] + [mom[c, 0, j] for c in range(3)] + [mag[c, 0, j] for c in range(3)]
+            + [jnp.broadcast_to(pot, (4, ny))]
+        )
+        for j in range(2):
+            low = pieces(rho_l, mom_l, mag_l, pot_l[0, 6 + j : 7 + j], j)
+            high = pieces(rho_h, mom_h, mag_h, pot_h[0, j : j + 1], j)
+            for f in range(8):
+                left = jnp.concatenate([before_ref[f, j], low[f]], axis=0)
+                right = jnp.concatenate([high[f], after_ref[f, j]], axis=0)
+                edge_out[f, j] = left + s_ref[f, j] if f < 4 else left
+                edge_out[f, 2 + j] = right + s_ref[f, half + 2 + j] if f < 4 else right
+
+    start = step_id * 8
+    sub = lax.broadcasted_iota(jnp.int32, (8, ny), 0)
+    begin = 0
+    for up_ref, down_ref, count in zip(ups, downs, counts):
+
+        @pl.when((step_id >= begin) & (step_id < begin + count))
+        def _(up_ref=up_ref, down_ref=down_ref, begin=begin):
+            k = step_id - begin
+
+            def messages(g, _):
+                lasts = [jnp.zeros((8, ny), jnp.float32) for _ in range(2)]
+                for j in range(4):
+                    r = 4 * g + j
+                    q = start + r + 2
+                    sb_out[r] = sb_ref[q]
+                    sa_out[r] = sa_ref[q]
+                    u = [pair(rho_ref, r) + s_ref[0, q]]
+                    u += [pair(mom_ref, c, r) + s_ref[1 + c, q] for c in range(3)]
+                    u += [pair(mag_ref, c, r) for c in range(3)]
+                    for f in range(7):
+                        u_out[f, r] = u[f]
+                    rows = [jnp.broadcast_to(pot_ref[h, pl.ds(r, 1), :], (4, ny)) for h in range(2)]
+                    u_out[7, r] = jnp.concatenate(rows, axis=0)
+                    near = [u[1], u[2], u[5], u[6]]
+                    up_ref[0, r] = gather_planes(near, 3)
+                    down_ref[0, r] = gather_planes(near, 0)
+                    f = fluxes(*shared(u[0], u[1:4], u[4:7]), u[1:4], u[4:7], 2)
+                    up_ref[0, 8 + r] = gather_planes(f[:4], 2)
+                    down_ref[0, 8 + r] = gather_planes(f[:4], 1)
+                    for i, plane in enumerate((2, 1)):
+                        for h in range(2):
+                            moved = turn(f[4], 2 * j + h - 4 * h - plane, 0)
+                            lasts[i] = jnp.where(sub == 2 * j + h, moved, lasts[i])
+                up_ref[0, 16 + g] = lasts[0]
+                down_ref[0, 16 + g] = lasts[1]
+                return 0
+
+            lax.fori_loop(0, 2, messages, 0)
+
+        begin += count
+
+
+def deposit(ev_ref, at_ref, s_ref, sb_ref, sa_ref, depth):
+    half, ny = s_ref.shape[1] - 4, s_ref.shape[3]
     rows, events = 2 * half, ev_ref.shape[0] // 4
     row_start, plane_start = at_ref[0], at_ref[1]
-
-    def raw(f, h, p):
-        if f == 0:
-            return rho_ref[h, p]
-        if f == 7:
-            return jnp.broadcast_to(pot_ref[pl.ds(h * half + p, 1), :], (4, ny))
-        return mom_ref[f - 1, h, p] if f < 4 else mag_ref[f - 4, h, p]
-
-    def fill(p, _):
-        for f in range(8):
-            u_ref[f, p + 2] = jnp.concatenate([raw(f, 0, p), raw(f, 1, p)], axis=0)
-        return 0
-
-    lax.fori_loop(0, half, fill, 0)
-    for f in range(8):
-        for j in range(2):
-            u_ref[f, j] = jnp.concatenate([before_ref[f, j], raw(f, 0, half - 2 + j)], axis=0)
-            u_ref[f, half + 2 + j] = jnp.concatenate([raw(f, 1, j), after_ref[f, j]], axis=0)
+    s_ref[...] = jnp.zeros_like(s_ref)
     sb_ref[...] = jnp.zeros_like(sb_ref)
     sa_ref[...] = jnp.zeros_like(sa_ref)
 
@@ -143,11 +198,11 @@
                         flat = dx * dx + dy2
                         size = lambda d: jnp.maximum(1.0 - (flat + d * d) * (1.0 / (RADIUS * RADIUS)), 0.0) * weight
                         w = size(dz)
-                        u_ref[0, q, :, lanes] += w
+                        s_ref[0, q, :, lanes] += w
                         w = w * IMPULSE
-                        u_ref[1, q, :, lanes] += w * dx
-                        u_ref[2, q, :, lanes] += w * dy
-                        u_ref[3, q, :, lanes] += w * dz
+                        s_ref[1, q, :, lanes] += w * dx
+                        s_ref[2, q, :, lanes] += w * dy
+                        s_ref[3, q, :, lanes] += w * dz
                         sb_ref[q, :, lanes] += size(dzb) * share(dzb)
                         sa_ref[q, :, lanes] += size(dza) * share(dza)
                         return 0
@@ -160,36 +215,6 @@
         return 0
 
     lax.fori_loop(0, events, event, 0)
-
-    def group(up_ref, down_ref, first, count):
-        def messages(g, _):
-            sub = lax.broadcasted_iota(jnp.int32, (8, ny), 0)
-            lasts = [jnp.zeros((8, ny), jnp.float32) for _ in range(2)]
-            for j in range(4):
-                r = 4 * g + j
-                p = r + first
-                sb_out[p] = sb_ref[p + 2]
-                sa_out[p] = sa_ref[p + 2]
-                u = [u_ref[f, p + 2] for f in range(7)]
-                near = [u[1], u[2], u[5], u[6]]
-                up_ref[r] = gather_planes(near, 3)
-                down_ref[r] = gather_planes(near, 0)
-                f = fluxes(*shared(u[0], u[1:4], u[4:7]), u[1:4], u[4:7], 2)
-                up_ref[count + r] = gather_planes(f[:4], 2)
-                down_ref[count + r] = gather_planes(f[:4], 1)
-                for i, plane in enumerate((2, 1)):
-                    for h in range(2):
-                        moved = turn(f[4], 2 * j + h - 4 * h - plane, 0)
-                        lasts[i] = jnp.where(sub == 2 * j + h, moved, lasts[i])
-            up_ref[2 * count + g] = lasts[0]
-            down_ref[2 * count + g] = lasts[1]
-            return 0
-
-        lax.fori_loop(0, count // 4, messages, 0)
-
-    split = up_0.shape[0] * 4 // 9
-    group(up_0, down_0, 0, split)
-    group(up_1, down_1, split, half - split)
 
 
 def ends(below, above, c):
@@ -214,7 +239,26 @@
     return out + FAR * (jnp.where(slot <= 1, turn(f, -2, 0), beyond) - jnp.where(slot >= 2, turn(f, 2, 0), beyond))
 
 
-def density_kernel(u_ref, below_ref, above_ref, sb_ref, sa_ref, order_ref, high_ref, low_ref, out_ref, wave_ref, d_ref):
+def fetch(u_hbm, edge_hbm, u_ref, sem, first):
+    fields, total = u_ref.shape[:2]
+    half = u_hbm.shape[1]
+    low, high = max(first - 2, 0), min(first + total - 2, half)
+    copies = [pltpu.make_async_copy(u_hbm.at[:fields, low:high], u_ref.at[:, low - first + 2 : high - first + 2], sem.at[0])]
+    if first == 0:
+        copies.append(pltpu.make_async_copy(edge_hbm.at[:fields, 0:2], u_ref.at[:, 0:2], sem.at[1]))
+    if first + total - 4 == half:
+        copies.append(pltpu.make_async_copy(edge_hbm.at[:fields, 2:4], u_ref.at[:, total - 2 : total], sem.at[2]))
+    for copy in copies:
+        copy.start()
+    for copy in copies:
+        copy.wait()
+
+
+def density_kernel(
+    at_ref, u_hbm, edge_hbm, below_ref, above_ref, sb_ref, sa_ref, order_ref, high_ref, low_ref, out_ref, *rest,
+):
+    *waves, d_ref, w_ref, u_ref, sem = rest
+    fetch(u_hbm, edge_hbm, u_ref, sem, 0)
     half = below_ref.shape[0]
     rows = 2 * half
 
@@ -242,10 +286,19 @@
     for part in range(2):
         c_high, c_low = high_ref[part], low_ref[part]
         wave = dot(high, c_high) + dot(high, c_low) + dot(low, c_high)
-        peers, band = wave_ref.shape[0], wave_ref.shape[4]
-        for j in range(peers):
+        if len(waves) == 1:
+            peers, band = waves[0].shape[0], waves[0].shape[4]
+            for j in range(peers):
+                for z in range(4):
+                    waves[0][j, part, z] = wave[z * rows : (z + 1) * rows, j * band : (j + 1) * band]
+            continue
+        w_ref[...] = wave
+        me = at_ref[0] // rows
+        for s, ref in enumerate(waves):
+            peer = jnp.where(me + s >= len(waves), me + s - len(waves), me + s)
+            lanes = pl.ds(pl.multiple_of(peer * 128, 128) if ref.shape[3] == 128 else peer * ref.shape[3], ref.shape[3])
             for z in range(4):
-                wave_ref[j, part, z] = wave[z * rows : (z + 1) * rows, j * band : (j + 1) * band]
+                ref[part, z] = w_ref[z * rows : (z + 1) * rows, lanes]
 
 
 def last_plane(below, above, j):
@@ -256,9 +309,7 @@
     return jnp.where(sub == 7, turn(above, 6 - 2 * j, 0), out)
 
 
-def main_kernel(
-    u_hbm, ba_ref, aa_ref, sb_ref, sa_ref, bn_ref, an_ref, bf_ref, af_ref, bl_ref, al_ref, *rest, first,
-):
+def main_kernel(u_hbm, edge_hbm, ba_ref, aa_ref, sb_ref, sa_ref, from_below, from_above, *rest, first):
     mom_ref, mag_ref, u_ref, f_ref, sem = rest[-5:]
     chunk, total = ba_ref.shape[0], u_ref.shape[1]
     start = pl.program_id(0) * chunk
@@ -266,9 +317,7 @@
 
     @pl.when(pl.program_id(0) == 0)
     def _():
-        copy = pltpu.make_async_copy(u_hbm.at[:, pl.ds(first, total)], u_ref, sem)
-        copy.start()
-        copy.wait()
+        fetch(u_hbm, edge_hbm, u_ref, sem, first)
 
         def fx(q, _):
             u = [u_ref[f, q] for f in range(7)]
@@ -286,12 +335,12 @@
         fy = fluxes(v, pressure, u[1:4], u[4:7], 1)
         fz = fluxes(v, pressure, u[1:4], u[4:7], 2)
         ba, aa = ba_ref[r] + sb_ref[r], aa_ref[r] + sa_ref[r]
-        bn, an, bf, af = bn_ref[r], an_ref[r], bf_ref[r], af_ref[r]
+        bn, an, bf, af = from_below[0, r], from_above[0, r], from_below[0, 8 + r], from_above[0, 8 + r]
         hm = [ends(bn, an, 0), ends(bn, an, 1), ends(ba, aa, 1)]
         hb = [ends(ba, aa, 3), ends(bn, an, 2), ends(bn, an, 3)]
         fh = fluxes(*shared(ends(ba, aa, 0), hm, hb), hm, hb, 2)
         halo = hm + hb
-        far = [ends(bf, af, c) for c in range(4)] + [last_plane(bl_ref[g], al_ref[g], j), None]
+        far = [ends(bf, af, c) for c in range(4)] + [last_plane(from_below[0, 16 + g], from_above[0, 16 + g], j), None]
         for c in range(6):
             field = u[c + 1]
             new = field * (1.0 - 6.0 * DIFFUSION)
@@ -325,16 +374,23 @@
     lax.fori_loop(0, chunk // 4, body, 0)
 
 
-def modes_kernel(at_ref, w_ref, ch_ref, cl_ref, sh_ref, sl_ref, out_ref, *, turned):
+def modes_kernel(at_ref, *rest, turned):
+    *pieces, ch_ref, cl_ref, sh_ref, sl_ref, out_ref, x_ref = rest
     dot = functools.partial(jnp.dot, preferred_element_type=jnp.float32)
     planes, band, nx = out_ref.shape[1:]
 
     def split(part):
         if turned:
-            x = jnp.concatenate([w_ref[part, z] for z in range(planes)], axis=0)
+            x = jnp.concatenate([pieces[0][part, z] for z in range(planes)], axis=0)
         else:
-            column = lambda z: jnp.concatenate([w_ref[j, part, z] for j in range(w_ref.shape[0])], axis=0)
-            x = jnp.concatenate([column(z).T for z in range(planes)], axis=0)
+            width = nx // len(pieces)
+            me = at_ref[0] // width
+            for s, ref in enumerate(pieces):
+                peer = jnp.where(me - s < 0, me - s + len(pieces), me - s)
+                lanes = pl.ds(pl.multiple_of(peer * 128, 128) if width == 128 else peer * width, width)
+                for z in range(planes):
+                    x_ref[z * band : (z + 1) * band, lanes] = ref[part, z].T
+            x = x_ref[...]
         high = x.astype(jnp.bfloat16)
         return high, (x - high.astype(jnp.float32)).astype(jnp.bfloat16)
 
@@ -394,8 +450,8 @@
     params = pltpu.CompilerParams(vmem_limit_bytes=VMEM)
     message = shape((2, half, planes, ny), f32)
     tile = shape((half, 8, ny), f32)
-    n0 = max(4, half * 5 // 32 * 4)
-    counts = (n0, half - n0)
+    steps = half // 8
+    counts = (steps // 4, (steps - steps // 4) // 2, steps - steps // 4 - (steps - steps // 4) // 2) if steps >= 4 else (steps,)
 
     slots_here = sn_cells.shape[0]
     mine = jnp.concatenate([sn_cells, sn_counts[:, None]], axis=1).reshape(1, 1, 4 * slots_here)
@@ -410,103 +466,129 @@
     mom = momentum.reshape(3, 2, half, planes, ny)
     mag = magnetic.reshape(3, 2, half, planes, ny)
 
-    def edge(s):
-        potential = jnp.broadcast_to(arm_potential[s][None, :, None, :], (1, 2, planes, ny))
-        return jnp.concatenate([density[None, s], momentum[:, s], magnetic[:, s], potential], axis=0)
-
-    before = shift(edge(slice(rows - 2, rows)), "xy", 1)
-    after = shift(edge(slice(0, 2)), "xy", -1)
-
+    pot = arm_potential.reshape(2, half, ny)
     one = lambda f: pl.BlockSpec((1, 2, half, planes, ny), lambda i, f=f: (f, 0, 0, 0, 0))
     full = lambda s: pl.BlockSpec(s, lambda i: (0,) * len(s))
-    up, down = pl.pallas_call(
+    edges = shape((8, 2, planes, ny), f32)
+    up, down, first_rows, last_rows = pl.pallas_call(
         pack_kernel,
         grid=(1,),
-        in_specs=[full(message.shape), one(2), one(0)],
-        out_specs=[full(tile.shape)] * 2,
-        out_shape=[tile] * 2,
+        in_specs=[full(message.shape), one(2), one(0)] + [
+            spec
+            for h, k in ((0, 0), (1, half // 2 - 1))
+            for spec in (
+                pl.BlockSpec((1, 2, planes, ny), lambda i, h=h, k=k: (h, k, 0, 0)),
+                pl.BlockSpec((3, 1, 2, planes, ny), lambda i, h=h, k=k: (0, h, k, 0, 0)),
+                pl.BlockSpec((3, 1, 2, planes, ny), lambda i, h=h, k=k: (0, h, k, 0, 0)),
+                pl.BlockSpec((8, ny), lambda i, h=h: (h * (rows // 8 - 1), 0)),
+            )
+        ],
+        out_specs=[full(tile.shape)] * 2 + [full(edges.shape)] * 2,
+        out_shape=[tile] * 2 + [edges] * 2,
         compiler_params=params,
         cost_estimate=cost(*PACK_COST),
         name="pack",
-    )(rho, mom, mag)
+    )(rho, mom, mag, *[rho, mom, mag, arm_potential] * 2)
+    before, after = shift(last_rows, "xy", 1), shift(first_rows, "xy", -1)
     below_a, above_a = shift(up, "gz", 1), shift(down, "gz", -1)
 
-    parcels = [shape((9 * n // 4, 8, ny), f32) for n in counts]
+    parcels = [shape((n, 18, 8, ny), f32) for n in counts]
     side = pltpu.VMEM((half + 4, 8, ny), f32)
-    state, sb, sa, up_0, down_0, up_1, down_1 = pl.pallas_call(
-        functools.partial(state_kernel, depth=planes * layers),
-        in_specs=[smem, smem] + [whole] * 6,
-        out_specs=[whole] * 7,
-        out_shape=[shape((8, half + 4, 8, ny), f32), tile, tile, parcels[0], parcels[0], parcels[1], parcels[1]],
-        scratch_shapes=[side, side],
+    begins = [sum(counts[:i]) for i in range(len(counts))]
+    parcel_specs = [
+        pl.BlockSpec((1, 18, 8, ny), lambda i, b=b, n=n: (jnp.clip(i - b, 0, n - 1), 0, 0, 0)) for b, n in zip(begins, counts)
+    ]
+    eight = pl.BlockSpec((8, 8, ny), lambda i: (i, 0, 0))
+    middle = [
+        spec
+        for h, k in ((0, steps - 1), (1, 0))
+        for spec in (
+            pl.BlockSpec((1, 2, planes, ny), lambda i, h=h, k=k: (h, k * 4 + 3 * (1 - h), 0, 0)),
+            pl.BlockSpec((3, 1, 2, planes, ny), lambda i, h=h, k=k: (0, h, k * 4 + 3 * (1 - h), 0, 0)),
+            pl.BlockSpec((3, 1, 2, planes, ny), lambda i, h=h, k=k: (0, h, k * 4 + 3 * (1 - h), 0, 0)),
+            pl.BlockSpec((1, 8, ny), lambda i, h=h, k=k: (h, k, 0)),
+        )
+    ]
+    rows_of = lambda n: pl.BlockSpec((n, 2, 8, planes, ny), lambda i: (0, 0, i, 0, 0))
+    state, edge, sb, sa, *messages = pl.pallas_call(
+        functools.partial(state_kernel, depth=planes * layers, counts=counts),
+        grid=(steps,),
+        in_specs=[
+            smem, smem, pl.BlockSpec((2, 8, planes, ny), lambda i: (0, i, 0, 0)), rows_of(3), rows_of(3),
+            pl.BlockSpec((2, 8, ny), lambda i: (0, i, 0)), full(edges.shape), full(edges.shape),
+        ] + middle,
+        out_specs=[pl.BlockSpec((8, 8, 8, ny), lambda i: (0, i, 0, 0)), full((8, 4, 8, ny)), eight, eight] + parcel_specs * 2,
+        out_shape=[shape((8, half, 8, ny), f32), shape((8, 4, 8, ny), f32), tile, tile] + parcels * 2,
+        scratch_shapes=[pltpu.VMEM((4, half + 4, 8, ny), f32), side, side],
         compiler_params=params,
         cost_estimate=cost(*STATE_COST),
         name="state",
-    )(events, at, rho, mom, mag, arm_potential, before, after)
-    parcels_below = [shift(up_0, "gz", 1)]
-    parcels_above = [shift(down_0, "gz", -1)]
-    parcels_below.append(shift(up_1, "gz", 1))
-    parcels_above.append(shift(down_1, "gz", -1))
+    )(events, at, rho, mom, mag, pot, before, after, *[rho, mom, mag, pot] * 2)
+    parcels_below, parcels_above = [], []
+    for i in range(len(counts)):
+        parcels_below.append(shift(messages[i], "gz", 1))
+        parcels_above.append(shift(messages[len(counts) + i], "gz", -1))
 
     cos_high, cos_low, sin_high, sin_low = tables(ny)
     band = ny // across
-    new_density, wave = pl.pallas_call(
+    turned = band % 128 != 0 or rows % 128 != 0
+    waves = [shape((across, 2, planes, rows, band), f32)] if turned else [shape((2, planes, rows, band), f32)] * across
+    hbm = pl.BlockSpec(memory_space=pl.ANY)
+    copies = pltpu.SemaphoreType.DMA((3,))
+    new_density, *waves = pl.pallas_call(
         density_kernel,
-        grid=(1,),
-        in_specs=[
-            full((4, half + 4, 8, ny)), full(tile.shape), full(tile.shape), full(tile.shape), full(tile.shape),
-            full((8 * half, 8 * half)), full((2, ny, ny)), full((2, ny, ny)),
+        in_specs=[smem, hbm, hbm] + [whole] * 7,
+        out_specs=[whole] * (1 + len(waves)),
+        out_shape=[message, *waves],
+        scratch_shapes=[
+            pltpu.VMEM((8 * half, ny), f32), pltpu.VMEM((8 * half, ny), f32), pltpu.VMEM((4, half + 4, 8, ny), f32), copies,
         ],
-        out_specs=[full(message.shape), full((across, 2, planes, rows, band))],
-        out_shape=[message, shape((across, 2, planes, rows, band), f32)],
-        scratch_shapes=[pltpu.VMEM((8 * half, ny), f32)],
         compiler_params=params,
         cost_estimate=cost(*DENSITY_COST),
         name="density",
     )(
-        state, below_a, above_a, sb, sa, row_order(half), np.stack([cos_high, -sin_high]), np.stack([cos_low, -sin_low]),
+        at, state, edge, below_a, above_a, sb, sa, row_order(half),
+        np.stack([cos_high, -sin_high]), np.stack([cos_low, -sin_low]),
     )
-    portion = lax.all_to_all(wave, "xy", split_axis=0, concat_axis=0, tiled=True)
-
-    turned = band % 128 != 0
+
     if turned:
-        portion = portion.transpose(1, 2, 4, 0, 3).reshape(2, planes, band, NX)
+        portion = lax.all_to_all(waves[0], "xy", split_axis=0, concat_axis=0, tiled=True)
+        pieces = [portion.transpose(1, 2, 4, 0, 3).reshape(2, planes, band, NX)]
+    else:
+        pieces = waves[:1] + [shift(waves[s], "xy", s) for s in range(1, across)]
     modes = pl.pallas_call(
         functools.partial(modes_kernel, turned=turned),
-        in_specs=[smem] + [whole] * 5,
+        in_specs=[smem] + [whole] * (len(pieces) + 4),
         out_specs=whole,
         out_shape=shape((2, planes, band, NX), f32),
+        scratch_shapes=[pltpu.VMEM((planes * band, NX), f32)],
         compiler_params=params,
         cost_estimate=cost(*MODES_COST),
         name="modes",
-    )(at, portion, *tables(NX))
+    )(at, *pieces, *tables(NX))
     results = [shape((3, 2, half, planes, ny), f32)] * 2
     new = []
     for i, n in enumerate(counts):
-        first = i * n0
-        chunk = math.gcd(math.gcd(n0, half - n0), 8)
-        here = pl.BlockSpec((chunk, 8, ny), lambda k, o=first // chunk: (o + k, 0, 0))
-        near = pl.BlockSpec((chunk, 8, ny), lambda k: (k, 0, 0))
-        far = pl.BlockSpec((chunk, 8, ny), lambda k, o=n // chunk: (o + k, 0, 0))
-        last = pl.BlockSpec((chunk // 4, 8, ny), lambda k, o=8 * n // chunk: (o + k, 0, 0))
-        three = pl.BlockSpec((3, 2, chunk, planes, ny), lambda k, o=first // chunk: (0, 0, o + k, 0, 0))
+        chunk, first = 8, begins[i] * 8
+        here = pl.BlockSpec((chunk, 8, ny), lambda k, o=begins[i]: (o + k, 0, 0))
+        parcel = pl.BlockSpec((1, 18, 8, ny), lambda k: (k, 0, 0, 0))
+        three = pl.BlockSpec((3, 2, chunk, planes, ny), lambda k, o=begins[i]: (0, 0, o + k, 0, 0))
         below, above = parcels_below[i], parcels_above[i]
-        extra = [*new, modes] if new else []
+        extra = [*new] + [modes] * (i > 0 and i == len(counts) - 1)
         new = pl.pallas_call(
             functools.partial(main_kernel, first=first),
-            grid=(n // chunk,),
-            in_specs=[pl.BlockSpec(memory_space=pl.ANY)] + [here] * 4 + [near] * 2 + [far] * 2 + [last] * 2
-            + [pl.BlockSpec(memory_space=pl.ANY)] * len(extra),
+            grid=(n,),
+            in_specs=[hbm, hbm] + [here] * 4 + [parcel] * 2 + [hbm] * len(extra),
             out_specs=[three, three],
             out_shape=results,
             scratch_shapes=[
-                pltpu.VMEM((8, n + 4, 8, ny), f32), pltpu.VMEM((5, n + 4, 8, ny), f32), pltpu.SemaphoreType.DMA,
+                pltpu.VMEM((8, n * 8 + 4, 8, ny), f32), pltpu.VMEM((5, n * 8 + 4, 8, ny), f32), copies,
             ],
-            input_output_aliases={11: 0, 12: 1} if new else {},
+            input_output_aliases={8: 0, 9: 1} if new else {},
             compiler_params=pltpu.CompilerParams(vmem_limit_bytes=62 * 1024 * 1024),
             cost_estimate=cost(*MAIN_COST),
             name=f"main{i}",
-        )(state, below_a, above_a, sb, sa, below, above, below, above, below, above, *extra)
+        )(state, edge, below_a, above_a, sb, sa, below, above, *extra)
     new_mom, new_mag = new
 
     return (

time: 132 us -> 133 us (level)
  Pallas kernels: 64.3 us -> 69.5 us
  starting transfers between devices: 25.6 us -> 22 us
  waiting for transfers between devices: 32.4 us -> 35.2 us
  local copies, waits for them, and re-layouts: 6.59 us -> 3.99 us
    all_to_all x1, waiting for transfers between devices: 0.01 us -> 17.2 us  [on_device(): lax.all_to_all(jnp.broadcast_to(mine, (devices, 1, mine.shape[2])), ('gz'...]
    ppermute x8 -> x13, waiting for transfers between devices: 32.4 us -> 18.1 us  [shift(): return lax.ppermute(block, axis, [(i, (i + step) % n) for i in range(n)])]
    pallas_call x4 -> x5, Pallas kernels: 53.2 us -> 57.8 us  [the longest x3 27.7 us: on_device(): pl.pallas_call(functools.partial(main_kernel, first=first), grid=(n,), in...]
    all_to_all x1 -> x0, starting transfers between devices: 4.58 us -> none  [on_device(): lax.all_to_all(wave, 'xy', split_axis=0, concat_axis=0, tiled=True)]
    ppermute x8 -> x13, starting transfers between devices: 13.7 us -> 17.5 us  [shift(): return lax.ppermute(block, axis, [(i, (i + step) % n) for i in range(n)])]
    all_to_all x1, starting transfers between devices: 7.3 us -> 4.5 us  [on_device(): lax.all_to_all(jnp.broadcast_to(mine, (devices, 1, mine.shape[2])), ('gz'...]
    slice x2 -> x0, local copies, waits for them, and re-layouts: 1.62 us -> none  [the longest x1 0.88 us: edge(): momentum[:, s]]
    unnamed x12 -> x18, local copies, waits for them, and re-layouts: 2.86 us -> 2.74 us
  transfers between devices with their start and end apart: 10 -> 14, of which waited for: 4 -> 4; matrix products, arithmetic and copies ran while one was open for 3% -> 1% of each run, Pallas kernels for 31% -> 42%
where the time goes in v5:
time: 133 us
  Pallas kernels  69.5 us (52%)
  waiting for transfers between devices  35.2 us (26%)
  starting transfers between devices  22 us (17%)
  local copies, waits for them, and re-layouts  3.99 us (3%)
  between operations  1.42 us (1%)
    pallas_call x3, Pallas kernels, on_device(): pl.pallas_call(functools.partial(main_kernel, first=first), grid=(n,), in...  27.7 us
    ppermute x13, waiting for transfers between devices, shift(): return lax.ppermute(block, axis, [(i, (i + step) % n) for i in range(n)])  18.1 us
    ppermute x13, starting transfers between devices, shift(): return lax.ppermute(block, axis, [(i, (i + step) % n) for i in range(n)])  17.5 us
    all_to_all x1, waiting for transfers between devices, on_device(): lax.all_to_all(jnp.broadcast_to(mine, (devices, 1, mine.shape[2])), ('gz'...  17.2 us
    pallas_call x1, Pallas kernels, on_device(): pl.pallas_call(functools.partial(state_kernel, depth=planes * layers, cou...  15.2 us
    pallas_call x1, Pallas kernels, on_device(): pl.pallas_call(density_kernel, in_specs=[smem, hbm, hbm] + [whole] * 7, o...  14.9 us
    pallas_call x1, Pallas kernels, on_device(): pl.pallas_call(functools.partial(modes_kernel, turned=turned), in_specs=[...  7.32 us
    all_to_all x1, starting transfers between devices, on_device(): lax.all_to_all(jnp.broadcast_to(mine, (devices, 1, mine.shape[2])), ('gz'...  4.5 us
  transfers between devices with their start and end apart: 14, of which 4 were waited for; matrix products, arithmetic and copies ran while one was open for 1% of the time, Pallas kernels for 42%

profile of v5, /device:TPU:0, one launch (start us, length us, event | category | flops | bytes accessed | tf_op | source)
XLA Modules:
  0.0 132.7 jit_solution(17464904179736932428)
XLA Ops:
  0.6 4.3 %pack.1 = (f32[64,8,512]{2,1,0:T(8,128)}, f32[64,8,512]{2,1,0:T(8,128)}, f32[8,2,4,512]{3,2,1,0:T(4,128)}, f32[8,2,4,512]{3,2,1,0:T(4,128)}) custom-call(f32[2,64,4,512]{3,2,1,0:T(4,128)} %bitcast.27, f32[3,2,64,4,512]{4,3,2,1,0:T(4,128)} %bitcast.15, f32[3,2,64,4,512]{4,3,2,1,0:T(4,128)} %bitcast.21, f32[2,64,4,512]{3,2,1,0:T(4,128)} %bitcast.28, ...), custom_call_target="tpu_custom_call" | custom-call | flops 1000000 | bytes 100000 | tf_op jit(solution)/shard_map/pack/pallas_call | solution.py:473
  4.9 0.5 collective-permute-start.2
  5.4 4.1 %collective-permute-start.3 = (f32[64,8,512]{2,1,0:T(8,128)}, f32[64,8,512]{2,1,0:T(8,128)S(1)}, u32[]{:S(2)}, u32[]{:S(2)}) collective-permute-start(f32[64,8,512]{2,1,0:T(8,128)} %get-tuple-element.34), channel_id=1, source_target_pairs={{0,28},{4,0},{8,4},{12,8},{16,12},{20,16},{24,20},{28,24},{1,29},{... | collective-permute-start | bytes 3145736 | tf_op jit(solution)/shard_map/ppermute | solution.py:436
  10.1 0.1 add_bitcast_fusion
  10.2 0.6 broadcast_in_dim.12
  10.8 4.5 %all-to-all-start = ((s32[32,1,128]{2,1,0:T(1,128)}), s32[32,1,128]{2,1,0:T(1,128)S(1)}, u32[]{:S(2)}, u32[]{:S(2)}) async-start(s32[32,1,128]{2,1,0:T(1,128)} %broadcast_in_dim.12), calls=%async_computation | async-start | bytes 32768 | tf_op jit(solution)/shard_map/all_to_all | solution.py:459
  15.3 1.8 %collective-permute-start = (f32[8,2,4,512]{3,2,1,0:T(4,128)}, f32[8,2,4,512]{3,2,1,0:T(4,128)S(1)}, u32[]{:S(2)}, u32[]{:S(2)}) collective-permute-start(f32[8,2,4,512]{3,2,1,0:T(4,128)} %get-tuple-element.29), channel_id=1, source_target_pairs={{0,1},{1,2},{2,3},{3,0},{4,5},{5,6},{6,7},{7,4},{8,9},{9,10},{10,1... | collective-permute-start | bytes 393224 | tf_op jit(solution)/shard_map/ppermute | solution.py:436
  17.2 1.2 collective-permute-start.1
  18.3 0.6 pad_add_fusion.at_ref
  18.9 17.2 %all-to-all-done = s32[32,1,128]{2,1,0:T(1,128)S(1)} async-done(((s32[32,1,128]{2,1,0:T(1,128)}), s32[32,1,128]{2,1,0:T(1,128)S(1)}, u32[]{:S(2)}, u32[]{:S(2)}) %all-to-all-start) | async-done | bytes 16416 | tf_op jit(solution)/shard_map/all_to_all | solution.py:459
  36.1 0.6 reshape_squeeze.3.ev_ref
  36.7 0.6 copy-done.6
  37.3 0.1 copy-done.7
  37.4 15.2 %state.1 = (f32[8,64,8,512]{3,2,1,0:T(8,128)}, f32[8,4,8,512]{3,2,1,0:T(8,128)}, f32[64,8,512]{2,1,0:T(8,128)}, f32[64,8,512]{2,1,0:T(8,128)}, f32[2,18,8,512]{3...) custom-call(s32[128]{0:T(128)} %reshape_squeeze.3.ev_ref, ...), custom_call_target="tpu_custom_call" | custom-call | flops 1000000 | bytes 400000000 | tf_op jit(solution)/shard_map/state/pallas_call | solution.py:513
  52.7 0.7 collective-permute-start.6
  53.4 2.9 %collective-permute-start.7 = (f32[3,18,8,512]{3,2,1,0:T(8,128)}, f32[3,18,8,512]{3,2,1,0:T(8,128)}, u32[]{:S(2)}, u32[]{:S(2)}) collective-permute-start(f32[3,18,8,512]{3,2,1,0:T(8,128)} %get-tuple-element.41), channel_id=1, source_target_pairs={{0,28},{4,0},{8,4},{12,8},{16,12},{20,16},{24,20},{28,24},{1,29},{... | collective-permute-start | bytes 2654216 | tf_op jit(solution)/shard_map/ppermute | solution.py:436
  56.3 13.4 %collective-permute-done.8.from_below = f32[2,18,8,512]{3,2,1,0:T(8,128)S(1)} collective-permute-done((f32[2,18,8,512]{3,2,1,0:T(8,128)}, f32[2,18,8,512]{3,2,1,0:T(8,128)S(1)}, u32[]{:S(2)}, u32[]{:S(2)}) %collective-permute-start.8) | collective-permute-done | bytes 589856 | tf_op jit(solution)/shard_map/ppermute | solution.py:436
  69.7 0.5 collective-permute-start.4
  70.2 0.3 copy-done.3
  70.5 2.8 %collective-permute-start.5 = (f32[3,18,8,512]{3,2,1,0:T(8,128)}, f32[3,18,8,512]{3,2,1,0:T(8,128)}, u32[]{:S(2)}, u32[]{:S(2)}) collective-permute-start(f32[3,18,8,512]{3,2,1,0:T(8,128)} %get-tuple-element.39), channel_id=1, source_target_pairs={{0,28},{4,0},{8,4},{12,8},{16,12},{20,16},{24,20},{28,24},{1,29},{... | collective-permute-start | bytes 2654216 | tf_op jit(solution)/shard_map/ppermute | solution.py:436
  73.3 14.9 %density.1 = (f32[2,64,4,512]{3,2,1,0:T(4,128)}, f32[2,4,128,128]{3,2,1,0:T(8,128)}, f32[2,4,128,128]{3,2,1,0:T(8,128)}, f32[2,4,128,128]{3,2,1,0:T(8,128)}, f32[2,4,128,128]{3,2,1,0:T(8,128)}) custom-call(s32[3]{0:T(128)} %pad_add_fusion.at_ref, f32[8,64,8,512]{3,2,1,0:T(8,128)} %get-tuple-element.31.u_hbm, f32[8,4,8,512]{3,2,1,0:T(8,128)} %get-tuple-element.32.edge_hbm, ...), custom_call_target="tpu_custom_call" | custom-call | flops 1000000 | bytes 100000 | tf_op jit(solution)/shard_map/density/pallas_call | solution.py:538
  88.2 1.1 collective-permute-done.9.from_above
  89.3 0.2 collective-permute-start.10
  89.6 1.4 %collective-permute-start.11 = (f32[2,4,128,128]{3,2,1,0:T(8,128)}, f32[2,4,128,128]{3,2,1,0:T(8,128)S(1)}, u32[]{:S(2)}, u32[]{:S(2)}) collective-permute-start(f32[2,4,128,128]{3,2,1,0:T(8,128)} %get-tuple-element.50), channel_id=1, source_target_pairs={{0,2},{1,3},{2,0},{3,1},{4,6},{5,7},{6,4},{7,5},{8,10},{9,11},{10,... | collective-permute-start | bytes 1572872 | tf_op jit(solution)/shard_map/ppermute | solution.py:436
  91.0 1.4 %collective-permute-start.12 = (f32[2,4,128,128]{3,2,1,0:T(8,128)}, f32[2,4,128,128]{3,2,1,0:T(8,128)}, u32[]{:S(2)}, u32[]{:S(2)}) collective-permute-start(f32[2,4,128,128]{3,2,1,0:T(8,128)} %get-tuple-element.51), channel_id=1, source_target_pairs={{0,3},{1,0},{2,1},{3,2},{4,7},{5,4},{6,5},{7,6},{8,11},{9,8},{10,9... | collective-permute-start | bytes 1572872 | tf_op jit(solution)/shard_map/ppermute | solution.py:436
  92.3 7.7 %main0.1 = (f32[3,2,64,4,512]{4,3,2,1,0:T(4,128)}, f32[3,2,64,4,512]{4,3,2,1,0:T(4,128)}) custom-call(f32[8,64,8,512]{3,2,1,0:T(8,128)} %get-tuple-element.31.u_hbm, f32[8,4,8,512]{3,2,1,0:T(8,128)} %get-tuple-element.32.edge_hbm, f32[64,8,512]{2,1,0:T(8,128)} %copy-done, f32[64,8,512]{2,1,0:T(8,128)} %copy-done.1, f32[64,8,512]{2,1,0:T(8,128)} %get-tuple-element.35.sb_ref, ...), custom_call_target="tpu_custom_call" | custom-call | flops 1000000 | bytes 400000000 | tf_op jit(solution)/shard_map/main0/pallas_call | solution.py:578
  100.1 10.0 %main1.1 = (f32[3,2,64,4,512]{4,3,2,1,0:T(4,128)}, f32[3,2,64,4,512]{4,3,2,1,0:T(4,128)}) custom-call(f32[8,64,8,512]{3,2,1,0:T(8,128)} %get-tuple-element.31.u_hbm, f32[8,4,8,512]{3,2,1,0:T(8,128)} %get-tuple-element.32.edge_hbm, f32[64,8,512]{2,1,0:T(8,128)} %copy-done, f32[64,8,512]{2,1,0:T(8,128)} %copy-done.1, ...), custom_call_target="tpu_custom_call", output_to_operand_aliasing={{0}: (8, {}), {1}: (9, {})} | custom-call | flops 1000000 | bytes 400000000 | tf_op jit(solution)/shard_map/main1/pallas_call | solution.py:578
  110.2 3.5 %collective-permute-done.11.rest_2_ = f32[2,4,128,128]{3,2,1,0:T(8,128)S(1)} collective-permute-done((f32[2,4,128,128]{3,2,1,0:T(8,128)}, f32[2,4,128,128]{3,2,1,0:T(8,128)S(1)}, u32[]{:S(2)}, u32[]{:S(2)}) %collective-permute-start.11) | collective-permute-done | bytes 524320 | tf_op jit(solution)/shard_map/ppermute | solution.py:436
  113.7 0.8 copy-done.5
  114.5 7.3 %modes.1.rest_2_ = f32[2,4,128,512]{3,2,1,0:T(8,128)} custom-call(s32[3]{0:T(128)} %pad_add_fusion.at_ref, f32[2,4,128,128]{3,2,1,0:T(8,128)} %get-tuple-element.48.rest_0_, f32[2,4,128,128]{3,2,1,0:T(8,128)} %copy-done.4, f32[2,4,128,128]{3,2,1,0:T(8,128)} %copy-done.5, f32[2,4,128,128]{3,2,1,0:T(8,128)} %collective-permute-done.12.rest_3_, ...), custom_call_target="tpu_custom_call" | custom-call | flops 1000000 | bytes 100000 | tf_op jit(solution)/shard_map/modes/pallas_call | solution.py:559
  121.8 0.9 copy-done.2
  122.8 9.9 %main2.1 = (f32[3,2,64,4,512]{4,3,2,1,0:T(4,128)}, f32[3,2,64,4,512]{4,3,2,1,0:T(4,128)}) custom-call(f32[8,64,8,512]{3,2,1,0:T(8,128)} %get-tuple-element.31.u_hbm, f32[8,4,8,512]{3,2,1,0:T(8,128)} %get-tuple-element.32.edge_hbm, f32[64,8,512]{2,1,0:T(8,128)} %copy-done, f32[64,8,512]{2,1,0:T(8,128)} %copy-done.1, ...), custom_call_target="tpu_custom_call", output_to_operand_aliasing={{0}: (8, {}), {1}: (9, {})} | custom-call | flops 1000000 | bytes 400000000 | tf_op jit(solution)/shard_map/main2/pallas_call | solution.py:578
  (27 shorter events, 0.2 us)
Async XLA Ops:
  0.6 9.5 %copy-start.8 = (s32[1,3]{1,0:T(1,128)S(1)}, s32[1,3]{1,0:T(1,128)}, u32[]{:S(2)}) copy-start(s32[1,3]{1,0:T(1,128)} %param.17) | copy-start | bytes 40
  4.9 64.7 %collective-permute-start.2 = (f32[64,8,512]{2,1,0:T(8,128)}, f32[64,8,512]{2,1,0:T(8,128)S(1)}, u32[]{:S(2)}, u32[]{:S(2)}) collective-permute-start(f32[64,8,512]{2,1,0:T(8,128)} %get-tuple-element.33), channel_id=1, source_target_pairs={{0,4},{4,8},{8,12},{12,16},{16,20},{20,24},{24,28},{28,0},{1,5},{5... | collective-permute-start | bytes 3145736 | tf_op jit(solution)/shard_map/ppermute | solution.py:436
  5.4 64.8 %collective-permute-start.3 = (f32[64,8,512]{2,1,0:T(8,128)}, f32[64,8,512]{2,1,0:T(8,128)S(1)}, u32[]{:S(2)}, u32[]{:S(2)}) collective-permute-start(f32[64,8,512]{2,1,0:T(8,128)} %get-tuple-element.34), channel_id=1, source_target_pairs={{0,28},{4,0},{8,4},{12,8},{16,12},{20,16},{24,20},{28,24},{1,29},{... | collective-permute-start | bytes 3145736 | tf_op jit(solution)/shard_map/ppermute | solution.py:436
  10.8 25.2 %all-to-all-start = ((s32[32,1,128]{2,1,0:T(1,128)}), s32[32,1,128]{2,1,0:T(1,128)S(1)}, u32[]{:S(2)}, u32[]{:S(2)}) async-start(s32[32,1,128]{2,1,0:T(1,128)} %broadcast_in_dim.12), calls=%async_computation | async-start | bytes 32768 | tf_op jit(solution)/shard_map/all_to_all | solution.py:459
  15.3 21.3 %collective-permute-start = (f32[8,2,4,512]{3,2,1,0:T(4,128)}, f32[8,2,4,512]{3,2,1,0:T(4,128)S(1)}, u32[]{:S(2)}, u32[]{:S(2)}) collective-permute-start(f32[8,2,4,512]{3,2,1,0:T(4,128)} %get-tuple-element.29), channel_id=1, source_target_pairs={{0,1},{1,2},{2,3},{3,0},{4,5},{5,6},{6,7},{7,4},{8,9},{9,10},{10,1... | collective-permute-start | bytes 393224 | tf_op jit(solution)/shard_map/ppermute | solution.py:436
  17.2 19.5 %collective-permute-start.1 = (f32[8,2,4,512]{3,2,1,0:T(4,128)}, f32[8,2,4,512]{3,2,1,0:T(4,128)S(1)}, u32[]{:S(2)}, u32[]{:S(2)}) collective-permute-start(f32[8,2,4,512]{3,2,1,0:T(4,128)} %get-tuple-element.30), channel_id=1, source_target_pairs={{0,3},{1,0},{2,1},{3,2},{4,7},{5,4},{6,5},{7,6},{8,11},{9,8},{10,9... | collective-permute-start | bytes 393224 | tf_op jit(solution)/shard_map/ppermute | solution.py:436
  36.7 0.6 copy-start.6
  36.7 0.7 copy-start.7
  52.6 17.0 %collective-permute-start.8 = (f32[2,18,8,512]{3,2,1,0:T(8,128)}, f32[2,18,8,512]{3,2,1,0:T(8,128)S(1)}, u32[]{:S(2)}, u32[]{:S(2)}) collective-permute-start(f32[2,18,8,512]{3,2,1,0:T(8,128)} %get-tuple-element.42), channel_id=1, source_target_pairs={{0,4},{4,8},{8,12},{12,16},{16,20},{20,24},{24,28},{28,0},{1,5},{5... | collective-permute-start | bytes 1769480 | tf_op jit(solution)/shard_map/ppermute | solution.py:436
  52.7 36.9 %collective-permute-start.6 = (f32[3,18,8,512]{3,2,1,0:T(8,128)}, f32[3,18,8,512]{3,2,1,0:T(8,128)}, u32[]{:S(2)}, u32[]{:S(2)}) collective-permute-start(f32[3,18,8,512]{3,2,1,0:T(8,128)} %get-tuple-element.40), channel_id=1, source_target_pairs={{0,4},{4,8},{8,12},{12,16},{16,20},{20,24},{24,28},{28,0},{1,5},{5... | collective-permute-start | bytes 2654216 | tf_op jit(solution)/shard_map/ppermute | solution.py:436
  53.4 37.6 %collective-permute-start.7 = (f32[3,18,8,512]{3,2,1,0:T(8,128)}, f32[3,18,8,512]{3,2,1,0:T(8,128)}, u32[]{:S(2)}, u32[]{:S(2)}) collective-permute-start(f32[3,18,8,512]{3,2,1,0:T(8,128)} %get-tuple-element.41), channel_id=1, source_target_pairs={{0,28},{4,0},{8,4},{12,8},{16,12},{20,16},{24,20},{28,24},{1,29},{... | collective-permute-start | bytes 2654216 | tf_op jit(solution)/shard_map/ppermute | solution.py:436
  69.7 0.8 copy-start.3
  69.7 19.7 %collective-permute-start.9 = (f32[2,18,8,512]{3,2,1,0:T(8,128)}, f32[2,18,8,512]{3,2,1,0:T(8,128)}, u32[]{:S(2)}, u32[]{:S(2)}) collective-permute-start(f32[2,18,8,512]{3,2,1,0:T(8,128)} %get-tuple-element.43), channel_id=1, source_target_pairs={{0,28},{4,0},{8,4},{12,8},{16,12},{20,16},{24,20},{28,24},{1,29},{... | collective-permute-start | bytes 1769480 | tf_op jit(solution)/shard_map/ppermute | solution.py:436
  69.7 3.7 %copy-start = (f32[64,8,512]{2,1,0:T(8,128)}, f32[64,8,512]{2,1,0:T(8,128)S(1)}, u32[]{:S(2)}) copy-start(f32[64,8,512]{2,1,0:T(8,128)S(1)} %collective-permute-done.2.below_ref.ba_ref) | copy-start | bytes 3145732
  69.7 52.1 %collective-permute-start.4 = (f32[3,18,8,512]{3,2,1,0:T(8,128)}, f32[3,18,8,512]{3,2,1,0:T(8,128)S(1)}, u32[]{:S(2)}, u32[]{:S(2)}) collective-permute-start(f32[3,18,8,512]{3,2,1,0:T(8,128)} %get-tuple-element.38), channel_id=1, source_target_pairs={{0,4},{4,8},{8,12},{12,16},{16,20},{20,24},{24,28},{28,0},{1,5},{5... | collective-permute-start | bytes 2654216 | tf_op jit(solution)/shard_map/ppermute | solution.py:436
  70.5 2.8 %copy-start.1 = (f32[64,8,512]{2,1,0:T(8,128)}, f32[64,8,512]{2,1,0:T(8,128)S(1)}, u32[]{:S(2)}) copy-start(f32[64,8,512]{2,1,0:T(8,128)S(1)} %collective-permute-done.3.above_ref.aa_ref) | copy-start | bytes 3145732
  70.5 51.3 %collective-permute-start.5 = (f32[3,18,8,512]{3,2,1,0:T(8,128)}, f32[3,18,8,512]{3,2,1,0:T(8,128)}, u32[]{:S(2)}, u32[]{:S(2)}) collective-permute-start(f32[3,18,8,512]{3,2,1,0:T(8,128)} %get-tuple-element.39), channel_id=1, source_target_pairs={{0,28},{4,0},{8,4},{12,8},{16,12},{20,16},{24,20},{28,24},{1,29},{... | collective-permute-start | bytes 2654216 | tf_op jit(solution)/shard_map/ppermute | solution.py:436
  89.3 20.8 %collective-permute-start.10 = (f32[2,4,128,128]{3,2,1,0:T(8,128)}, f32[2,4,128,128]{3,2,1,0:T(8,128)S(1)}, u32[]{:S(2)}, u32[]{:S(2)}) collective-permute-start(f32[2,4,128,128]{3,2,1,0:T(8,128)} %get-tuple-element.49), channel_id=1, source_target_pairs={{0,1},{1,2},{2,3},{3,0},{4,5},{5,6},{6,7},{7,4},{8,9},{9,10},{10,1... | collective-permute-start | bytes 1572872 | tf_op jit(solution)/shard_map/ppermute | solution.py:436
  89.6 24.1 %collective-permute-start.11 = (f32[2,4,128,128]{3,2,1,0:T(8,128)}, f32[2,4,128,128]{3,2,1,0:T(8,128)S(1)}, u32[]{:S(2)}, u32[]{:S(2)}) collective-permute-start(f32[2,4,128,128]{3,2,1,0:T(8,128)} %get-tuple-element.50), channel_id=1, source_target_pairs={{0,2},{1,3},{2,0},{3,1},{4,6},{5,7},{6,4},{7,5},{8,10},{9,11},{10,... | collective-permute-start | bytes 1572872 | tf_op jit(solution)/shard_map/ppermute | solution.py:436
  91.0 22.7 %collective-permute-start.12 = (f32[2,4,128,128]{3,2,1,0:T(8,128)}, f32[2,4,128,128]{3,2,1,0:T(8,128)}, u32[]{:S(2)}, u32[]{:S(2)}) collective-permute-start(f32[2,4,128,128]{3,2,1,0:T(8,128)} %get-tuple-element.51), channel_id=1, source_target_pairs={{0,3},{1,0},{2,1},{3,2},{4,7},{5,4},{6,5},{7,6},{8,11},{9,8},{10,9... | collective-permute-start | bytes 1572872 | tf_op jit(solution)/shard_map/ppermute | solution.py:436
  110.1 3.6 %copy-start.4 = (f32[2,4,128,128]{3,2,1,0:T(8,128)}, f32[2,4,128,128]{3,2,1,0:T(8,128)S(1)}, u32[]{:S(2)}) copy-start(f32[2,4,128,128]{3,2,1,0:T(8,128)S(1)} %collective-permute-done.10.rest_1_) | copy-start | bytes 1572868
  113.7 0.8 copy-start.5
  121.8 0.9 copy-start.2

commit v6 on v5

--- a/solution.py
+++ b/solution.py
@@ -19,7 +19,8 @@
 FAR = TIME_STEP / 12.0
 VMEM = 56 * 1024 * 1024
 PACK_COST = DENSITY_COST = MODES_COST = (1e6, 1e5)
-STATE_COST = MAIN_COST = (1e6, 4e8)
+STATE_COST = (1e6, 4e8)
+MAIN_COST = (1e12, 4e9)
 
 
 def pair(ref, *index):
@@ -59,7 +60,19 @@
     return push + turned
 
 
-def pack_kernel(rho_ref, mz_ref, bx_ref, rho_a, mom_a, mag_a, pot_a, rho_z, mom_z, mag_z, pot_z, up_ref, down_ref, first_ref, last_ref):
+def first_kernel(cell_ref, count_ref, rho_a, mom_a, mag_a, pot_a, rho_z, mom_z, mag_z, pot_z, ev_ref, first_ref, last_ref):
+    shape = (1, ev_ref.shape[2])
+    lane = lax.broadcasted_iota(jnp.int32, shape, 1)
+    row = jnp.zeros(shape, jnp.int32)
+    for e in range(count_ref.shape[0]):
+        for i in range(4):
+            row = jnp.where(lane == 4 * e + i, cell_ref[e, i] if i < 3 else count_ref[e], row)
+
+    def copy(d, _):
+        ev_ref[d] = row
+        return 0
+
+    lax.fori_loop(0, ev_ref.shape[0], copy, 0)
     for ref, rho, mom, mag, pot, skip in (
         (first_ref, rho_a, mom_a, mag_a, pot_a, 0), (last_ref, rho_z, mom_z, mag_z, pot_z, pot_z.shape[0] - 2),
     ):
@@ -69,6 +82,9 @@
                 ref[1 + c, j] = mom[c, 0, j]
                 ref[4 + c, j] = mag[c, 0, j]
             ref[7, j] = jnp.broadcast_to(pot[skip + j : skip + j + 1], ref.shape[2:])
+
+
+def pack_kernel(rho_ref, mz_ref, bx_ref, after_ref, up_ref, down_ref):
     half = rho_ref.shape[1]
 
     def body(p, _):
@@ -84,8 +100,8 @@
 
 
 def state_kernel(
-    ev_ref, at_ref, rho_ref, mom_ref, mag_ref, pot_ref, before_ref, after_ref, rho_l, mom_l, mag_l, pot_l,
-    rho_h, mom_h, mag_h, pot_h, u_out, edge_out, sb_out, sa_out, *rest, depth, counts,
+    ev_ref, rho_ref, mom_ref, mag_ref, pot_ref, before_ref, after_ref, rho_l, mom_l, mag_l, pot_l,
+    rho_h, mom_h, mag_h, pot_h, u_out, edge_out, sb_out, sa_out, *rest, depth, counts, per_device,
 ):
     ups, downs, (s_ref, sb_ref, sa_ref) = rest[: len(rest) // 2 - 1], rest[len(rest) // 2 - 1 : -3], rest[-3:]
     half, ny = s_ref.shape[1] - 4, s_ref.shape[3]
@@ -93,7 +109,7 @@
 
     @pl.when(step_id == 0)
     def _():
-        deposit(ev_ref, at_ref, s_ref, sb_ref, sa_ref, depth)
+        deposit(ev_ref, s_ref, sb_ref, sa_ref, depth, per_device)
         pieces = lambda rho, mom, mag, pot, j: (
             [rho[0, j]] + [mom[c, 0, j] for c in range(3)] + [mag[c, 0, j] for c in range(3)]
             + [jnp.broadcast_to(pot, (4, ny))]
@@ -149,10 +165,10 @@
         begin += count
 
 
-def deposit(ev_ref, at_ref, s_ref, sb_ref, sa_ref, depth):
+def deposit(ev_ref, s_ref, sb_ref, sa_ref, depth, per_device):
     half, ny = s_ref.shape[1] - 4, s_ref.shape[3]
-    rows, events = 2 * half, ev_ref.shape[0] // 4
-    row_start, plane_start = at_ref[0], at_ref[1]
+    rows, events = 2 * half, ev_ref.shape[0] * per_device
+    row_start, plane_start = lax.axis_index("xy") * rows, lax.axis_index("gz") * 4
     s_ref[...] = jnp.zeros_like(s_ref)
     sb_ref[...] = jnp.zeros_like(sb_ref)
     sa_ref[...] = jnp.zeros_like(sa_ref)
@@ -168,7 +184,8 @@
         return jnp.where(distance < -(size // 2), distance + size, distance)
 
     def event(e, _):
-        row, col, plane, count = (ev_ref[4 * e + i] for i in range(4))
+        device, slot_id = (e, 0) if per_device == 1 else (lax.div(e, per_device), lax.rem(e, per_device))
+        row, col, plane, count = (ev_ref[device, 0, 4 * slot_id + i] for i in range(4))
         rel = wrapped(row - row_start - half, NX)
         rel = rel + half
 
@@ -255,9 +272,8 @@
 
 
 def density_kernel(
-    at_ref, u_hbm, edge_hbm, below_ref, above_ref, sb_ref, sa_ref, order_ref, high_ref, low_ref, out_ref, *rest,
+    u_hbm, edge_hbm, below_ref, above_ref, sb_ref, sa_ref, order_ref, high_ref, low_ref, out_ref, wave_ref, d_ref, u_ref, sem,
 ):
-    *waves, d_ref, w_ref, u_ref, sem = rest
     fetch(u_hbm, edge_hbm, u_ref, sem, 0)
     half = below_ref.shape[0]
     rows = 2 * half
@@ -286,19 +302,10 @@
     for part in range(2):
         c_high, c_low = high_ref[part], low_ref[part]
         wave = dot(high, c_high) + dot(high, c_low) + dot(low, c_high)
-        if len(waves) == 1:
-            peers, band = waves[0].shape[0], waves[0].shape[4]
-            for j in range(peers):
-                for z in range(4):
-                    waves[0][j, part, z] = wave[z * rows : (z + 1) * rows, j * band : (j + 1) * band]
-            continue
-        w_ref[...] = wave
-        me = at_ref[0] // rows
-        for s, ref in enumerate(waves):
-            peer = jnp.where(me + s >= len(waves), me + s - len(waves), me + s)
-            lanes = pl.ds(pl.multiple_of(peer * 128, 128) if ref.shape[3] == 128 else peer * ref.shape[3], ref.shape[3])
+        peers, band = wave_ref.shape[0], wave_ref.shape[4]
+        for j in range(peers):
             for z in range(4):
-                ref[part, z] = w_ref[z * rows : (z + 1) * rows, lanes]
+                wave_ref[j, part, z] = wave[z * rows : (z + 1) * rows, j * band : (j + 1) * band]
 
 
 def last_plane(below, above, j):
@@ -374,22 +381,18 @@
     lax.fori_loop(0, chunk // 4, body, 0)
 
 
-def modes_kernel(at_ref, *rest, turned):
-    *pieces, ch_ref, cl_ref, sh_ref, sl_ref, out_ref, x_ref = rest
+def modes_kernel(w_ref, ch_ref, cl_ref, sh_ref, sl_ref, out_ref, x_ref, *, turned):
     dot = functools.partial(jnp.dot, preferred_element_type=jnp.float32)
     planes, band, nx = out_ref.shape[1:]
 
     def split(part):
         if turned:
-            x = jnp.concatenate([pieces[0][part, z] for z in range(planes)], axis=0)
+            x = jnp.concatenate([w_ref[part, z] for z in range(planes)], axis=0)
         else:
-            width = nx // len(pieces)
-            me = at_ref[0] // width
-            for s, ref in enumerate(pieces):
-                peer = jnp.where(me - s < 0, me - s + len(pieces), me - s)
-                lanes = pl.ds(pl.multiple_of(peer * 128, 128) if width == 128 else peer * width, width)
+            width = w_ref.shape[3]
+            for s in range(w_ref.shape[0]):
                 for z in range(planes):
-                    x_ref[z * band : (z + 1) * band, lanes] = ref[part, z].T
+                    x_ref[z * band : (z + 1) * band, s * width : (s + 1) * width] = w_ref[s, part, z].T
             x = x_ref[...]
         high = x.astype(jnp.bfloat16)
         return high, (x - high.astype(jnp.float32)).astype(jnp.bfloat16)
@@ -398,7 +401,7 @@
     times = lambda x, h, l: dot(x[0], h[...]) + dot(x[0], l[...]) + dot(x[1], h[...])
     scale = 1.0 / math.sqrt(NX * nx)
     shape = (band, nx)
-    ky = lax.broadcasted_iota(jnp.int32, shape, 0) + at_ref[2]
+    ky = lax.broadcasted_iota(jnp.int32, shape, 0) + lax.axis_index("xy") * band
     kx = lax.broadcasted_iota(jnp.int32, shape, 1)
     keep = jnp.where((ky == 0) & (kx == 0), 0.0, scale)
     out_re = times(re, ch_ref, cl_ref) + times(im, sh_ref, sl_ref)
@@ -451,29 +454,21 @@
     message = shape((2, half, planes, ny), f32)
     tile = shape((half, 8, ny), f32)
     steps = half // 8
-    counts = (steps // 4, (steps - steps // 4) // 2, steps - steps // 4 - (steps - steps // 4) // 2) if steps >= 4 else (steps,)
+    counts = (steps * 5 // 8, steps - steps * 5 // 8) if steps >= 2 else (steps,)
 
     slots_here = sn_cells.shape[0]
-    mine = jnp.concatenate([sn_cells, sn_counts[:, None]], axis=1).reshape(1, 1, 4 * slots_here)
-    mine = jnp.pad(mine, ((0, 0), (0, 0), (0, -(4 * slots_here) % 128)))
-    events = lax.all_to_all(
-        jnp.broadcast_to(mine, (devices, 1, mine.shape[2])), ("gz", "xy"), split_axis=0, concat_axis=0, tiled=True
-    )
-    events = events[:, 0, : 4 * slots_here].reshape(-1)
-    at = jnp.stack([tile_row * rows, tile_plane * planes, tile_row * (ny // across)]).astype(jnp.int32)
-
     rho = density.reshape(2, half, planes, ny)
     mom = momentum.reshape(3, 2, half, planes, ny)
     mag = magnetic.reshape(3, 2, half, planes, ny)
 
     pot = arm_potential.reshape(2, half, ny)
-    one = lambda f: pl.BlockSpec((1, 2, half, planes, ny), lambda i, f=f: (f, 0, 0, 0, 0))
+    edges = shape((8, 2, planes, ny), f32)
+    mine = shape((devices, 1, -(-4 * slots_here // 128) * 128), jnp.int32)
     full = lambda s: pl.BlockSpec(s, lambda i: (0,) * len(s))
-    edges = shape((8, 2, planes, ny), f32)
-    up, down, first_rows, last_rows = pl.pallas_call(
-        pack_kernel,
+    mine, first_rows, last_rows = pl.pallas_call(
+        first_kernel,
         grid=(1,),
-        in_specs=[full(message.shape), one(2), one(0)] + [
+        in_specs=[smem, smem] + [
             spec
             for h, k in ((0, 0), (1, half // 2 - 1))
             for spec in (
@@ -483,13 +478,28 @@
                 pl.BlockSpec((8, ny), lambda i, h=h: (h * (rows // 8 - 1), 0)),
             )
         ],
-        out_specs=[full(tile.shape)] * 2 + [full(edges.shape)] * 2,
-        out_shape=[tile] * 2 + [edges] * 2,
+        out_specs=[full(mine.shape)] + [full(edges.shape)] * 2,
+        out_shape=[mine] + [edges] * 2,
+        compiler_params=params,
+        cost_estimate=cost(*PACK_COST),
+        name="first",
+    )(sn_cells, sn_counts, *[rho, mom, mag, arm_potential] * 2)
+    events = lax.all_to_all(mine, ("gz", "xy"), split_axis=0, concat_axis=0, tiled=True)
+    before, after = shift(last_rows, "xy", 1), shift(first_rows, "xy", -1)
+
+    some = math.gcd(half, 16)
+    up, down = pl.pallas_call(
+        pack_kernel,
+        grid=(half // some,),
+        in_specs=[pl.BlockSpec((2, some, planes, ny), lambda i: (0, i, 0, 0))] + [
+            pl.BlockSpec((1, 2, some, planes, ny), lambda i, f=f: (f, 0, i, 0, 0)) for f in (2, 0)
+        ] + [pl.BlockSpec(memory_space=pl.ANY)],
+        out_specs=[pl.BlockSpec((some, 8, ny), lambda i: (i, 0, 0))] * 2,
+        out_shape=[tile] * 2,
         compiler_params=params,
         cost_estimate=cost(*PACK_COST),
         name="pack",
-    )(rho, mom, mag, *[rho, mom, mag, arm_potential] * 2)
-    before, after = shift(last_rows, "xy", 1), shift(first_rows, "xy", -1)
+    )(rho, mom, mag, mine)
     below_a, above_a = shift(up, "gz", 1), shift(down, "gz", -1)
 
     parcels = [shape((n, 18, 8, ny), f32) for n in counts]
@@ -511,10 +521,10 @@
     ]
     rows_of = lambda n: pl.BlockSpec((n, 2, 8, planes, ny), lambda i: (0, 0, i, 0, 0))
     state, edge, sb, sa, *messages = pl.pallas_call(
-        functools.partial(state_kernel, depth=planes * layers, counts=counts),
+        functools.partial(state_kernel, depth=planes * layers, counts=counts, per_device=slots_here),
         grid=(steps,),
         in_specs=[
-            smem, smem, pl.BlockSpec((2, 8, planes, ny), lambda i: (0, i, 0, 0)), rows_of(3), rows_of(3),
+            smem, pl.BlockSpec((2, 8, planes, ny), lambda i: (0, i, 0, 0)), rows_of(3), rows_of(3),
             pl.BlockSpec((2, 8, ny), lambda i: (0, i, 0)), full(edges.shape), full(edges.shape),
         ] + middle,
         out_specs=[pl.BlockSpec((8, 8, 8, ny), lambda i: (0, i, 0, 0)), full((8, 4, 8, ny)), eight, eight] + parcel_specs * 2,
@@ -523,7 +533,7 @@
         compiler_params=params,
         cost_estimate=cost(*STATE_COST),
         name="state",
-    )(events, at, rho, mom, mag, pot, before, after, *[rho, mom, mag, pot] * 2)
+    )(events, rho, mom, mag, pot, before, after, *[rho, mom, mag, pot] * 2)
     parcels_below, parcels_above = [], []
     for i in range(len(counts)):
         parcels_below.append(shift(messages[i], "gz", 1))
@@ -532,40 +542,37 @@
     cos_high, cos_low, sin_high, sin_low = tables(ny)
     band = ny // across
     turned = band % 128 != 0 or rows % 128 != 0
-    waves = [shape((across, 2, planes, rows, band), f32)] if turned else [shape((2, planes, rows, band), f32)] * across
     hbm = pl.BlockSpec(memory_space=pl.ANY)
     copies = pltpu.SemaphoreType.DMA((3,))
-    new_density, *waves = pl.pallas_call(
+    new_density, wave = pl.pallas_call(
         density_kernel,
-        in_specs=[smem, hbm, hbm] + [whole] * 7,
-        out_specs=[whole] * (1 + len(waves)),
-        out_shape=[message, *waves],
+        in_specs=[hbm, hbm] + [whole] * 7,
+        out_specs=[whole] * 2,
+        out_shape=[message, shape((across, 2, planes, rows, band), f32)],
         scratch_shapes=[
-            pltpu.VMEM((8 * half, ny), f32), pltpu.VMEM((8 * half, ny), f32), pltpu.VMEM((4, half + 4, 8, ny), f32), copies,
+            pltpu.VMEM((8 * half, ny), f32), pltpu.VMEM((4, half + 4, 8, ny), f32), copies,
         ],
         compiler_params=params,
         cost_estimate=cost(*DENSITY_COST),
         name="density",
     )(
-        at, state, edge, below_a, above_a, sb, sa, row_order(half),
+        state, edge, below_a, above_a, sb, sa, row_order(half),
         np.stack([cos_high, -sin_high]), np.stack([cos_low, -sin_low]),
     )
 
+    portion = lax.all_to_all(wave, "xy", split_axis=0, concat_axis=0, tiled=True)
     if turned:
-        portion = lax.all_to_all(waves[0], "xy", split_axis=0, concat_axis=0, tiled=True)
-        pieces = [portion.transpose(1, 2, 4, 0, 3).reshape(2, planes, band, NX)]
-    else:
-        pieces = waves[:1] + [shift(waves[s], "xy", s) for s in range(1, across)]
+        portion = portion.transpose(1, 2, 4, 0, 3).reshape(2, planes, band, NX)
     modes = pl.pallas_call(
         functools.partial(modes_kernel, turned=turned),
-        in_specs=[smem] + [whole] * (len(pieces) + 4),
+        in_specs=[whole] * 5,
         out_specs=whole,
         out_shape=shape((2, planes, band, NX), f32),
         scratch_shapes=[pltpu.VMEM((planes * band, NX), f32)],
         compiler_params=params,
         cost_estimate=cost(*MODES_COST),
         name="modes",
-    )(at, *pieces, *tables(NX))
+    )(portion, *tables(NX))
     results = [shape((3, 2, half, planes, ny), f32)] * 2
     new = []
     for i, n in enumerate(counts):

time: 133 us -> 158 us (1.19)
  waiting for transfers between devices: 35.2 us -> 58.9 us
  blocking collectives: 0 us -> 12.7 us
  starting transfers between devices: 22 us -> 15.5 us
  Pallas kernels: 69.5 us -> 67.2 us
  local copies, waits for them, and re-layouts: 3.99 us -> 1.96 us
    ppermute x13 -> x8, waiting for transfers between devices: 18.1 us -> 47.6 us  [shift(): return lax.ppermute(block, axis, [(i, (i + step) % n) for i in range(n)])]
    all_to_all x0 -> x1, blocking collectives: none -> 12.7 us  [on_device(): lax.all_to_all(mine, ('gz', 'xy'), split_axis=0, concat_axis=0, tiled=True)]
    ppermute x13 -> x8, starting transfers between devices: 17.5 us -> 11 us  [shift(): return lax.ppermute(block, axis, [(i, (i + step) % n) for i in range(n)])]
    all_to_all x1, waiting for transfers between devices: 17.2 us -> 11.2 us  [on_device(): lax.all_to_all(wave, 'xy', split_axis=0, concat_axis=0, tiled=True)]
    pallas_call x3 -> x2, Pallas kernels: 27.7 us -> 24.3 us  [on_device(): pl.pallas_call(functools.partial(main_kernel, first=first), grid=(n,), in...]
    pallas_call x2 -> x3, Pallas kernels: 19.2 us -> 20.9 us  [the longest x1 14.7 us: on_device(): pl.pallas_call(density_kernel, in_specs=[hbm, hbm] + [whole] * 7, out_spe...]
  transfers between devices with their start and end apart: 14 -> 9, of which waited for: 4 -> 2; matrix products, arithmetic and copies ran while one was open for 1% -> 0% of each run, Pallas kernels for 42% -> 26%
where the time goes in v6:
time: 158 us
  Pallas kernels  67.2 us (43%)
  waiting for transfers between devices  58.9 us (37%)
  starting transfers between devices  15.5 us (10%)
  blocking collectives  12.7 us (8%)
  local copies, waits for them, and re-layouts  1.96 us (1%)
    ppermute x8, waiting for transfers between devices, shift(): return lax.ppermute(block, axis, [(i, (i + step) % n) for i in range(n)])  47.6 us
    pallas_call x2, Pallas kernels, on_device(): pl.pallas_call(functools.partial(main_kernel, first=first), grid=(n,), in...  24.3 us
    pallas_call x1, Pallas kernels, on_device(): pl.pallas_call(functools.partial(state_kernel, depth=planes * layers, cou...  15 us
    pallas_call x1, Pallas kernels, on_device(): pl.pallas_call(density_kernel, in_specs=[hbm, hbm] + [whole] * 7, out_spe...  14.7 us
    all_to_all x1, blocking collectives, on_device(): lax.all_to_all(mine, ('gz', 'xy'), split_axis=0, concat_axis=0, tiled=True)  12.7 us
    all_to_all x1, waiting for transfers between devices, on_device(): lax.all_to_all(wave, 'xy', split_axis=0, concat_axis=0, tiled=True)  11.2 us
    ppermute x8, starting transfers between devices, shift(): return lax.ppermute(block, axis, [(i, (i + step) % n) for i in range(n)])  11 us
    pallas_call x1, Pallas kernels, on_device(): pl.pallas_call(functools.partial(modes_kernel, turned=turned), in_specs=[...  6.99 us
  transfers between devices with their start and end apart: 9, of which 2 were waited for; matrix products, arithmetic and copies ran while one was open for 0% of the time, Pallas kernels for 26%

profile of v6, /device:TPU:0, one launch (start us, length us, event | category | flops | bytes accessed | tf_op | source)
XLA Modules:
  0.0 157.6 jit_solution(10665088420667354235)
XLA Ops:
  1.3 1.8 %first.1 = (s32[32,1,128]{2,1,0:T(1,128)}, f32[8,2,4,512]{3,2,1,0:T(4,128)}, f32[8,2,4,512]{3,2,1,0:T(4,128)}) custom-call(s32[1,3]{1,0:T(1,128)} %cell_ref.1, s32[1]{0:T(128)S(6)} %copy.21.count_ref, f32[2,64,4,512]{3,2,1,0:T(4,128)} %bitcast.19, f32[3,2,64,4,512]{4,3,2,1,0:T(4,128)} %bitcast.7, f32[3,2,64,4,512]{4,3,2,1,0:T(4,128)} %bitcast.13, ...), custom_call_target="tpu_custom_call" | custom-call | flops 1000000 | bytes 100000 | tf_op jit(solution)/shard_map/first/pallas_call | solution.py:468
  3.1 2.9 %collective-permute-start = (f32[8,2,4,512]{3,2,1,0:T(4,128)}, f32[8,2,4,512]{3,2,1,0:T(4,128)S(1)}, u32[]{:S(2)}, u32[]{:S(2)}) collective-permute-start(f32[8,2,4,512]{3,2,1,0:T(4,128)} %get-tuple-element.24), channel_id=1, source_target_pairs={{0,1},{1,2},{2,3},{3,0},{4,5},{5,6},{6,7},{7,4},{8,9},{9,10},{10,1... | collective-permute-start | bytes 393224 | tf_op jit(solution)/shard_map/ppermute | solution.py:439
  6.1 1.0 collective-permute-start.1
  7.0 12.7 %all_to_all.10.ev_ref = s32[32,1,128]{2,1,0:T(1,128)} all-to-all(s32[32,1,128]{2,1,0:T(1,128)} %get-tuple-element.23.after_ref), channel_id=1, replica_groups=mesh['gz'=8,'xy'=4] {'gz','xy'}, dimensions={0} | all-to-all | bytes 32768 | tf_op jit(solution)/shard_map/all_to_all | solution.py:487
  19.7 0.0 collective-permute-done.before_ref
  19.7 0.0 collective-permute-done.1.after_ref
  19.7 0.0 copy-start.3
  19.7 0.6 copy-done.2
  20.4 0.0 copy-done.3
  20.4 15.0 %state.1 = (f32[8,64,8,512]{3,2,1,0:T(8,128)}, f32[8,4,8,512]{3,2,1,0:T(8,128)}, f32[64,8,512]{2,1,0:T(8,128)}, f32[64,8,512]{2,1,0:T(8,128)}, f32[5,18,8,512]{3...) custom-call(s32[32,1,128]{2,1,0:T(1,128)} %all_to_all.10.ev_ref, ...), custom_call_target="tpu_custom_call" | custom-call | flops 1000000 | bytes 400000000 | tf_op jit(solution)/shard_map/state/pallas_call | solution.py:523
  35.4 0.1 collective-permute-start.6
  35.4 3.5 %collective-permute-start.7 = (f32[5,18,8,512]{3,2,1,0:T(8,128)}, f32[5,18,8,512]{3,2,1,0:T(8,128)}, u32[]{:S(2)}, u32[]{:S(2)}) collective-permute-start(f32[5,18,8,512]{3,2,1,0:T(8,128)} %get-tuple-element.36), channel_id=1, source_target_pairs={{0,28},{4,0},{8,4},{12,8},{16,12},{20,16},{24,20},{28,24},{1,29},{... | collective-permute-start | bytes 4423688 | tf_op jit(solution)/shard_map/ppermute | solution.py:439
  39.0 4.3 %pack.1 = (f32[64,8,512]{2,1,0:T(8,128)}, f32[64,8,512]{2,1,0:T(8,128)}) custom-call(f32[2,64,4,512]{3,2,1,0:T(4,128)} %bitcast.24, f32[3,2,64,4,512]{4,3,2,1,0:T(4,128)} %bitcast.12, f32[3,2,64,4,512]{4,3,2,1,0:T(4,128)} %bitcast.18, s32[32,1,128]{2,1,0:T(1,128)} %get-tuple-element.23.after_ref), custom_call_target="tpu_custom_call" | custom-call | flops 1000000 | bytes 100000 | tf_op jit(solution)/shard_map/pack/pallas_call | solution.py:491
  43.3 0.0 collective-permute-start.2
  43.3 3.5 %collective-permute-start.3 = (f32[64,8,512]{2,1,0:T(8,128)}, f32[64,8,512]{2,1,0:T(8,128)S(1)}, u32[]{:S(2)}, u32[]{:S(2)}) collective-permute-start(f32[64,8,512]{2,1,0:T(8,128)} %get-tuple-element.29), channel_id=1, source_target_pairs={{0,28},{4,0},{8,4},{12,8},{16,12},{20,16},{24,20},{28,24},{1,29},{... | collective-permute-start | bytes 3145736 | tf_op jit(solution)/shard_map/ppermute | solution.py:439
  46.9 0.0 collective-permute-start.4
  46.9 47.6 %collective-permute-done.2.below_ref.ba_ref = f32[64,8,512]{2,1,0:T(8,128)S(1)} collective-permute-done((f32[64,8,512]{2,1,0:T(8,128)}, f32[64,8,512]{2,1,0:T(8,128)S(1)}, u32[]{:S(2)}, u32[]{:S(2)}) %collective-permute-start.2) | collective-permute-done | bytes 1048608 | tf_op jit(solution)/shard_map/ppermute | solution.py:439
  94.5 0.0 collective-permute-start.5
  94.5 0.0 collective-permute-done.3.above_ref.aa_ref
  94.5 0.0 copy-start.1
  94.5 1.0 copy-done
  95.5 0.3 copy-done.1
  95.8 14.7 %density.1 = (f32[2,64,4,512]{3,2,1,0:T(4,128)}, f32[4,2,4,128,128]{4,3,2,1,0:T(8,128)}) custom-call(f32[8,64,8,512]{3,2,1,0:T(8,128)} %get-tuple-element.26.u_hbm, f32[8,4,8,512]{3,2,1,0:T(8,128)} %get-tuple-element.27.edge_hbm, f32[64,8,512]{2,1,0:T(8,128)} %copy-done, f32[64,8,512]{2,1,0:T(8,128)} %copy-done.1, f32[64,8,512]{2,1,0:T(8,128)} %get-tuple-element.30.sb_ref, ...), custom_call_target="tpu_custom_call" | custom-call | flops 1000000 | bytes 100000 | tf_op jit(solution)/shard_map/density/pallas_call | solution.py:547
  110.5 4.5 %all-to-all-start.1 = ((f32[4,2,4,128,128]{4,3,2,1,0:T(8,128)}), f32[4,2,4,128,128]{4,3,2,1,0:T(8,128)}, u32[]{:S(2)}, u32[]{:S(2)}) async-start(f32[4,2,4,128,128]{4,3,2,1,0:T(8,128)} %get-tuple-element.39), calls=%async_computation.1 | async-start | bytes 4194304 | tf_op jit(solution)/shard_map/all_to_all | solution.py:563
  115.1 0.0 collective-permute-done.6.from_below
  115.1 0.0 collective-permute-done.7.from_above
  115.1 14.3 %main0.1 = (f32[3,2,64,4,512]{4,3,2,1,0:T(4,128)}, f32[3,2,64,4,512]{4,3,2,1,0:T(4,128)}) custom-call(f32[8,64,8,512]{3,2,1,0:T(8,128)} %get-tuple-element.26.u_hbm, f32[8,4,8,512]{3,2,1,0:T(8,128)} %get-tuple-element.27.edge_hbm, f32[64,8,512]{2,1,0:T(8,128)} %copy-done, f32[64,8,512]{2,1,0:T(8,128)} %copy-done.1, f32[64,8,512]{2,1,0:T(8,128)} %get-tuple-element.30.sb_ref, ...), custom_call_target="tpu_custom_call" | custom-call | flops 999999995904 | bytes 4000000000 | tf_op jit(solution)/shard_map/main0/pallas_call | solution.py:585
  129.4 11.2 %all-to-all-done.1.w_ref = f32[4,2,4,128,128]{4,3,2,1,0:T(8,128)} async-done(((f32[4,2,4,128,128]{4,3,2,1,0:T(8,128)}), f32[4,2,4,128,128]{4,3,2,1,0:T(8,128)}, u32[]{:S(2)}, u32[]{:S(2)}) %all-to-all-start.1) | async-done | bytes 2097184 | tf_op jit(solution)/shard_map/all_to_all | solution.py:563
  140.6 7.0 %modes.1.rest_2_ = f32[2,4,128,512]{3,2,1,0:T(8,128)} custom-call(f32[4,2,4,128,128]{4,3,2,1,0:T(8,128)} %all-to-all-done.1.w_ref, bf16[512,512]{1,0:T(8,128)(2,1)} %constant.17.clone.ch_ref, bf16[512,512]{1,0:T(8,128)(2,1)} %constant.18.clone.cl_ref, bf16[512,512]{1,0:T(8,128)(2,1)} %constant.19.clone.sh_ref, bf16[512,512]{1,0:T(8,128)(2,1)} %constant.20.clone.sl_ref), custom_call_target="tpu_custom_call" | custom-call | flops 1000000 | bytes 100000 | tf_op jit(solution)/shard_map/modes/pallas_call | solution.py:566
  147.6 0.0 collective-permute-done.4.from_below
  147.6 0.0 collective-permute-done.5.from_above
  147.6 10.0 %main1.1 = (f32[3,2,64,4,512]{4,3,2,1,0:T(4,128)}, f32[3,2,64,4,512]{4,3,2,1,0:T(4,128)}) custom-call(f32[8,64,8,512]{3,2,1,0:T(8,128)} %get-tuple-element.26.u_hbm, f32[8,4,8,512]{3,2,1,0:T(8,128)} %get-tuple-element.27.edge_hbm, f32[64,8,512]{2,1,0:T(8,128)} %copy-done, f32[64,8,512]{2,1,0:T(8,128)} %copy-done.1, ...), custom_call_target="tpu_custom_call", output_to_operand_aliasing={{0}: (8, {}), {1}: (9, {})} | custom-call | flops 999999995904 | bytes 4000000000 | tf_op jit(solution)/shard_map/main1/pallas_call | solution.py:585
  (2 shorter events, 0.0 us)
Async XLA Ops:
  3.1 16.6 %collective-permute-start = (f32[8,2,4,512]{3,2,1,0:T(4,128)}, f32[8,2,4,512]{3,2,1,0:T(4,128)S(1)}, u32[]{:S(2)}, u32[]{:S(2)}) collective-permute-start(f32[8,2,4,512]{3,2,1,0:T(4,128)} %get-tuple-element.24), channel_id=1, source_target_pairs={{0,1},{1,2},{2,3},{3,0},{4,5},{5,6},{6,7},{7,4},{8,9},{9,10},{10,1... | collective-permute-start | bytes 393224 | tf_op jit(solution)/shard_map/ppermute | solution.py:439
  6.1 13.7 %collective-permute-start.1 = (f32[8,2,4,512]{3,2,1,0:T(4,128)}, f32[8,2,4,512]{3,2,1,0:T(4,128)S(1)}, u32[]{:S(2)}, u32[]{:S(2)}) collective-permute-start(f32[8,2,4,512]{3,2,1,0:T(4,128)} %get-tuple-element.25), channel_id=1, source_target_pairs={{0,3},{1,0},{2,1},{3,2},{4,7},{5,4},{6,5},{7,6},{8,11},{9,8},{10,9... | collective-permute-start | bytes 393224 | tf_op jit(solution)/shard_map/ppermute | solution.py:439
  19.7 0.7 copy-start.2
  19.7 0.7 copy-start.3
  35.4 79.7 %collective-permute-start.6 = (f32[5,18,8,512]{3,2,1,0:T(8,128)}, f32[5,18,8,512]{3,2,1,0:T(8,128)}, u32[]{:S(2)}, u32[]{:S(2)}) collective-permute-start(f32[5,18,8,512]{3,2,1,0:T(8,128)} %get-tuple-element.35), channel_id=1, source_target_pairs={{0,4},{4,8},{8,12},{12,16},{16,20},{20,24},{24,28},{28,0},{1,5},{5... | collective-permute-start | bytes 4423688 | tf_op jit(solution)/shard_map/ppermute | solution.py:439
  35.4 79.6 %collective-permute-start.7 = (f32[5,18,8,512]{3,2,1,0:T(8,128)}, f32[5,18,8,512]{3,2,1,0:T(8,128)}, u32[]{:S(2)}, u32[]{:S(2)}) collective-permute-start(f32[5,18,8,512]{3,2,1,0:T(8,128)} %get-tuple-element.36), channel_id=1, source_target_pairs={{0,28},{4,0},{8,4},{12,8},{16,12},{20,16},{24,20},{28,24},{1,29},{... | collective-permute-start | bytes 4423688 | tf_op jit(solution)/shard_map/ppermute | solution.py:439
  43.3 51.2 %collective-permute-start.2 = (f32[64,8,512]{2,1,0:T(8,128)}, f32[64,8,512]{2,1,0:T(8,128)S(1)}, u32[]{:S(2)}, u32[]{:S(2)}) collective-permute-start(f32[64,8,512]{2,1,0:T(8,128)} %get-tuple-element.28), channel_id=1, source_target_pairs={{0,4},{4,8},{8,12},{12,16},{16,20},{20,24},{24,28},{28,0},{1,5},{5... | collective-permute-start | bytes 3145736 | tf_op jit(solution)/shard_map/ppermute | solution.py:439
  43.3 51.2 %collective-permute-start.3 = (f32[64,8,512]{2,1,0:T(8,128)}, f32[64,8,512]{2,1,0:T(8,128)S(1)}, u32[]{:S(2)}, u32[]{:S(2)}) collective-permute-start(f32[64,8,512]{2,1,0:T(8,128)} %get-tuple-element.29), channel_id=1, source_target_pairs={{0,28},{4,0},{8,4},{12,8},{16,12},{20,16},{24,20},{28,24},{1,29},{... | collective-permute-start | bytes 3145736 | tf_op jit(solution)/shard_map/ppermute | solution.py:439
  46.9 100.7 %collective-permute-start.4 = (f32[3,18,8,512]{3,2,1,0:T(8,128)}, f32[3,18,8,512]{3,2,1,0:T(8,128)}, u32[]{:S(2)}, u32[]{:S(2)}) collective-permute-start(f32[3,18,8,512]{3,2,1,0:T(8,128)} %get-tuple-element.33), channel_id=1, source_target_pairs={{0,4},{4,8},{8,12},{12,16},{16,20},{20,24},{24,28},{28,0},{1,5},{5... | collective-permute-start | bytes 2654216 | tf_op jit(solution)/shard_map/ppermute | solution.py:439
  94.5 1.0 copy-start
  94.5 53.1 %collective-permute-start.5 = (f32[3,18,8,512]{3,2,1,0:T(8,128)}, f32[3,18,8,512]{3,2,1,0:T(8,128)}, u32[]{:S(2)}, u32[]{:S(2)}) collective-permute-start(f32[3,18,8,512]{3,2,1,0:T(8,128)} %get-tuple-element.34), channel_id=1, source_target_pairs={{0,28},{4,0},{8,4},{12,8},{16,12},{20,16},{24,20},{28,24},{1,29},{... | collective-permute-start | bytes 2654216 | tf_op jit(solution)/shard_map/ppermute | solution.py:439
  94.5 1.3 copy-start.1
  110.5 30.1 %all-to-all-start.1 = ((f32[4,2,4,128,128]{4,3,2,1,0:T(8,128)}), f32[4,2,4,128,128]{4,3,2,1,0:T(8,128)}, u32[]{:S(2)}, u32[]{:S(2)}) async-start(f32[4,2,4,128,128]{4,3,2,1,0:T(8,128)} %get-tuple-element.39), calls=%async_computation.1 | async-start | bytes 4194304 | tf_op jit(solution)/shard_map/all_to_all | solution.py:563
